TPU v7x, 32 devices: a whole 2x2x4 slice. The times are simulated.
32 devices in a mesh: seq: 8 (over z, x), tp: 4 (over y, core).
Axes of the slice: x: 2, y: 2, z: 4, core: 2. Of those that a mesh axis runs over, the one named last changes fastest.
Arguments:
- inputs: bfloat16 [8192, 2048], P('seq'), may hold values from -6 to 6
- cotangent: bfloat16 [8192, 2048], P('seq'), may hold values from -6 to 6
- lengths: int32 [9], replicated, may hold values from 0 to 2048, as said below
- offsets: int32 [9], replicated, may hold values from 0 to 8192, as said below
- first_gain: float32 [2048], P('seq'), may hold values from 0.5 to 1.5
- first_bias: float32 [2048], P('seq'), may hold values from -2.5 to 2.5
- query_weight: float32 [2048, 2048], P('seq', 'tp'), may hold values from -0.125 to 0.125
- key_weight: float32 [2048, 2048], P('seq', 'tp'), may hold values from -0.125 to 0.125
- value_weight: float32 [2048, 4096], P('seq', 'tp'), may hold values from -0.125 to 0.125
- gate_weight: float32 [2048, 4096], P('seq', 'tp'), may hold values from -0.125 to 0.125
- group_gain: float32 [4096], P(('tp', 'seq')), may hold values from 0.5 to 1.5
- group_bias: float32 [4096], P(('tp', 'seq')), may hold values from -2.5 to 2.5
- out_weight: float32 [4096, 2048], P('tp', 'seq'), may hold values from -0.09375 to 0.09375
- second_gain: float32 [2048], P('seq'), may hold values from 0.5 to 1.5
- second_bias: float32 [2048], P('seq'), may hold values from -2.5 to 2.5
- up_weight: float32 [2048, 4096], P('seq', 'tp'), may hold values from -0.125 to 0.125
- up_bias: float32 [4096], P(('tp', 'seq')), may hold values from -2.5 to 2.5
- down_weight: float32 [4096, 2048], P('tp', 'seq'), may hold values from -0.09375 to 0.09375
- down_bias: float32 [2048], P('seq'), may hold values from -2.5 to 2.5
Outputs:
- output: bfloat16 [8192, 2048], P('seq')
- grad_inputs: float32 [8192, 2048], P('seq')
- grad_first_gain: float32 [2048], P('seq')
- grad_first_bias: float32 [2048], P('seq')
- grad_query_weight: float32 [2048, 2048], P('seq', 'tp')
- grad_key_weight: float32 [2048, 2048], P('seq', 'tp')
- grad_value_weight: float32 [2048, 4096], P('seq', 'tp')
- grad_gate_weight: float32 [2048, 4096], P('seq', 'tp')
- grad_group_gain: float32 [4096], P(('tp', 'seq'))
- grad_group_bias: float32 [4096], P(('tp', 'seq'))
- grad_out_weight: float32 [4096, 2048], P('tp', 'seq')
- grad_second_gain: float32 [2048], P('seq')
- grad_second_bias: float32 [2048], P('seq')
- grad_up_weight: float32 [2048, 4096], P('seq', 'tp')
- grad_up_bias: float32 [4096], P(('tp', 'seq'))
- grad_down_weight: float32 [4096, 2048], P('tp', 'seq')
- grad_down_bias: float32 [2048], P('seq')
Inputs may be any that keep to these rules, and one draw needn't show every extreme that they name: `lengths`: sequences lie in order without intersection, the first at slot 0 and the last ending at slot 8192; each has 1024 to 2048 tokens, entry 1 or 2 exactly 2048; between two sequences lie 0 to 128 padding slots; entries after the last sequence have length 0 and offset 8192. Every block of 1024 slots but the first begins inside a sequence that began in an earlier block. `offsets`: the first slots of the sequences of lengths, increasing.
All inputs are finite; a program needn't handle non-finite values.
Results may differ from a plain program's by a relative error of at most 0.013.
The roundings to bfloat16 on the way count: a program that leaves them out, or rounds other values in their place, can miss the bound.
Values may be sent and summed in bfloat16 or wider, within the bound.
No kernel may reach another device: no remote copies, remote signals or barrier semaphores. Data moves between devices by JAX's collectives and lax.ppermute only.
A program may use at most 320 MiB of HBM per device.

v0:
```python
import math

import jax
import jax.numpy as jnp
from jax import lax
from jax.sharding import PartitionSpec as P

KD = 256
VD = 512


epsilon = 1e-05


def from_behind(block, axis, distance):
    devices = range(lax.axis_size(axis))
    route = [(i - distance, i) for i in devices if i - distance in devices]
    return lax.ppermute(block, axis, route)


def layer_norm(values, gain_vec, bias_vec):
    average = jnp.mean(values, axis=-1, keepdims=True)
    centred = values - average
    variance = jnp.mean(centred * centred, axis=-1, keepdims=True)
    return centred * lax.rsqrt(variance + epsilon) * gain_vec + bias_vec


def gate_norm(retained, gate_raw, gain_vec, bias_vec):
    average = jnp.mean(retained, axis=-1, keepdims=True)
    centred = retained - average
    variance = jnp.mean(centred * centred, axis=-1, keepdims=True)
    normed = (centred * lax.rsqrt(variance + epsilon)).reshape(gate_raw.shape)
    return (normed * gain_vec + bias_vec) * jax.nn.silu(gate_raw)


def smooth(values):
    return jax.nn.gelu(values, approximate=False)


def rotate(values, cosine_table, sine_table):
    half_size = values.shape[-1] // 2
    turned = jnp.concatenate([-values[..., half_size:], values[..., :half_size]], axis=-1)
    return values * cosine_table + turned * sine_table


def token_layout(first_row, row_total, lengths, offsets):
    position = first_row + jnp.arange(row_total, dtype=jnp.int32)
    inside = (position[:, None] >= offsets[None, :]) & (
        position[:, None] < offsets[None, :] + lengths[None, :]
    )
    member = inside.astype(jnp.int32)
    labels = jnp.arange(1, lengths.shape[0] + 1, dtype=jnp.int32)
    number = jnp.sum(member * labels[None, :], axis=1) - 1
    seq_start = jnp.sum(member * offsets[None, :], axis=1)
    return (number, position - seq_start)


def block_decay(first_row, row_total, lengths, offsets, log_decay, key_size):
    number, within = token_layout(first_row, row_total, lengths, offsets)
    before = token_layout(first_row - 1, 1, lengths, offsets)[0][0]
    final_seq = number[row_total - 1]
    slot_index = jnp.arange(row_total).astype(jnp.float32)
    distance = slot_index[:, None] - slot_index[None, :]
    linked = (number[:, None] == number[None, :]) & (number[:, None] >= 0) & (distance >= 0)
    exponent = jnp.where(linked, distance, 0.0)
    decay_mask = jnp.where(linked[None], jnp.exp(log_decay[:, None, None] * exponent[None]), 0.0)
    entry_weight = jnp.where(
        ((number == before) & (number >= 0))[None, :],
        jnp.exp(log_decay[:, None] * (slot_index[None, :] + 1.0)),
        0.0,
    )
    exit_weight = jnp.where(
        ((number == final_seq) & (number >= 0))[None, :],
        jnp.exp(log_decay[:, None] * (row_total - 1.0 - slot_index[None, :])),
        0.0,
    )
    passing = jnp.where((final_seq == before) & (before >= 0), jnp.exp(log_decay * row_total), 0.0)
    half_size = key_size // 2
    frequency = jnp.exp(
        -math.log(10000.0) * 2.0 * jnp.arange(half_size).astype(jnp.float32) / key_size
    )
    angles = within.astype(jnp.float32)[:, None] * frequency[None, :]
    angles = jnp.concatenate([angles, angles], axis=-1)[:, None, :]
    return (decay_mask, entry_weight, exit_weight, passing, jnp.cos(angles), jnp.sin(angles))


def body(
    inputs,
    cotangent,
    lengths,
    offsets,
    first_gain,
    first_bias,
    query_weight,
    key_weight,
    value_weight,
    gate_weight,
    group_gain,
    group_bias,
    out_weight,
    second_gain,
    second_bias,
    up_weight,
    up_bias,
    down_weight,
    down_bias,
):
    row_count = inputs.shape[0]
    head_count = query_weight.shape[1] // KD
    (
        gain_one,
        bias_one,
        query_mat,
        key_mat,
        value_mat,
        gate_mat,
        group_scale,
        group_shift,
        gain_two,
        bias_two,
        up_mat,
        up_shift,
        down_shift,
        out_mat,
        down_mat,
    ) = (
        lax.all_gather(first_gain.astype(jnp.bfloat16), "seq", axis=0, tiled=True),
        lax.all_gather(first_bias.astype(jnp.bfloat16), "seq", axis=0, tiled=True),
        lax.all_gather(query_weight.astype(jnp.bfloat16), "seq", axis=0, tiled=True),
        lax.all_gather(key_weight.astype(jnp.bfloat16), "seq", axis=0, tiled=True),
        lax.all_gather(value_weight.astype(jnp.bfloat16), "seq", axis=0, tiled=True),
        lax.all_gather(gate_weight.astype(jnp.bfloat16), "seq", axis=0, tiled=True),
        lax.all_gather(group_gain.astype(jnp.bfloat16), "seq", axis=0, tiled=True),
        lax.all_gather(group_bias.astype(jnp.bfloat16), "seq", axis=0, tiled=True),
        lax.all_gather(second_gain.astype(jnp.bfloat16), "seq", axis=0, tiled=True),
        lax.all_gather(second_bias.astype(jnp.bfloat16), "seq", axis=0, tiled=True),
        lax.all_gather(up_weight.astype(jnp.bfloat16), "seq", axis=0, tiled=True),
        lax.all_gather(up_bias.astype(jnp.bfloat16), "seq", axis=0, tiled=True),
        lax.all_gather(down_bias.astype(jnp.bfloat16), "seq", axis=0, tiled=True),
        lax.all_gather(out_weight.astype(jnp.bfloat16), "seq", axis=1, tiled=True),
        lax.all_gather(down_weight.astype(jnp.bfloat16), "seq", axis=1, tiled=True),
    )
    first_row = lax.axis_index("seq") * row_count
    head_base = lax.axis_index("tp") * head_count
    log_decay = jnp.log(
        1.0
        - jnp.exp2(-5.0 - (head_base + jnp.arange(head_count, dtype=jnp.int32)).astype(jnp.float32))
    )
    decay_mask, entry_weight, exit_weight, passing, cosine_table, sine_table = block_decay(
        first_row, row_count, lengths, offsets, log_decay, KD
    )
    entry_cols = entry_weight.T[:, :, None]
    exit_cols = exit_weight.T[:, :, None]
    residual_in = inputs.astype(jnp.float32)
    normed_one, pull_one = jax.vjp(
        layer_norm, residual_in, gain_one.astype(jnp.float32), bias_one.astype(jnp.float32)
    )
    normed_bf = normed_one.astype(jnp.bfloat16)
    query_raw = jnp.dot(normed_bf, query_mat, preferred_element_type=jnp.float32).reshape(
        row_count, head_count, KD
    )
    key_raw = jnp.dot(normed_bf, key_mat, preferred_element_type=jnp.float32).reshape(
        row_count, head_count, KD
    )
    value_half_width = (
        jnp.dot(normed_bf, value_mat, preferred_element_type=jnp.float32)
        .astype(jnp.bfloat16)
        .reshape(row_count, head_count, VD)
    )
    gate_raw = jnp.dot(normed_bf, gate_mat, preferred_element_type=jnp.float32)
    query_bf = rotate(query_raw, cosine_table, sine_table).astype(jnp.bfloat16)
    key_bf = rotate(key_raw, cosine_table, sine_table).astype(jnp.bfloat16)
    query_decay_factor = (query_bf * entry_cols).astype(jnp.bfloat16)
    key_decay_factor = (key_bf * exit_cols).astype(jnp.bfloat16)
    scores = jnp.einsum("bhk,chk->hbc", query_bf, key_bf, preferred_element_type=jnp.float32)
    retained = (scores * decay_mask).astype(jnp.bfloat16)
    local_out = jnp.einsum(
        "hbc,chv->bhv", retained, value_half_width, preferred_element_type=jnp.float32
    )
    local_block_state = jnp.einsum(
        "scr,scq->crq", key_decay_factor, value_half_width, preferred_element_type=jnp.float32
    )

    def forward_turn(turn, carried_over_state):
        return from_behind(
            passing[:, None, None] * carried_over_state + local_block_state, "seq", 1
        )

    entering = lax.fori_loop(
        0, lax.axis_size("seq") - 1, forward_turn, jnp.zeros_like(local_block_state)
    )
    state_half_width = entering.astype(jnp.bfloat16)
    cross_block_output = jnp.einsum(
        "lda,daf->ldf", query_decay_factor, state_half_width, preferred_element_type=jnp.float32
    )
    retained_out = local_out + cross_block_output
    gated, pull_gate = jax.vjp(
        gate_norm,
        retained_out,
        gate_raw,
        group_scale.astype(jnp.float32),
        group_shift.astype(jnp.float32),
    )
    gated_bf = gated.astype(jnp.bfloat16)
    branch_part = jnp.dot(gated_bf, out_mat, preferred_element_type=jnp.float32)
    mid_rows = residual_in + lax.psum(branch_part, "tp")
    normed_two, pull_two = jax.vjp(
        layer_norm, mid_rows, gain_two.astype(jnp.float32), bias_two.astype(jnp.float32)
    )
    normed_two_bf = normed_two.astype(jnp.bfloat16)
    up_rows = jnp.dot(normed_two_bf, up_mat, preferred_element_type=jnp.float32) + up_shift.astype(
        jnp.float32
    )
    acted, pull_act = jax.vjp(smooth, up_rows)
    acted_bf = acted.astype(jnp.bfloat16)
    ffn_part = jnp.dot(acted_bf, down_mat, preferred_element_type=jnp.float32)
    ffn_rows = lax.psum(ffn_part, "tp") + down_shift.astype(jnp.float32)
    output = (mid_rows + ffn_rows).astype(jnp.bfloat16)
    out_mat, down_mat = (out_mat, down_mat)
    cot_float = cotangent.astype(jnp.float32)
    grad_down_bias = jnp.sum(cot_float, axis=0)
    grad_down_weight = jnp.einsum(
        "bf,bd->fd", acted_bf, cotangent, preferred_element_type=jnp.float32
    )
    d_act = jnp.einsum("bd,fd->bf", cotangent, down_mat, preferred_element_type=jnp.float32)
    d_up = pull_act(d_act)[0].astype(jnp.bfloat16)
    grad_up_bias = jnp.sum(d_up.astype(jnp.float32), axis=0)
    grad_up_weight = jnp.einsum(
        "bd,bf->df", normed_two_bf, d_up, preferred_element_type=jnp.float32
    )
    d_normed_two = lax.psum(
        jnp.einsum("bf,df->bd", d_up, up_mat, preferred_element_type=jnp.float32), "tp"
    )
    d_mid_norm, grad_second_gain, grad_second_bias = pull_two(d_normed_two)
    d_mid = cot_float + d_mid_norm
    d_branch = d_mid.astype(jnp.bfloat16)
    grad_out_weight = jnp.einsum(
        "bv,bd->vd", gated_bf, d_branch, preferred_element_type=jnp.float32
    )
    d_gated = jnp.einsum("bd,vd->bv", d_branch, out_mat, preferred_element_type=jnp.float32)
    d_retained, d_gate, grad_group_gain, grad_group_bias = pull_gate(d_gated)
    retained_gradient_half = d_retained.astype(jnp.bfloat16)
    d_gate_bf = d_gate.astype(jnp.bfloat16)
    d_weights = jnp.einsum(
        "bhv,chv->hbc", retained_gradient_half, value_half_width, preferred_element_type=jnp.float32
    )
    d_scores = (d_weights * decay_mask).astype(jnp.bfloat16)
    d_query = jnp.einsum("hbc,chk->bhk", d_scores, key_bf, preferred_element_type=jnp.float32)
    d_key = jnp.einsum("hbc,bhk->chk", d_scores, query_bf, preferred_element_type=jnp.float32)
    d_value = jnp.einsum(
        "hbc,bhv->chv", retained, retained_gradient_half, preferred_element_type=jnp.float32
    )
    d_query = (
        d_query
        + jnp.einsum(
            "dpc,pnc->dpn",
            retained_gradient_half,
            state_half_width,
            preferred_element_type=jnp.float32,
        )
        * entry_cols
    )
    own_grad = jnp.einsum(
        "scr,scq->crq",
        query_decay_factor,
        retained_gradient_half,
        preferred_element_type=jnp.float32,
    )

    def backward_turn(turn, carried_over_state):
        return from_behind(
            (own_grad + passing[:, None, None] * carried_over_state).astype(jnp.bfloat16), "seq", -1
        ).astype(jnp.float32)

    leaving = lax.fori_loop(0, lax.axis_size("seq") - 1, backward_turn, jnp.zeros_like(own_grad))
    leaving_state_half = leaving.astype(jnp.bfloat16)
    d_key = (
        d_key
        + jnp.einsum(
            "dpc,pnc->dpn", value_half_width, leaving_state_half, preferred_element_type=jnp.float32
        )
        * exit_cols
    )
    d_value = d_value + jnp.einsum(
        "lda,daf->ldf", key_decay_factor, leaving_state_half, preferred_element_type=jnp.float32
    )
    d_query_bf = (
        rotate(d_query, cosine_table, -sine_table)
        .astype(jnp.bfloat16)
        .reshape(row_count, head_count * KD)
    )
    d_key_bf = (
        rotate(d_key, cosine_table, -sine_table)
        .astype(jnp.bfloat16)
        .reshape(row_count, head_count * KD)
    )
    d_value_bf = d_value.astype(jnp.bfloat16).reshape(row_count, head_count * VD)
    grad_query_weight = jnp.einsum(
        "bd,bq->dq", normed_bf, d_query_bf, preferred_element_type=jnp.float32
    )
    grad_key_weight = jnp.einsum(
        "bd,bq->dq", normed_bf, d_key_bf, preferred_element_type=jnp.float32
    )
    grad_value_weight = jnp.einsum(
        "bd,bv->dv", normed_bf, d_value_bf, preferred_element_type=jnp.float32
    )
    grad_gate_weight = jnp.einsum(
        "bd,bv->dv", normed_bf, d_gate_bf, preferred_element_type=jnp.float32
    )
    d_normed_part = jnp.einsum(
        "bq,dq->bd", d_query_bf, query_mat, preferred_element_type=jnp.float32
    )
    d_normed_part = d_normed_part + jnp.einsum(
        "bq,dq->bd", d_key_bf, key_mat, preferred_element_type=jnp.float32
    )
    d_normed_part = d_normed_part + jnp.einsum(
        "bv,dv->bd", d_value_bf, value_mat, preferred_element_type=jnp.float32
    )
    d_normed_part = d_normed_part + jnp.einsum(
        "bv,dv->bd", d_gate_bf, gate_mat, preferred_element_type=jnp.float32
    )
    d_normed_one = lax.psum(d_normed_part, "tp")
    d_input_norm, grad_first_gain, grad_first_bias = pull_one(d_normed_one)
    grad_inputs = d_mid + d_input_norm
    (
        own_first_gain,
        own_first_bias,
        own_query,
        own_key,
        own_value,
        own_gate,
        own_group_gain,
        own_group_bias,
        own_second_gain,
        own_second_bias,
        own_up,
        own_up_bias,
        own_down_bias,
        own_out,
        own_down,
    ) = (
        lax.psum_scatter(grad_first_gain, "seq", scatter_dimension=0, tiled=True),
        lax.psum_scatter(grad_first_bias, "seq", scatter_dimension=0, tiled=True),
        lax.psum_scatter(grad_query_weight, "seq", scatter_dimension=0, tiled=True),
        lax.psum_scatter(grad_key_weight, "seq", scatter_dimension=0, tiled=True),
        lax.psum_scatter(grad_value_weight, "seq", scatter_dimension=0, tiled=True),
        lax.psum_scatter(grad_gate_weight, "seq", scatter_dimension=0, tiled=True),
        lax.psum_scatter(grad_group_gain, "seq", scatter_dimension=0, tiled=True),
        lax.psum_scatter(grad_group_bias, "seq", scatter_dimension=0, tiled=True),
        lax.psum_scatter(grad_second_gain, "seq", scatter_dimension=0, tiled=True),
        lax.psum_scatter(grad_second_bias, "seq", scatter_dimension=0, tiled=True),
        lax.psum_scatter(grad_up_weight, "seq", scatter_dimension=0, tiled=True),
        lax.psum_scatter(grad_up_bias, "seq", scatter_dimension=0, tiled=True),
        lax.psum_scatter(grad_down_bias, "seq", scatter_dimension=0, tiled=True),
        lax.psum_scatter(grad_out_weight, "seq", scatter_dimension=1, tiled=True),
        lax.psum_scatter(grad_down_weight, "seq", scatter_dimension=1, tiled=True),
    )
    return (
        output,
        grad_inputs,
        own_first_gain,
        own_first_bias,
        own_query,
        own_key,
        own_value,
        own_gate,
        own_group_gain,
        own_group_bias,
        own_out,
        own_second_gain,
        own_second_bias,
        own_up,
        own_up_bias,
        own_down,
        own_down_bias,
    )


def solution(mesh):
    placed = (
        P("seq", None),
        P("seq", None),
        P(),
        P(),
        P("seq"),
        P("seq"),
        P("seq", "tp"),
        P("seq", "tp"),
        P("seq", "tp"),
        P("seq", "tp"),
        P(("tp", "seq")),
        P(("tp", "seq")),
        P("tp", "seq"),
        P("seq"),
        P("seq"),
        P("seq", "tp"),
        P(("tp", "seq")),
        P("tp", "seq"),
        P("seq"),
    )
    return jax.shard_map(
        body,
        mesh=mesh,
        in_specs=placed,
        out_specs=(
            P("seq", None),
            P("seq", None),
            P("seq"),
            P("seq"),
            P("seq", "tp"),
            P("seq", "tp"),
            P("seq", "tp"),
            P("seq", "tp"),
            P(("tp", "seq")),
            P(("tp", "seq")),
            P("tp", "seq"),
            P("seq"),
            P("seq"),
            P("seq", "tp"),
            P(("tp", "seq")),
            P("tp", "seq"),
            P("seq"),
        ),
        check_vma=False,
    )
```

profile of v0, /device:TPU:0, one launch (start us, length us, event | category | flops | bytes accessed | tf_op | source)
XLA Modules:
  0.0 2433.1 jit_solution(17207470539772142372)
XLA Ops:
  22.9 22.4 all-gather.3
  141.7 45.8 %all-gather.16.cloned.1.call-done = bf16[2048,1024]{1,0:T(8,128)(2,1)} async-done(((bf16[256,1024]{1,0:T(8,128)(2,1)}), bf16[2048,1024]{1,0:T(8,128)(2,1)}) %all-gather.16.cloned.1.call-update) | async-done | bytes 4194320 | tf_op jit(solution)/shard_map/all_gather | solution.py:131
  203.2 257.2 %while.22 = (s32[]{:T(128)}, f32[2,256,512]{2,1,0:T(8,128)S(1)}, f32[2,256,512]{2,1,0:T(8,128)S(1)}, s32[]{:T(128)}, pred[]{:T(512)}, /*index=5*/s32[]{:T(128)}) while((s32[]{:T(128)}, f32[2,256,512]{2,1,0:T(8,128)S(1)}, f32[2,256,512]{2,1,0:T(8,128)S(1)}, s32[]{:T(128)}, pred[]{:T(512)}, /*index=5*/s32[]{:T(128)}) %tuple.73), condition=%wide.region_6.7_spmd.clone, body=%wide.region_5.6_spmd.clone.sunk | while | flops 524304 | bytes 7340162 | solution.py:189
  206.1 21.0 collective-permute-done
  227.5 21.6 collective-permute-start
  249.0 24.6 %collective-permute-done = f32[2,256,512]{2,1,0:T(8,128)S(1)} collective-permute-done((f32[2,256,512]{2,1,0:T(8,128)S(1)}, f32[2,256,512]{2,1,0:T(8,128)S(1)}, u32[]{:S(2)}, u32[]{:S(2)}) %collective-permute-start) | collective-permute-done | bytes 1048608 | tf_op jit(solution)/shard_map/while/body/eval_jaxpr/ppermute | solution.py:18
  274.0 22.8 collective-permute-start
  296.8 27.2 %collective-permute-done = f32[2,256,512]{2,1,0:T(8,128)S(1)} collective-permute-done((f32[2,256,512]{2,1,0:T(8,128)S(1)}, f32[2,256,512]{2,1,0:T(8,128)S(1)}, u32[]{:S(2)}, u32[]{:S(2)}) %collective-permute-start) | collective-permute-done | bytes 1048608 | tf_op jit(solution)/shard_map/while/body/eval_jaxpr/ppermute | solution.py:18
  340.9 41.5 %collective-permute-done = f32[2,256,512]{2,1,0:T(8,128)S(1)} collective-permute-done((f32[2,256,512]{2,1,0:T(8,128)S(1)}, f32[2,256,512]{2,1,0:T(8,128)S(1)}, u32[]{:S(2)}, u32[]{:S(2)}) %collective-permute-start) | collective-permute-done | bytes 1048608 | tf_op jit(solution)/shard_map/while/body/eval_jaxpr/ppermute | solution.py:18
  493.5 35.3 %all-gather.6 = bf16[8,1,128]{2,1,0:T(2,128)(2,1)S(1)} all-gather(bf16[1,1,128]{2,1,0:T(2,128)(2,1)S(1)} %convert_bitcast_fusion), channel_id=1, replica_groups=mesh['seq'=8,'tp'=4] {'seq'}, dimensions={0}, use_global_device_ids=true | all-gather | bytes 2304 | tf_op jit(solution)/shard_map/all_gather | solution.py:138
  563.4 96.4 %all-reduce.14.cloned.1.call-done = f32[1024,2048]{1,0:T(8,128)} async-done(((f32[1024,2048]{1,0:T(8,128)}), f32[1024,2048]{1,0:T(8,128)}) %all-reduce.14.cloned.1.call-update) | async-done | bytes 8388624 | tf_op jit(solution)/shard_map/psum | solution.py:206
  672.0 64.1 %all-gather.26.cloned.1.call-done = bf16[2048,1024]{1,0:T(8,128)(2,1)} async-done(((bf16[256,1024]{1,0:T(8,128)(2,1)}), bf16[2048,1024]{1,0:T(8,128)(2,1)}) %all-gather.26.cloned.1.call-update) | async-done | bytes 4194320 | tf_op jit(solution)/shard_map/all_gather | solution.py:137
  746.1 65.9 %all-gather.28.cloned.1.call-done = bf16[1024,2048]{1,0:T(8,128)(2,1)} async-done(((bf16[1024,256]{1,0:T(8,128)(2,1)}), bf16[1024,2048]{1,0:T(8,128)(2,1)}) %all-gather.28.cloned.1.call-update) | async-done | bytes 4194320 | tf_op jit(solution)/shard_map/all_gather | solution.py:141
  812.0 19.4 convert_reduce_fusion.2
  852.8 138.1 %all-reduce.16.cloned.1.call-done = f32[1024,2048]{1,0:T(8,128)} async-done(((f32[1024,2048]{1,0:T(8,128)}), f32[1024,2048]{1,0:T(8,128)}) %all-reduce.16.cloned.1.call-update) | async-done | bytes 8388624 | tf_op jit(solution)/shard_map/psum | solution.py:231
  1043.5 98.6 %while.23 = (s32[]{:T(128)}, f32[2,256,512]{2,1,0:T(8,128)S(1)}, f32[2,256,512]{2,1,0:T(8,128)S(1)}, s32[]{:T(128)}, pred[]{:T(512)}, /*index=5*/s32[]{:T(128)}, s32[]{:T(128)}) while((s32[]{:T(128)}, f32[2,256,512]{2,1,0:T(8,128)S(1)}, f32[2,256,512]{2,1,0:T(8,128)S(1)}, s32[]{:T(128)}, pred[]{:T(512)}, /*index=5*/s32[]{:T(128)}, ...), condition=%wide.region_19.20_spmd.clone, body=%wide.region_18.19_spmd.clone.sunk | while | flops 1310737 | bytes 6291604 | solution.py:275
  1274.8 202.3 %all-reduce.18.cloned.1.call-done = (f32[1024,2048]{1,0:T(8,128)}, f32[1024,2048]{1,0:T(8,128)}) async-done(((f32[1024,2048]{1,0:T(8,128)}, f32[1024,2048]{1,0:T(8,128)}), (f32[1024,2048]{1,0:T(8,128)}, f32[1024,2048]{1,0:T(8,128)})) %all-reduce.18.cloned.1.call-update) | async-done | bytes 16777232 | tf_op jit(solution)/shard_map/psum | solution.py:217
  1499.3 39.1 %all-reduce.8 = (f32[2048]{0:T(1024)S(1)}, f32[2048]{0:T(1024)S(1)}, f32[1024]{0:T(1024)S(1)}, f32[1024]{0:T(1024)S(1)}, f32[2048]{0:T(1024)S(1)}, /*index=5*/f3...) all-reduce(f32[2048]{0:T(1024)} %get-tuple-element.101, ...), channel_id=2, replica_groups=mesh['seq'=8,'tp'=4] {'seq'}, use_global_device_ids=true, to_apply=%region_24.25.clone | all-reduce | flops 13312 | bytes 106496
  1571.0 92.2 %reduce-scatter.10.cloned.1.call-done = f32[256,512]{1,0:T(8,128)} async-done(((f32[2048,512]{1,0:T(8,128)}), f32[256,512]{1,0:T(8,128)}) %reduce-scatter.10.cloned.1.call-update) | async-done | bytes 524304 | tf_op jit(solution)/shard_map/reduce_scatter | solution.py:345
  1663.2 153.0 %reduce-scatter.18.cloned.1.call-done = f32[256,1024]{1,0:T(8,128)} async-done(((f32[2048,1024]{1,0:T(8,128)}), f32[256,1024]{1,0:T(8,128)}) %reduce-scatter.18.cloned.1.call-update) | async-done | bytes 1048592 | tf_op jit(solution)/shard_map/reduce_scatter | solution.py:352
  1816.2 152.9 %reduce-scatter.20.cloned.1.call-done = f32[1024,256]{1,0:T(8,128)} async-done(((f32[1024,2048]{1,0:T(8,128)}), f32[1024,256]{1,0:T(8,128)}) %reduce-scatter.20.cloned.1.call-update) | async-done | bytes 1048592 | tf_op jit(solution)/shard_map/reduce_scatter | solution.py:356
  1969.1 152.5 %reduce-scatter.16.cloned.1.call-done = f32[1024,256]{1,0:T(8,128)} async-done(((f32[1024,2048]{1,0:T(8,128)}), f32[1024,256]{1,0:T(8,128)}) %reduce-scatter.16.cloned.1.call-update) | async-done | bytes 1048592 | tf_op jit(solution)/shard_map/reduce_scatter | solution.py:355
  2121.7 152.6 %reduce-scatter.14.cloned.1.call-done = f32[256,1024]{1,0:T(8,128)} async-done(((f32[2048,1024]{1,0:T(8,128)}), f32[256,1024]{1,0:T(8,128)}) %reduce-scatter.14.cloned.1.call-update) | async-done | bytes 1048592 | tf_op jit(solution)/shard_map/reduce_scatter | solution.py:347
  2274.2 152.1 %reduce-scatter.12.cloned.1.call-done = f32[256,1024]{1,0:T(8,128)} async-done(((f32[2048,1024]{1,0:T(8,128)}), f32[256,1024]{1,0:T(8,128)}) %reduce-scatter.12.cloned.1.call-update) | async-done | bytes 1048592 | tf_op jit(solution)/shard_map/reduce_scatter | solution.py:346
  (393 shorter events, 671.2 us)
Async XLA Ops:
  7.2 111.5 %all-gather.18.cloned.1.call-start = ((), (), s32[]{:S(2)}) async-start(), calls=%async_computation.8 | async-start | bytes 2359296 | tf_op jit(solution)/shard_map/all_gather | solution.py:129
  9.2 117.8 %all-gather.20.cloned.1.call-start = ((), (), s32[]{:S(2)}) async-start(), calls=%async_computation.9 | async-start | bytes 2359296 | tf_op jit(solution)/shard_map/all_gather | solution.py:130
  11.1 176.4 %all-gather.16.cloned.1.call-start = ((), (), s32[]{:S(2)}) async-start(), calls=%async_computation.7 | async-start | bytes 4718592 | tf_op jit(solution)/shard_map/all_gather | solution.py:131
  13.2 455.4 %all-gather.22.cloned.1.call-start = ((), (), s32[]{:S(2)}) async-start(), calls=%async_computation.10 | async-start | bytes 4718592 | tf_op jit(solution)/shard_map/all_gather | solution.py:132
  14.2 466.4 %all-gather.24.cloned.1.call-start = ((), (), s32[]{:S(2)}) async-start(), calls=%async_computation.11 | async-start | bytes 4718592 | tf_op jit(solution)/shard_map/all_gather | solution.py:140
  15.2 644.7 %all-reduce.14.cloned.1.call-start = ((), (), s32[]{:S(2)}) async-start(), calls=%async_computation.12 | async-start | bytes 16777216 | tf_op jit(solution)/shard_map/psum | solution.py:206
  203.6 23.6 collective-permute-start
  227.5 46.2 %collective-permute-start = (f32[2,256,512]{2,1,0:T(8,128)S(1)}, f32[2,256,512]{2,1,0:T(8,128)S(1)}, u32[]{:S(2)}, u32[]{:S(2)}) collective-permute-start(f32[2,256,512]{2,1,0:T(8,128)S(1)} %multiply_add_fusion.5), channel_id=1, source_target_pairs={{0,4},{4,8},{8,12},{12,16},{16,20},{20,24},{24,28},{1,5},{5,9},{9,... | collective-permute-start | bytes 3145736 | tf_op jit(solution)/shard_map/while/body/eval_jaxpr/ppermute | solution.py:18
  274.0 50.0 %collective-permute-start = (f32[2,256,512]{2,1,0:T(8,128)S(1)}, f32[2,256,512]{2,1,0:T(8,128)S(1)}, u32[]{:S(2)}, u32[]{:S(2)}) collective-permute-start(f32[2,256,512]{2,1,0:T(8,128)S(1)} %multiply_add_fusion.5), channel_id=1, source_target_pairs={{0,4},{4,8},{8,12},{12,16},{16,20},{20,24},{24,28},{1,5},{5,9},{9,... | collective-permute-start | bytes 3145736 | tf_op jit(solution)/shard_map/while/body/eval_jaxpr/ppermute | solution.py:18
  324.3 58.1 %collective-permute-start = (f32[2,256,512]{2,1,0:T(8,128)S(1)}, f32[2,256,512]{2,1,0:T(8,128)S(1)}, u32[]{:S(2)}, u32[]{:S(2)}) collective-permute-start(f32[2,256,512]{2,1,0:T(8,128)S(1)} %multiply_add_fusion.5), channel_id=1, source_target_pairs={{0,4},{4,8},{8,12},{12,16},{16,20},{20,24},{24,28},{1,5},{5,9},{9,... | collective-permute-start | bytes 3145736 | tf_op jit(solution)/shard_map/while/body/eval_jaxpr/ppermute | solution.py:18
  382.7 20.8 collective-permute-start
  403.9 34.2 %collective-permute-start = (f32[2,256,512]{2,1,0:T(8,128)S(1)}, f32[2,256,512]{2,1,0:T(8,128)S(1)}, u32[]{:S(2)}, u32[]{:S(2)}) collective-permute-start(f32[2,256,512]{2,1,0:T(8,128)S(1)} %multiply_add_fusion.5), channel_id=1, source_target_pairs={{0,4},{4,8},{8,12},{12,16},{16,20},{20,24},{24,28},{1,5},{5,9},{9,... | collective-permute-start | bytes 3145736 | tf_op jit(solution)/shard_map/while/body/eval_jaxpr/ppermute | solution.py:18
  438.4 21.8 collective-permute-start
  490.4 245.7 %all-gather.26.cloned.1.call-start = ((), (), s32[]{:S(2)}) async-start(), calls=%async_computation.13 | async-start | bytes 4718592 | tf_op jit(solution)/shard_map/all_gather | solution.py:137
  492.5 319.5 %all-gather.28.cloned.1.call-start = ((), (), s32[]{:S(2)}) async-start(), calls=%async_computation.14 | async-start | bytes 4718592 | tf_op jit(solution)/shard_map/all_gather | solution.py:141
  493.4 497.5 %all-reduce.16.cloned.1.call-start = ((), (), s32[]{:S(2)}) async-start(), calls=%async_computation.15 | async-start | bytes 16777216 | tf_op jit(solution)/shard_map/psum | solution.py:231
  839.7 637.3 %all-reduce.18.cloned.1.call-start = ((), (), s32[]{:S(2)}) async-start(), calls=%async_computation.23 | async-start | bytes 33554432 | tf_op jit(solution)/shard_map/psum | solution.py:217
  1185.8 385.2 %reduce-scatter.8.cloned.1.call-start = ((), (), s32[]{:S(2)}) async-start(), calls=%async_computation.16 | async-start | bytes 4718592 | tf_op jit(solution)/shard_map/reduce_scatter | solution.py:344
  1192.5 470.7 %reduce-scatter.10.cloned.1.call-start = ((), (), s32[]{:S(2)}) async-start(), calls=%async_computation.17 | async-start | bytes 4718592 | tf_op jit(solution)/shard_map/reduce_scatter | solution.py:345
  1200.1 616.0 %reduce-scatter.18.cloned.1.call-start = ((), (), s32[]{:S(2)}) async-start(), calls=%async_computation.21 | async-start | bytes 9437184 | tf_op jit(solution)/shard_map/reduce_scatter | solution.py:352
  1211.1 758.1 %reduce-scatter.20.cloned.1.call-start = ((), (), s32[]{:S(2)}) async-start(), calls=%async_computation.22 | async-start | bytes 9437184 | tf_op jit(solution)/shard_map/reduce_scatter | solution.py:356
  1221.6 900.1 %reduce-scatter.16.cloned.1.call-start = ((), (), s32[]{:S(2)}) async-start(), calls=%async_computation.20 | async-start | bytes 9437184 | tf_op jit(solution)/shard_map/reduce_scatter | solution.py:355
  1232.2 1042.1 %reduce-scatter.14.cloned.1.call-start = ((), (), s32[]{:S(2)}) async-start(), calls=%async_computation.19 | async-start | bytes 9437184 | tf_op jit(solution)/shard_map/reduce_scatter | solution.py:347
  1243.1 1183.3 %reduce-scatter.12.cloned.1.call-start = ((), (), s32[]{:S(2)}) async-start(), calls=%async_computation.18 | async-start | bytes 9437184 | tf_op jit(solution)/shard_map/reduce_scatter | solution.py:346
  (89 other events, 2238.0 us)
Sparse Core Ops, SparseCore 0:
  10.8 52.0 all-gather.17
  65.0 47.8 all-gather.19
  115.6 71.8 all-gather.15
  190.0 91.6 all-gather.21
  283.6 117.3 all-gather.23
  490.5 169.2 all-reduce.13
  662.5 73.5 all-gather.25
  738.7 73.2 all-gather.27
  839.8 151.0 all-reduce.15
  1185.9 291.0 all-reduce.17
  1481.2 89.7 reduce-scatter.7
  1575.5 87.6 reduce-scatter.9
  1667.4 148.7 reduce-scatter.17
  1820.7 148.4 reduce-scatter.19
  1973.2 148.4 reduce-scatter.15
  2126.2 148.0 reduce-scatter.13
  2278.3 148.0 reduce-scatter.11
where the time goes:
time: 2440 us; the launch traced here: 2430 us
  waiting for transfers between devices  1740 us (71%)
  matrix products  219 us (9%)
  blocking collectives  201 us (8%)
  other arithmetic  111 us (5%)
  starting transfers between devices  99.5 us (4%)
  local copies, waits for them, and re-layouts  46.4 us (2%)
    ppermute x14, waiting for transfers between devices, from_behind(): return lax.ppermute(block, axis, route)  251 us
    psum x1, waiting for transfers between devices, body(): ffn_rows = lax.psum(ffn_part, 'tp') + down_shift.astype(jnp.float32)  202 us
    reduce_scatter x1, waiting for transfers between devices, body(): lax.psum_scatter(grad_up_weight, 'seq', scatter_dimension=0, tiled=True)  153 us
    reduce_scatter x1, waiting for transfers between devices, body(): lax.psum_scatter(grad_down_weight, 'seq', scatter_dimension=1, tiled=True)  153 us
    reduce_scatter x1, waiting for transfers between devices, body(): lax.psum_scatter(grad_gate_weight, 'seq', scatter_dimension=0, tiled=True)  153 us
    reduce_scatter x1, waiting for transfers between devices, body(): lax.psum_scatter(grad_out_weight, 'seq', scatter_dimension=1, tiled=True)  153 us
    reduce_scatter x1, waiting for transfers between devices, body(): lax.psum_scatter(grad_value_weight, 'seq', scatter_dimension=0, tiled=True)  152 us
    psum x1, waiting for transfers between devices, body(): lax.psum(jnp.einsum('bf,df->bd', d_up, up_mat, preferred_element_type=jnp...  138 us
  transfers between devices with their start and end apart: 31, of which 27 were waited for; matrix products, arithmetic and copies ran while one was open for 9% of the time, Pallas kernels for 0%

commit v1 on v0

v1 whole, which is shorter than its diff:
```python
import math

import jax
import jax.numpy as jnp
from jax import lax
from jax.experimental import pallas as pl
from jax.experimental.pallas import tpu as pltpu
from jax.sharding import PartitionSpec as P

KD = 256
VD = 512
EPS = 1e-05
BF = jnp.bfloat16
F32 = jnp.float32
RING_MOST = 16


def dot(a, b, dims):
    return lax.dot_general(a, b, (dims, ((), ())), preferred_element_type=F32)


def from_others(block, direction, send=lax.ppermute):
    size = lax.axis_size("seq")
    parts = []
    for turn in range(1, max(1, size // 4) + 1):
        distance = direction * turn
        route = [(i - distance, i) for i in range(size) if 0 <= i - distance < size]
        parts.append(send(block, "seq", route))
    return parts


def ring_owner(place, size):
    place = lax.rem(place + 2 * size, size)
    return jnp.where(place < size // 2, 2 * place, 2 * (size - 1 - place) + 1)


def ring_place(index, size):
    return jnp.where(index % 2 == 0, index // 2, size - 1 - index // 2)


def ring_routes(size):
    order = list(range(0, size, 2)) + list(range(size - 1, 0, -2))
    ahead = [(order[i], order[(i + 1) % size]) for i in range(size)]
    return ahead, [(b, a) for a, b in ahead]


def assemble(own, ahead_parts, back_parts):
    size = lax.axis_size("seq")
    rows, cols = own.shape
    half = rows // 2
    count = 2 * (size - 1) + 1

    def kernel(*refs):
        parts, out, sems = refs[:count], refs[count], refs[count + 1]
        me = lax.axis_index("seq")
        place = ring_place(me, size)
        copies = [pltpu.make_async_copy(parts[0], out.at[pl.ds(me * rows, rows)], sems.at[0])]
        for k in range(1, size):
            a = ring_owner(place - k, size)
            b = ring_owner(place + k, size)
            copies.append(
                pltpu.make_async_copy(parts[k], out.at[pl.ds(a * rows, half)], sems.at[k])
            )
            copies.append(
                pltpu.make_async_copy(
                    parts[size - 1 + k],
                    out.at[pl.ds(b * rows + half, half)],
                    sems.at[size - 1 + k],
                )
            )
        for copy in copies:
            copy.start()
        for copy in copies:
            copy.wait()

    return pl.pallas_call(
        kernel,
        out_shape=jax.ShapeDtypeStruct((size * rows, cols), own.dtype),
        in_specs=[pl.BlockSpec(memory_space=pl.ANY)] * count,
        out_specs=pl.BlockSpec(memory_space=pltpu.VMEM),
        scratch_shapes=[pltpu.SemaphoreType.DMA((count,))],
        compiler_params=pltpu.CompilerParams(vmem_limit_bytes=60 * 2**20),
        cost_estimate=pl.CostEstimate(
            flops=4 * 10**9, bytes_accessed=0, transcendentals=0
        ),
        name="assemble",
    )(own, *ahead_parts, *back_parts)


def barrier(*values):
    return lax.optimization_barrier(values)


class Gather:
    def __init__(self, own, extra=None):
        self.size = lax.axis_size("seq")
        self.own = own
        half = own.shape[0] // 2
        self.now = [own[:half], own[half:]] + ([] if extra is None else [extra])
        self.parts = [[own[:half]], [own[half:]], [extra]]
        self.left = self.size - 1

    def tick(self, *values):
        count = len(self.now)
        done = barrier(*self.now, *values)
        self.now, values = list(done[:count]), done[count:]
        if self.left > 0:
            ahead, back = ring_routes(self.size)
            routes = [ahead, back, ahead]
            self.now = [
                lax.ppermute(block, "seq", route) for block, route in zip(self.now, routes)
            ]
            for part, block in zip(self.parts, self.now):
                part.append(block)
        self.left -= 1
        return values

    @property
    def ended(self):
        return self.left < 0

    def result(self):
        return assemble(self.own, self.parts[0][1:], self.parts[1][1:])

    def table(self):
        place = ring_place(lax.axis_index("seq"), self.size)
        stack = jnp.concatenate(self.parts[2], axis=0)
        index = jnp.arange(self.size)
        return stack[lax.rem(place - ring_place(index, self.size) + self.size, self.size)]


class Line:
    def __init__(self, token):
        self.token = token

    def run(self, function, *values):
        *values, self.token = barrier(*values, self.token)
        out = function(*values)
        first, *rest = out if isinstance(out, (tuple, list)) else (out,)
        first, self.token = barrier(first, self.token)
        return (first, *rest) if len(rest) else first

    def send(self, block, axis, route):
        block, self.token = barrier(block, self.token)
        return lax.ppermute(block, axis, route)

    def tick(self, *rings):
        for ring in rings:
            if not ring.ended:
                (self.token,) = ring.tick(self.token)

    def meet(self, *values):
        *values, self.token = barrier(*values, self.token)
        return values


class Reduce:
    def __init__(self, ahead, back=None):
        self.size = lax.axis_size("seq")
        self.halves = back is None
        self.grads = (ahead, ahead if back is None else back)
        self.place = ring_place(lax.axis_index("seq"), self.size)
        self.arrived = ()
        self.step = 0

    def tick(self, *values):
        self.step += 1
        if self.arrived:
            *self.arrived, first = barrier(*self.arrived, values[0])
            values = (first, *values[1:])
        self.now = ring_add(self.grads, self.arrived, self.place, self.step, self.halves)
        *self.now, first = barrier(*self.now, values[0])
        if self.step < self.size:
            routes = ring_routes(self.size)
            self.arrived = [
                lax.ppermute(block, "seq", route) for block, route in zip(self.now, routes)
            ]
        return (first, *values[1:])

    @property
    def ended(self):
        return self.step >= self.size

    def result(self):
        if self.halves:
            return jnp.concatenate(self.now, axis=0)
        return self.now


class Builtin:
    def __init__(self, value):
        self.value = value
        self.ended = True

    def result(self):
        return self.value


class Clock:
    def __init__(self, lanes):
        self.lanes = [[] for _ in range(lanes)]
        self.turn = 0

    def add(self, lane, chain, *values):
        self.lanes[lane].append(chain)
        if len(self.lanes[lane]) == 1:
            values = self.settle(lane, values)
        return values

    def settle(self, lane, values):
        queue = self.lanes[lane]
        while queue:
            if not queue[0].ended:
                values = queue[0].tick(*values)
            if not queue[0].ended:
                break
            queue.pop(0)
        return values

    def until(self, ring, *values):
        while any(ring in lane for lane in self.lanes):
            values = self.tick(*values)
            values = values if isinstance(values, tuple) else (values,)
        return values[0] if len(values) == 1 else values

    def tick(self, *values, count=1):
        for _ in range(count):
            for _ in self.lanes:
                lane = self.turn
                self.turn = (self.turn + 1) % len(self.lanes)
                if self.lanes[lane]:
                    values = self.settle(lane, values)
                    break
        return values[0] if len(values) == 1 else tuple(values)


def gather(own, extra=None):
    if lax.axis_size("seq") > RING_MOST:
        return Builtin(lax.all_gather(own, "seq", axis=0, tiled=True))
    return Gather(own, extra)


def reduce(ahead, back=None):
    if lax.axis_size("seq") > RING_MOST:
        total = [
            lax.psum_scatter(grad.astype(F32), "seq", scatter_dimension=0, tiled=True)
            for grad in (ahead, back)
            if grad is not None
        ]
        return Builtin(total[0] if back is None else total)
    return Reduce(ahead, back)


def small_reduce(table):
    me = lax.axis_index("seq")
    distance = table.shape[0] // 2
    while distance >= 1:
        route = [(i, i ^ distance) for i in range(lax.axis_size("seq"))]
        high = (me // distance) % 2
        kept = lax.dynamic_slice_in_dim(table, high * distance, distance)
        sent = lax.dynamic_slice_in_dim(table, (1 - high) * distance, distance)
        table = kept + lax.ppermute(sent, "seq", route)
        distance //= 2
    return table[0]


def swap(block, bit):
    return lax.ppermute(block, "tp", [(i, i ^ bit) for i in range(lax.axis_size("tp"))])


def token_layout(first_row, row_total, lengths, offsets):
    position = first_row + jnp.arange(row_total, dtype=jnp.int32)
    inside = (position[:, None] >= offsets[None, :]) & (
        position[:, None] < offsets[None, :] + lengths[None, :]
    )
    member = inside.astype(jnp.int32)
    labels = jnp.arange(1, lengths.shape[0] + 1, dtype=jnp.int32)
    number = jnp.sum(member * labels[None, :], axis=1) - 1
    seq_start = jnp.sum(member * offsets[None, :], axis=1)
    return (number, position - seq_start)


def passing_weight(first_row, row_total, lengths, offsets, log_decay):
    before = token_layout(first_row - 1, 1, lengths, offsets)[0][0]
    last = token_layout(first_row + row_total - 1, 1, lengths, offsets)[0][0]
    return jnp.where((last == before) & (before >= 0), jnp.exp(log_decay * row_total), 0.0)


def block_decay(first_row, row_total, lengths, offsets, log_decay):
    number, within = token_layout(first_row, row_total, lengths, offsets)
    before = token_layout(first_row - 1, 1, lengths, offsets)[0][0]
    final_seq = number[row_total - 1]
    slot_index = jnp.arange(row_total).astype(jnp.float32)
    entry_weight = jnp.where(
        ((number == before) & (number >= 0))[None, :],
        jnp.exp(log_decay[:, None] * (slot_index[None, :] + 1.0)),
        0.0,
    )
    exit_weight = jnp.where(
        ((number == final_seq) & (number >= 0))[None, :],
        jnp.exp(log_decay[:, None] * (row_total - 1.0 - slot_index[None, :])),
        0.0,
    )
    half_size = KD // 2
    frequency = jnp.exp(-math.log(10000.0) * 2.0 * jnp.arange(half_size).astype(jnp.float32) / KD)
    angles = within.astype(jnp.float32)[:, None] * frequency[None, :]
    return (number, entry_weight, exit_weight, jnp.cos(angles), jnp.sin(angles))


def standardize(values):
    average = jnp.mean(values, axis=-1, keepdims=True)
    centred = values - average
    variance = jnp.mean(centred * centred, axis=-1, keepdims=True)
    scale = lax.rsqrt(variance + EPS)
    return centred * scale, scale


def standardize_back(d_normed, normed, scale):
    first = jnp.mean(d_normed, axis=-1, keepdims=True)
    second = jnp.mean(d_normed * normed, axis=-1, keepdims=True)
    return scale * (d_normed - first - normed * second)


def kernel_call(body, name, grid, ins, outs, shapes, weight, prefetch=(), vmem=60):
    arrays = [a for a, _, _ in ins]
    return pl.pallas_call(
        body,
        out_shape=[jax.ShapeDtypeStruct(s, t) for s, t in shapes],
        grid_spec=pltpu.PrefetchScalarGridSpec(
            num_scalar_prefetch=len(prefetch),
            grid=grid,
            in_specs=[pl.BlockSpec(block, index) for _, block, index in ins],
            out_specs=[pl.BlockSpec(block, index) for block, index in outs],
        ),
        compiler_params=pltpu.CompilerParams(vmem_limit_bytes=vmem * 2**20),
        cost_estimate=pl.CostEstimate(
            flops=weight * 10**9, bytes_accessed=0, transcendentals=0
        ),
        name=name,
    )(*prefetch, *arrays)


def row_tile(i, *_):
    return (i, 0)


def fixed(*_):
    return (0, 0)


def fixed3(*_):
    return (0, 0, 0)


def turn(values, cosine, sine):
    low, high = values[:, : KD // 2], values[:, KD // 2 :]
    return jnp.concatenate([low * cosine - high * sine, high * cosine + low * sine], axis=1)


def norm_rows(x, gain, shift, tile=256):
    rows, width = x.shape

    def kernel(x_ref, gain_ref, shift_ref, out_ref):
        hat, _ = standardize(x_ref[...].astype(F32))
        out_ref[...] = (hat * gain_ref[...] + shift_ref[...]).astype(BF)

    return kernel_call(
        kernel,
        "first_norm",
        (rows // tile,),
        [
            (x, (tile, width), row_tile),
            (gain[None, :], (1, width), fixed),
            (shift[None, :], (1, width), fixed),
        ],
        [((tile, width), row_tile)],
        [((rows, width), BF)],
        6,
    )[0]


def project_turn(n1, qk_mat, cosine, sine, tile=256):
    rows, width = n1.shape
    cols = qk_mat.shape[1] // 2

    def kernel(n1_ref, mat_ref, cos_ref, sin_ref, q_ref, k_ref):
        raw = jnp.dot(n1_ref[...], mat_ref[...], preferred_element_type=F32)
        cos, sin = cos_ref[...], sin_ref[...]
        for at in range(0, cols, KD):
            q_ref[:, at : at + KD] = turn(raw[:, at : at + KD], cos, sin).astype(BF)
            k_ref[:, at : at + KD] = turn(raw[:, cols + at : cols + at + KD], cos, sin).astype(BF)

    return kernel_call(
        kernel,
        "query_key",
        (rows // tile,),
        [
            (n1, (tile, width), row_tile),
            (qk_mat, (width, 2 * cols), fixed),
            (cosine, (tile, KD // 2), row_tile),
            (sine, (tile, KD // 2), row_tile),
        ],
        [((tile, cols), row_tile)] * 2,
        [((rows, cols), BF)] * 2,
        9,
    )


def decay_block(first, count, wide, number_col, number_row, log_decay):
    distance = (
        first
        + lax.broadcasted_iota(jnp.int32, (count, wide), 0)
        - lax.broadcasted_iota(jnp.int32, (count, wide), 1)
    )
    linked = (number_col == number_row) & (number_col >= 0) & (distance >= 0)
    exponent = jnp.maximum(distance, 0).astype(F32)
    return jnp.where(linked, jnp.exp(log_decay * exponent), 0.0)


def own_column(table):
    here = lax.broadcasted_iota(jnp.int32, table.shape, 1) == pl.program_id(0)
    return jnp.sum(jnp.where(here, table, 0.0), axis=1, keepdims=True)


def retain(q, k, v, number, exit_weight, log_decay, tile=256):
    rows = q.shape[0]
    heads = q.shape[1] // KD

    def kernel(decay_ref, q_ref, k_ref, v_ref, col_ref, row_ref, exit_ref, out_ref, state_ref):
        decay = decay_ref[pl.program_id(0)]
        for first in range(0, rows, tile):
            wide = first + tile
            scores = lax.dot_general(
                q_ref[first:wide], k_ref[:wide], (((1,), (1,)), ((), ())), preferred_element_type=F32
            )
            mask = decay_block(first, tile, wide, col_ref[first:wide], row_ref[:, :wide], decay)
            out_ref[first:wide] = jnp.dot(
                (scores * mask).astype(BF), v_ref[:wide], preferred_element_type=F32
            )
        kd = (k_ref[...].astype(F32) * own_column(exit_ref[...])).astype(BF)
        state_ref[0] = lax.dot_general(
            kd, v_ref[...], (((0,), (0,)), ((), ())), preferred_element_type=F32
        )

    def head(h, *_):
        return (0, h)

    def head3(h, *_):
        return (h, 0, 0)

    return kernel_call(
        kernel,
        "retain",
        (heads,),
        [
            (q, (rows, KD), head),
            (k, (rows, KD), head),
            (v, (rows, VD), head),
            (number[:, None], (rows, 1), fixed),
            (number[None, :], (1, rows), fixed),
            (exit_weight, (rows, heads), fixed),
        ],
        [((rows, VD), head), ((1, KD, VD), head3)],
        [((rows, heads * VD), F32), ((heads, KD, VD), F32)],
        8,
        prefetch=(log_decay,),
    )


def gate_forward(n1, gate_mat, q, entry, state, local_out, scale, shift, tile=256):
    rows, width = n1.shape
    cols = gate_mat.shape[1]
    heads = cols // VD

    def kernel(
        n1_ref, mat_ref, q_ref, entry_ref, state_ref, local_ref, scale_ref, shift_ref,
        y_ref, gate_ref, hat_ref, dev_ref,
    ):
        gate = jnp.dot(n1_ref[...], mat_ref[...], preferred_element_type=F32)
        gate_ref[...] = gate
        swish = gate * jax.nn.sigmoid(gate)
        devs = []
        for h in range(heads):
            at = slice(h * VD, (h + 1) * VD)
            qd = (q_ref[:, h * KD : (h + 1) * KD].astype(F32) * entry_ref[:, h : h + 1]).astype(BF)
            r = local_ref[:, at] + jnp.dot(qd, state_ref[h], preferred_element_type=F32)
            hat, dev = standardize(r)
            hat_ref[:, at] = hat
            devs.append(dev)
            affine = hat * scale_ref[:, at] + shift_ref[:, at]
            y_ref[:, at] = (affine * swish[:, at]).astype(BF)
        dev_ref[...] = jnp.concatenate(devs, axis=1)

    return kernel_call(
        kernel,
        "gate_forward",
        (rows // tile,),
        [
            (n1, (tile, width), row_tile),
            (gate_mat, (width, cols), fixed),
            (q, (tile, heads * KD), row_tile),
            (entry, (tile, heads), row_tile),
            (state, state.shape, fixed3),
            (local_out, (tile, cols), row_tile),
            (scale[None, :], (1, cols), fixed),
            (shift[None, :], (1, cols), fixed),
        ],
        [((tile, cols), row_tile)] * 3 + [((tile, heads), row_tile)],
        [((rows, cols), BF), ((rows, cols), F32), ((rows, cols), F32), ((rows, heads), F32)],
        12,
    )


def gate_backward(d_branch, out_mat, gate, hat, dev, scale, shift, tile=256):
    rows, width = d_branch.shape
    cols = out_mat.shape[1]
    heads = cols // VD

    def kernel(
        db_ref, mat_ref, gate_ref, hat_ref, dev_ref, scale_ref, shift_ref,
        dg_ref, dr_ref, gain_ref, bias_ref,
    ):
        @pl.when(pl.program_id(0) == 0)
        def _():
            gain_ref[...] = jnp.zeros_like(gain_ref)
            bias_ref[...] = jnp.zeros_like(bias_ref)

        d_y = jnp.dot(db_ref[...], mat_ref[...], preferred_element_type=F32)
        for h in range(heads):
            at = slice(h * VD, (h + 1) * VD)
            z, dy, r_hat = gate_ref[:, at], d_y[:, at], hat_ref[:, at]
            sigma = jax.nn.sigmoid(z)
            affine = r_hat * scale_ref[:, at] + shift_ref[:, at]
            dg_ref[:, at] = (dy * affine * (sigma * (1.0 + z * (1.0 - sigma)))).astype(BF)
            d_affine = dy * (z * sigma)
            gain_ref[:, at] += jnp.sum(d_affine * r_hat, axis=0, keepdims=True)
            bias_ref[:, at] += jnp.sum(d_affine, axis=0, keepdims=True)
            d_hat = d_affine * scale_ref[:, at]
            dr_ref[:, at] = standardize_back(d_hat, r_hat, dev_ref[:, h : h + 1]).astype(BF)

    return kernel_call(
        kernel,
        "gate_backward",
        (rows // tile,),
        [
            (d_branch, (tile, width), row_tile),
            (out_mat, (width, cols), fixed),
            (gate, (tile, cols), row_tile),
            (hat, (tile, cols), row_tile),
            (dev, (tile, heads), row_tile),
            (scale[None, :], (1, cols), fixed),
            (shift[None, :], (1, cols), fixed),
        ],
        [((tile, cols), row_tile)] * 2 + [((1, cols), fixed)] * 2,
        [((rows, cols), BF), ((rows, cols), BF), ((1, cols), F32), ((1, cols), F32)],
        0,
    )


def feed_forward(n2, up_mat, up_shift, cotangent, down_mat, tile=256):
    rows, width = n2.shape
    cols = up_mat.shape[1]

    def kernel(n2_ref, up_ref, shift_ref, cot_ref, down_ref, act_ref, dup_ref, sum_ref):
        @pl.when(pl.program_id(0) == 0)
        def _():
            sum_ref[...] = jnp.zeros_like(sum_ref)

        for at in range(0, cols, 256):
            part = slice(at, at + 256)
            z = jnp.dot(n2_ref[...], up_ref[:, part], preferred_element_type=F32)
            z = z + shift_ref[:, part]
            d_act = jnp.dot(cot_ref[...], down_ref[:, part], preferred_element_type=F32)
            half = 0.5 * (1.0 + lax.erf(z * (0.5**0.5)))
            act_ref[:, part] = (z * half).astype(BF)
            slope = half + z * (jnp.exp(-0.5 * z * z) * (1.0 / math.sqrt(2.0 * math.pi)))
            d_up = (slope * d_act).astype(BF)
            dup_ref[:, part] = d_up
            sum_ref[:, part] += jnp.sum(d_up.astype(F32), axis=0, keepdims=True)

    return kernel_call(
        kernel,
        "feed_forward",
        (rows // tile,),
        [
            (n2, (tile, width), row_tile),
            (up_mat, (width, cols), fixed),
            (up_shift[None, :], (1, cols), fixed),
            (cotangent, (tile, width), row_tile),
            (down_mat, (width, cols), fixed),
        ],
        [((tile, cols), row_tile)] * 2 + [((1, cols), fixed)],
        [((rows, cols), BF), ((rows, cols), BF), ((1, cols), F32)],
        16,
    )


def retain_backward(q, k, v, d_r, state, number, entry, log_decay, cosine, sine, tile=256):
    rows = q.shape[0]
    heads = q.shape[1] // KD

    def kernel(
        decay_ref, q_ref, k_ref, v_ref, dr_ref, state_ref, col_ref, row_ref, entry_ref,
        cos_ref, sin_ref, dq_ref, dk_ref, dv_ref,
    ):
        decay = decay_ref[pl.program_id(0)]
        across = (((1,), (1,)), ((), ()))
        down = (((0,), (0,)), ((), ()))
        for first in reversed(range(0, rows, tile)):
            wide = first + tile
            here = slice(first, wide)
            q_i, dr_i = q_ref[here], dr_ref[here]
            mask = decay_block(first, tile, wide, col_ref[here], row_ref[:, :wide], decay)
            scores = lax.dot_general(q_i, k_ref[:wide], across, preferred_element_type=F32)
            weights = (scores * mask).astype(BF)
            d_scores = lax.dot_general(dr_i, v_ref[:wide], across, preferred_element_type=F32)
            d_scores = (d_scores * mask).astype(BF)
            dq = jnp.dot(d_scores, k_ref[:wide], preferred_element_type=F32)
            dq = dq + own_column(entry_ref[here]) * lax.dot_general(
                dr_i, state_ref[0], across, preferred_element_type=F32
            )
            dq_ref[here] = turn(dq, cos_ref[here], -sin_ref[here]).astype(BF)
            dk = lax.dot_general(d_scores, q_i, down, preferred_element_type=F32)
            dv = lax.dot_general(weights, dr_i, down, preferred_element_type=F32)
            if wide == rows:
                dk_ref[...] = dk
                dv_ref[...] = dv
            else:
                dk_ref[:wide] += dk
                dv_ref[:wide] += dv

    def head(h, *_):
        return (0, h)

    def head3(h, *_):
        return (h, 0, 0)

    return kernel_call(
        kernel,
        "retain_backward",
        (heads,),
        [
            (q, (rows, KD), head),
            (k, (rows, KD), head),
            (v, (rows, VD), head),
            (d_r, (rows, VD), head),
            (state, (1, KD, VD), head3),
            (number[:, None], (rows, 1), fixed),
            (number[None, :], (1, rows), fixed),
            (entry, (rows, heads), fixed),
            (cosine, (rows, KD // 2), fixed),
            (sine, (rows, KD // 2), fixed),
        ],
        [((rows, KD), head), ((rows, KD), head), ((rows, VD), head)],
        [((rows, heads * KD), BF), ((rows, heads * KD), F32), ((rows, heads * VD), F32)],
        0,
        prefetch=(log_decay,),
    )


def state_backward(k, v, exit_weight, leaving, dk, dv, cosine, sine, tile=256):
    rows = k.shape[0]
    heads = k.shape[1] // KD

    def kernel(
        k_ref, v_ref, exit_ref, leaving_ref, dk_in, dv_in, cos_ref, sin_ref, dk_ref, dv_ref
    ):
        for h in range(heads):
            at, wide = slice(h * KD, (h + 1) * KD), slice(h * VD, (h + 1) * VD)
            weight = exit_ref[:, h : h + 1]
            kd = (k_ref[:, at].astype(F32) * weight).astype(BF)
            d_k = dk_in[:, at] + weight * lax.dot_general(
                v_ref[:, wide], leaving_ref[h], (((1,), (1,)), ((), ())), preferred_element_type=F32
            )
            dk_ref[:, at] = turn(d_k, cos_ref[...], -sin_ref[...]).astype(BF)
            d_v = dv_in[:, wide] + jnp.dot(kd, leaving_ref[h], preferred_element_type=F32)
            dv_ref[:, wide] = d_v.astype(BF)

    return kernel_call(
        kernel,
        "state_backward",
        (rows // tile,),
        [
            (k, (tile, heads * KD), row_tile),
            (v, (tile, heads * VD), row_tile),
            (exit_weight, (tile, heads), row_tile),
            (leaving, leaving.shape, fixed3),
            (dk, (tile, heads * KD), row_tile),
            (dv, (tile, heads * VD), row_tile),
            (cosine, (tile, KD // 2), row_tile),
            (sine, (tile, KD // 2), row_tile),
        ],
        [((tile, heads * KD), row_tile), ((tile, heads * VD), row_tile)],
        [((rows, heads * KD), BF), ((rows, heads * VD), BF)],
        0,
    )


def second_norm(inputs, side, kept, other, gain, shift, tile=128):
    half, width = kept.shape
    steps = half // tile

    def kernel(side_ref, x_ref, kept_ref, other_ref, gain_ref, shift_ref, mid_ref, n2_ref):
        mid = x_ref[...].astype(F32) + (kept_ref[...].astype(F32) + other_ref[...].astype(F32))
        mid_ref[...] = mid
        hat, _ = standardize(mid)
        n2_ref[...] = (hat * gain_ref[...] + shift_ref[...]).astype(BF)

    return kernel_call(
        kernel,
        "second_norm",
        (steps,),
        [
            (inputs, (tile, width), lambda i, side_ref: (side_ref[0] * steps + i, 0)),
            (kept, (tile, width), row_tile),
            (other, (tile, width), row_tile),
            (gain[None, :], (1, width), fixed),
            (shift[None, :], (1, width), fixed),
        ],
        [((tile, width), row_tile)] * 2,
        [((half, width), F32), ((half, width), BF)],
        6,
        prefetch=(side[None],),
    )


def norm_backward(x, x_rows, kept, other, base, base_rows, gain, side, tile=128):
    half, width = kept.shape
    steps = half // tile

    def kernel(
        side_ref, x_ref, kept_ref, other_ref, base_ref, gain_ref,
        out_ref, low_ref, gain_out, bias_out,
    ):
        @pl.when(pl.program_id(0) == 0)
        def _():
            gain_out[...] = jnp.zeros_like(gain_out)
            bias_out[...] = jnp.zeros_like(bias_out)

        d_n = kept_ref[...].astype(F32) + other_ref[...].astype(F32)
        hat, dev = standardize(x_ref[...].astype(F32))
        gain_out[...] += jnp.sum(d_n * hat, axis=0, keepdims=True)
        bias_out[...] += jnp.sum(d_n, axis=0, keepdims=True)
        out = base_ref[...].astype(F32) + standardize_back(d_n * gain_ref[...], hat, dev)
        out_ref[...] = out
        low_ref[...] = out.astype(BF)

    def picked(i, side_ref):
        return (side_ref[0] * steps + i, 0)

    return kernel_call(
        kernel,
        "norm_backward",
        (steps,),
        [
            (x, (tile, width), picked if x_rows else row_tile),
            (kept, (tile, width), row_tile),
            (other, (tile, width), row_tile),
            (base, (tile, width), picked if base_rows else row_tile),
            (gain[None, :], (1, width), fixed),
        ],
        [((tile, width), row_tile)] * 2 + [((1, width), fixed)] * 2,
        [((half, width), F32), ((half, width), BF), ((1, width), F32), ((1, width), F32)],
        0,
        prefetch=(side[None],),
    )


def partial_rows(values, mats, which, added=(), pieces=1, tile=512):
    rows, width = values[0].shape[0], mats[0].shape[0]
    half, count = rows // 2, len(values)

    def kernel(which_ref, *refs):
        total = sum(
            lax.dot_general(v[...], m[...], (((1,), (1,)), ((), ())), preferred_element_type=F32)
            for v, m in zip(refs[:count], refs[count : 2 * count])
        )
        if added:
            total = total + jnp.concatenate(
                [ref[...].astype(F32) for ref in refs[2 * count : 2 * count + len(added)]], axis=0
            )
        for piece, ref in enumerate(refs[-pieces:]):
            ref[...] = total[piece * half // pieces : (piece + 1) * half // pieces].astype(BF)

    def column_tile(i, *_):
        return (0, i)

    ins = [(v, (half, v.shape[1]), lambda i, which_ref: (which_ref[0], 0)) for v in values]
    ins += [(m, (tile, m.shape[1]), row_tile) for m in mats]
    ins += [(part, (part.shape[0], tile), column_tile) for part in added]
    return kernel_call(
        kernel,
        "partial_rows",
        (width // tile,),
        ins,
        [((half // pieces, tile), column_tile)] * pieces,
        [((half // pieces, width), BF)] * pieces,
        0,
        prefetch=(which[None],),
    )


def finish_output(mid, kept, other, shift, tile=256):
    half, width = mid.shape

    def kernel(mid_ref, kept_ref, other_ref, shift_ref, out_ref):
        ffn = kept_ref[...].astype(F32) + other_ref[...].astype(F32)
        out_ref[...] = (mid_ref[...] + ffn + shift_ref[...]).astype(BF)

    return kernel_call(
        kernel,
        "finish_output",
        (half // tile,),
        [
            (mid, (tile, width), row_tile),
            (kept, (tile, width), row_tile),
            (other, (tile, width), row_tile),
            (shift[None, :], (1, width), fixed),
        ],
        [((tile, width), row_tile)],
        [((half, width), BF)],
        0,
    )[0]


def both_halves(mine, others, side, tile=256):
    half, width = mine.shape
    tile = min(tile, half // len(others))
    steps = half // tile
    each = steps // len(others)

    def kernel(side_ref, mine_ref, *refs):
        out_ref = refs[-1]
        at = pl.program_id(0)

        @pl.when(at // steps == side_ref[0])
        def _():
            out_ref[...] = mine_ref[...]

        for piece, ref in enumerate(refs[:-1]):

            @pl.when((at // steps != side_ref[0]) & (at % steps // each == piece))
            def _(ref=ref):
                out_ref[...] = ref[...]

    def within(which, first, count):
        def index(i, side_ref):
            return (jnp.clip(i - (side_ref[0] ^ which) * steps - first, 0, count - 1), 0)

        return index

    return kernel_call(
        kernel,
        "both_halves",
        (2 * steps,),
        [(mine, (tile, width), within(0, 0, steps))]
        + [(ref, (tile, width), within(1, p * each, each)) for p, ref in enumerate(others)],
        [((tile, width), row_tile)],
        [((2 * half, width), mine.dtype)],
        0,
        prefetch=(side[None],),
    )[0]


def ring_add(grads, arrived, place, step, halves):
    size = lax.axis_size("seq")
    rows = grads[0].shape[0] // size // (2 if halves else 1)
    kind = BF if step < size else F32

    def kernel(place_ref, *refs):
        for i in range(2):
            total = refs[i][...].astype(F32)
            if arrived:
                total = total + refs[2 + i][...].astype(F32)
            refs[i - 2][...] = total.astype(kind)

    def own(sign, low):
        def index(i, place_ref):
            owner = ring_owner(place_ref[0] + sign * step, size)
            return (2 * owner + low if halves else owner, 0)

        return index

    blocks = [(rows, grad.shape[1]) for grad in grads]
    ins = [(grads[0], blocks[0], own(-1, 0)), (grads[1], blocks[1], own(1, 1))]
    ins += [(block, block.shape, fixed) for block in arrived]
    return kernel_call(
        kernel,
        "ring_add",
        (1,),
        ins,
        [(block, fixed) for block in blocks],
        [(block, kind) for block in blocks],
        0,
        prefetch=(place[None],),
    )


def body(
    inputs,
    cotangent,
    lengths,
    offsets,
    first_gain,
    first_bias,
    query_weight,
    key_weight,
    value_weight,
    gate_weight,
    group_gain,
    group_bias,
    out_weight,
    second_gain,
    second_bias,
    up_weight,
    up_bias,
    down_weight,
    down_bias,
):
    size = lax.axis_size("seq")
    rows, width = inputs.shape
    shard = first_gain.shape[0]
    unit = group_gain.shape[0]
    heads = query_weight.shape[1] // KD
    half = rows // 2
    tp_me = lax.axis_index("tp")
    side = lax.rem(tp_me, 2)
    mine = side * half

    qk_own = jnp.concatenate([query_weight, key_weight], axis=1).astype(BF)
    v_own = value_weight.astype(BF)
    own_vector = jnp.concatenate(
        [
            first_gain,
            first_bias,
            second_gain,
            second_bias,
            down_bias,
            group_gain,
            group_bias,
            up_bias,
        ]
    ).astype(BF)[None, :]
    clock = Clock(2)
    qk_ring = gather(qk_own, own_vector)
    v_ring = gather(v_own)
    x = inputs
    (x,) = clock.add(0, qk_ring, x)
    (x,) = clock.add(1, v_ring, x)
    g_own = gate_weight.astype(BF)
    o_own = out_weight.astype(BF).T
    u_own = up_weight.astype(BF)
    w_own = down_weight.astype(BF).T
    g_ring, o_ring, u_ring, w_ring = [gather(own) for own in (g_own, o_own, u_own, w_own)]
    for lane, ring in enumerate((g_ring, o_ring, u_ring, w_ring)):
        clock.add(lane % 2, ring)

    first_row = lax.axis_index("seq") * rows
    log_decay = jnp.log(
        1.0
        - jnp.exp2(-5.0 - (tp_me * heads + jnp.arange(heads, dtype=jnp.int32)).astype(jnp.float32))
    )
    number, entry_weight, exit_weight, cosine, sine = block_decay(
        first_row, rows, lengths, offsets, log_decay
    )
    entry_cols, exit_cols = entry_weight.T, exit_weight.T
    x = clock.tick(x, count=3)
    x, cosine, sine, number, entry_cols, exit_cols = clock.tick(
        x, cosine, sine, number, entry_cols, exit_cols
    )
    x = clock.until(v_ring, x)

    if isinstance(qk_ring, Builtin):
        table = lax.all_gather(own_vector, "seq", axis=0, tiled=True).astype(F32)
    else:
        table = qk_ring.table().astype(F32)

    def wide(i):
        return table[:, i * shard : (i + 1) * shard].reshape(-1)

    def narrow(i):
        start = 5 * shard + i * unit
        return table[:, start : start + unit].reshape(-1)

    gain_one, bias_one, gain_two, bias_two, down_shift = [wide(i) for i in range(5)]
    group_scale, group_shift, up_shift = [narrow(i) for i in range(3)]

    n1 = norm_rows(x, gain_one, bias_one)
    n1 = clock.tick(n1)
    qk_mat = qk_ring.result()
    n1, qk_mat = clock.tick(n1, qk_mat)
    q, k = project_turn(n1, qk_mat, cosine, sine)
    q, k, n1 = clock.tick(q, k, n1, count=2)
    v_mat = v_ring.result()
    n1, v_mat = clock.tick(n1, v_mat)
    v = dot(n1, v_mat, ((1,), (0,))).astype(BF)
    q, k, v = clock.tick(q, k, v)
    local_out, local_state = retain(q, k, v, number, exit_cols, log_decay)
    local_out, local_state = clock.tick(local_out, local_state)
    state_parts = from_others(local_state.astype(BF), 1)
    local_out = clock.until(o_ring, local_out)

    def gathered_state(first, rest, direction):
        total, weight = first.astype(F32), 1.0
        for turn, part in enumerate(rest, 1):
            block = first_row - direction * turn * rows
            passed = passing_weight(block, rows, lengths, offsets, log_decay)
            weight = weight * passed
            total = total + weight[:, None, None] * part.astype(F32)
        return total.astype(BF)

    state = gathered_state(state_parts[0], state_parts[1:], 1)
    state, local_out = barrier(state, local_out)
    g_mat = g_ring.result()
    g_mat, state = clock.tick(g_mat, state)
    y, gate, r_hat, r_dev = gate_forward(
        n1, g_mat, q, entry_cols, state, local_out, group_scale, group_shift
    )
    y = clock.tick(y, count=2)
    o_mat = o_ring.result()
    y, o_mat = clock.tick(y, o_mat)

    def pick(values, which):
        return lax.dynamic_slice_in_dim(values, which * half, half)

    def tp_first(make, value):
        sent = make(pick(value, 1 - side)).astype(BF)
        sent, value = clock.tick(sent, value)
        sent = swap(sent, 1)
        return (make(pick(value, side)) + sent.astype(F32)).astype(BF)

    kept = tp_first(lambda part: dot(part, o_mat, ((1,), (1,))), y)
    kept = clock.tick(kept)
    other = swap(kept, 2)
    kept = clock.tick(kept, count=7)
    kept, other = barrier(kept, other)
    mid, n2_mine = second_norm(inputs, side, kept, other, gain_two, bias_two)
    n2_mine = clock.tick(n2_mine)
    n2 = both_halves(n2_mine, [swap(n2_mine, 1)], side)
    n2 = clock.until(w_ring, n2)
    u_mat = u_ring.result()
    w_mat = w_ring.result()
    act, d_up, grad_up_bias = feed_forward(n2, u_mat, up_shift, cotangent, w_mat)

    line = Line(grad_up_bias)
    pairs_two = [(i, i ^ 2) for i in range(lax.axis_size("tp"))]
    pairs_one = [(i, i ^ 1) for i in range(lax.axis_size("tp"))]

    def to_partner(block, pieces=2):
        count = block.shape[0] // pieces
        return [
            line.send(block[i * count : (i + 1) * count], "tp", pairs_one) for i in range(pieces)
        ]

    def partial_sent(values, mats, pieces=2):
        parts = line.run(lambda *v: partial_rows(v, mats, 1 - side, pieces=pieces), *values)
        parts = parts if isinstance(parts, tuple) else (parts,)
        return [line.send(part, "tp", pairs_one) for part in parts]

    def partial_kept(values, mats, sent):
        return line.run(lambda *v: partial_rows(v, mats, side, sent), *values)

    def gradient(x, dy):
        return dot(x, dy, ((0,), (0,)))

    grad_w = line.run(gradient, cotangent, act)
    sent_two = partial_sent((d_up,), (u_mat,), 1)
    grad_u = line.run(gradient, n2, d_up)
    kept_two = partial_kept((d_up,), (u_mat,), sent_two)
    other_two = line.send(kept_two, "tp", pairs_two)
    wu_back = reduce(grad_w, grad_u)
    line.tick(wu_back)
    sent_out = partial_sent((act,), (w_mat,), 1)
    kept_out = partial_kept((act,), (w_mat,), sent_out)
    line.tick(wu_back)
    line.tick(wu_back)
    d_mid, d_branch_mine, grad_second_gain, grad_second_bias = line.run(
        lambda kept, other: norm_backward(
            mid, False, kept, other, cotangent, True, gain_two, side
        ),
        kept_two,
        other_two,
    )
    d_branch_other = to_partner(d_branch_mine, 1)
    line.tick(wu_back)
    d_branch = line.run(lambda mine: both_halves(mine, d_branch_other, side), d_branch_mine)

    d_gate, d_r, grad_group_gain, grad_group_bias = line.run(
        lambda d: gate_backward(d, o_mat, gate, r_hat, r_dev, group_scale, group_shift), d_branch
    )
    line.tick(wu_back)

    def state_part(d_r):
        qd = (q.reshape(rows, heads, KD) * entry_cols[:, :, None]).astype(BF)
        return jnp.einsum(
            "scr,scq->crq", qd, d_r.reshape(rows, heads, VD), preferred_element_type=F32
        ).astype(BF)

    own_grad = line.run(state_part, d_r)
    leaving_parts = from_others(own_grad, -1, line.send)
    grad_o = line.run(gradient, d_branch, y)
    grad_g = line.run(gradient, n1, d_gate)
    line.tick(wu_back)
    og_back = reduce(grad_o, grad_g)
    line.tick(og_back)
    d_q, d_k, d_v = line.run(
        lambda d_r: retain_backward(
            q, k, v, d_r, state, number, entry_cols, log_decay, cosine, sine
        ),
        d_r,
    )
    line.tick(wu_back, og_back)
    leaving = line.run(lambda first, *rest: gathered_state(first, rest, -1), *leaving_parts)
    d_k, d_v = line.run(
        lambda d_k, d_v: state_backward(k, v, exit_cols, leaving, d_k, d_v, cosine, sine),
        d_k,
        d_v,
    )
    line.tick(wu_back)
    grad_v = line.run(gradient, n1, d_v)
    grad_qk = line.run(gradient, n1, jnp.concatenate([d_q, d_k], axis=1))
    line.tick(og_back)
    vqk_back = reduce(grad_v, grad_qk)
    line.tick(vqk_back)
    d_all = (d_gate, d_v, d_q, d_k)
    mats_all = (g_mat, v_mat, qk_mat[:, : heads * KD], qk_mat[:, heads * KD :])
    sent_one = partial_sent(d_all, mats_all, 1)
    line.tick(og_back, vqk_back)
    kept_one = partial_kept(d_all, mats_all, sent_one)
    other_one = line.send(kept_one, "tp", pairs_two)
    line.tick(og_back, vqk_back, og_back, vqk_back, og_back)
    grad_mine, _, grad_first_gain, grad_first_bias = line.run(
        lambda kept, other: norm_backward(
            inputs, True, kept, other, d_mid, False, gain_one, side
        ),
        kept_one,
        other_one,
    )
    other_out = line.send(kept_out, "tp", pairs_two)
    grad_other = to_partner(grad_mine, 1)
    line.tick(vqk_back, og_back)
    grad_inputs = line.run(lambda mine: both_halves(mine, grad_other, side), grad_mine)
    line.tick(vqk_back, og_back)

    grad_up_bias = line.token
    grad_down_bias = jnp.sum(cotangent.astype(F32), axis=0)
    vectors = jnp.concatenate(
        [
            vector.reshape(size, -1)
            for vector in (
                grad_first_gain,
                grad_first_bias,
                grad_second_gain,
                grad_second_bias,
                grad_down_bias,
                grad_group_gain,
                grad_group_bias,
                grad_up_bias,
            )
        ],
        axis=1,
    )
    small = small_reduce(vectors)
    halves = small[: 4 * shard]
    halves = halves + swap(halves, 1)
    line.token = halves
    line.tick(vqk_back, og_back)
    output_mine = line.run(
        lambda kept: finish_output(mid, kept, other_out, down_shift), kept_out
    )
    output_other = to_partner(output_mine, 1)
    line.tick(vqk_back)
    output = line.run(lambda mine: both_halves(mine, output_other, side), output_mine)
    while not (og_back.ended and vqk_back.ended):
        line.tick(og_back, vqk_back)
    halves = line.token
    own = [halves[i * shard : (i + 1) * shard] for i in range(4)]
    own_down_bias = small[4 * shard : 5 * shard]
    own_units = [small[5 * shard + i * unit : 5 * shard + (i + 1) * unit] for i in range(3)]
    own_w, own_u = wu_back.result()
    own_o, own_g = og_back.result()
    own_v, own_qk = vqk_back.result()
    own_q, own_k = own_qk[:, : heads * KD], own_qk[:, heads * KD :]
    return (
        output,
        grad_inputs,
        own[0],
        own[1],
        own_q,
        own_k,
        own_v,
        own_g,
        own_units[0],
        own_units[1],
        own_o.T,
        own[2],
        own[3],
        own_u,
        own_units[2],
        own_w.T,
        own_down_bias,
    )


def solution(mesh):
    placed = (
        P("seq", None),
        P("seq", None),
        P(),
        P(),
        P("seq"),
        P("seq"),
        P("seq", "tp"),
        P("seq", "tp"),
        P("seq", "tp"),
        P("seq", "tp"),
        P(("tp", "seq")),
        P(("tp", "seq")),
        P("tp", "seq"),
        P("seq"),
        P("seq"),
        P("seq", "tp"),
        P(("tp", "seq")),
        P("tp", "seq"),
        P("seq"),
    )
    return jax.shard_map(
        body,
        mesh=mesh,
        in_specs=placed,
        out_specs=(
            P("seq", None),
            P("seq", None),
            P("seq"),
            P("seq"),
            P("seq", "tp"),
            P("seq", "tp"),
            P("seq", "tp"),
            P("seq", "tp"),
            P(("tp", "seq")),
            P(("tp", "seq")),
            P("tp", "seq"),
            P("seq"),
            P("seq"),
            P("seq", "tp"),
            P(("tp", "seq")),
            P("tp", "seq"),
            P("seq"),
        ),
        check_vma=False,
    )
```

time: 2440 us -> 879 us (0.36)
  waiting for transfers between devices: 1740 us -> 250 us
  Pallas kernels: 0 us -> 279 us
  blocking collectives: 201 us -> 0 us
  matrix products: 219 us -> 74.2 us
  starting transfers between devices: 99.5 us -> 185 us
  other arithmetic: 111 us -> 29.3 us
    reduce_scatter x7 -> x0, waiting for transfers between devices: 873 us -> none  [the longest x1 153 us: body(): lax.psum_scatter(grad_up_weight, 'seq', scatter_dimension=0, tiled=True)]
    psum x3 -> x0, waiting for transfers between devices: 437 us -> none  [the longest x1 202 us: body(): ffn_rows = lax.psum(ffn_part, 'tp') + down_shift.astype(jnp.float32)]
    pallas_call x0 -> x52, Pallas kernels: none -> 279 us  [the longest x46 253 us: kernel_call(): pl.pallas_call(body, out_shape=[jax.ShapeDtypeStruct(s, t) for s, t in sh...]
    all_gather x7 -> x0, waiting for transfers between devices: 176 us -> none  [the longest x1 65.9 us: body(): lax.all_gather(down_weight.astype(jnp.bfloat16), 'seq', axis=1, tiled=True)]
    all_gather x8 -> x0, blocking collectives: 162 us -> none  [the longest x1 35.3 us: body(): lax.all_gather(up_bias.astype(jnp.bfloat16), 'seq', axis=0, tiled=True)]
    dot_general x33 -> x10, matrix products: 219 us -> 74.2 us  [the longest x9 71 us: dot(): return lax.dot_general(a, b, (dims, ((), ())), preferred_element_type=F32)]
    ppermute x14 -> x153, starting transfers between devices: 98.8 us -> 185 us  [the longest x133 167 us: tick(): lax.ppermute(block, 'seq', route)]
    reduce_sum x13 -> x1, other arithmetic: 46 us -> 2.83 us  [body(): grad_down_bias = jnp.sum(cotangent.astype(F32), axis=0)]
  transfers between devices with their start and end apart: 31 -> 153, of which waited for: 27 -> 70; matrix products, arithmetic and copies ran while one was open for 9% -> 11% of each run, Pallas kernels for 0% -> 20%
where the time goes in v1:
time: 879 us; the launch traced here: 871 us
  Pallas kernels  279 us (32%)
  waiting for transfers between devices  250 us (28%)
  starting transfers between devices  185 us (21%)
  matrix products  74.2 us (8%)
  local copies, waits for them, and re-layouts  48.2 us (5%)
  other arithmetic  29.3 us (3%)
    pallas_call x46, Pallas kernels, kernel_call(): pl.pallas_call(body, out_shape=[jax.ShapeDtypeStruct(s, t) for s, t in sh...  253 us
    ppermute x133, waiting for transfers between devices, tick(): lax.ppermute(block, 'seq', route)  215 us
    ppermute x133, starting transfers between devices, tick(): lax.ppermute(block, 'seq', route)  167 us
    dot_general x9, matrix products, dot(): return lax.dot_general(a, b, (dims, ((), ())), preferred_element_type=F32)  71 us
    unnamed x290, local copies, waits for them, and re-layouts  33.5 us
    pallas_call x6, Pallas kernels, assemble(): pl.pallas_call(kernel, out_shape=jax.ShapeDtypeStruct((size * rows, cols)...  25.9 us
    ppermute x11, waiting for transfers between devices, send(): return lax.ppermute(block, axis, route)  20 us
  transfers between devices with their start and end apart: 153, of which 70 were waited for; matrix products, arithmetic and copies ran while one was open for 11% of the time, Pallas kernels for 20%

profile of v1, /device:TPU:0, one launch (start us, length us, event | category | flops | bytes accessed | tf_op | source)
XLA Modules:
  0.0 871.2 jit_solution(12735033400431586492)
XLA Ops:
  121.1 8.6 query_key.1
  138.6 9.5 %convolution_convert_fusion.1.v_ref = bf16[1024,1024]{1,0:T(8,128)(2,1)} fusion(bf16[1024,2048]{1,0:T(8,128)(2,1)} %first_norm.1.n1_ref, bf16[2048,1024]{1,0:T(8,128)(2,1)} %assemble.7.refs_5_), kind=kOutput, calls=%fused_computation.9 | convolution fusion | flops 4296015872 | bytes 10485760 | tf_op jit(solution)/shard_map/dot_general | solution.py:19
  183.6 9.4 %collective-permute-done.54.refs_13_ = bf16[128,1024]{1,0:T(8,128)(2,1)} collective-permute-done((bf16[128,1024]{1,0:T(8,128)(2,1)}, bf16[128,1024]{1,0:T(8,128)(2,1)}, u32[]{:S(2)}, u32[]{:S(2)}) %collective-permute-start.54) | collective-permute-done | bytes 262176 | tf_op jit(solution)/shard_map/ppermute | solution.py:111
  194.8 14.3 %collective-permute-start.66 = (bf16[128,1024]{1,0:T(8,128)(2,1)}, bf16[128,1024]{1,0:T(8,128)(2,1)S(1)}, u32[]{:S(2)}, u32[]{:S(2)}) collective-permute-start(bf16[128,1024]{1,0:T(8,128)(2,1)} %collective-permute-done.60.refs_13_), channel_id=1, source_target_pairs={{8,0},{16,8},{24,16},{28,24},{20,28},{12,20},{4,12},{0,4},{9,1},{1... | collective-permute-start | bytes 786440 | tf_op jit(solution)/shard_map/ppermute | solution.py:111
  212.7 8.5 collective-permute-done.57.refs_7_
  230.2 12.1 %gate_forward.1 = (bf16[1024,1024]{1,0:T(8,128)(2,1)}, f32[1024,1024]{1,0:T(8,128)}, f32[1024,1024]{1,0:T(8,128)}, f32[1024,2]{1,0:T(8,128)}) custom-call(bf16[1024,2048]{1,0:T(8,128)(2,1)} %first_norm.1.n1_ref, bf16[2048,1024]{1,0:T(8,128)(2,1)} %assemble.8.mat_ref.refs_4_, bf16[1024,512]{1,0:T(8,128)(2,1)} %get-tuple-element.590.q_ref, ...), custom_call_target="tpu_custom_call" | custom-call | flops 12000000000 | tf_op jit(solution)/shard_map/gate_forward/pallas_call | solution.py:326
  313.6 8.6 collective-permute-start.94
  345.3 16.4 %feed_forward.1 = (bf16[1024,1024]{1,0:T(8,128)(2,1)}, bf16[1024,1024]{1,0:T(8,128)(2,1)}, f32[1,1024]{1,0:T(1,128)}) custom-call(bf16[1024,2048]{1,0:T(8,128)(2,1)} %both_halves.4.n2_ref, bf16[2048,1024]{1,0:T(8,128)(2,1)} %assemble.10.up_ref.refs_1_, f32[1,1024]{1,0:T(1,128)} %bitcast.106, bf16[1024,2048]{1,0:T(8,128)(2,1)} %base_ref.1, ...), custom_call_target="tpu_custom_call" | custom-call | flops 16000000000 | tf_op jit(solution)/shard_map/feed_forward/pallas_call | solution.py:326
  361.7 10.7 %fusion.30.refs_0_ = f32[2048,1024]{1,0:T(8,128)} fusion(bf16[1024,2048]{1,0:T(8,128)(2,1)} %base_ref.1, bf16[1024,1024]{1,0:T(8,128)(2,1)} %get-tuple-element.701.refs_0_), kind=kOutput, calls=%fused_computation.109 | convolution fusion | flops 4294967296 | bytes 14680064 | tf_op jit(solution)/shard_map/dot_general | solution.py:19
  379.2 9.0 %fusion.31.refs_1_ = f32[2048,1024]{1,0:T(8,128)} fusion(bf16[1024,2048]{1,0:T(8,128)(2,1)} %both_halves.4.n2_ref, bf16[1024,1024]{1,0:T(8,128)(2,1)S(1)} %copy-done.6), kind=kOutput, calls=%fused_computation.110 | convolution fusion | flops 4294967296 | bytes 14680064 | tf_op jit(solution)/shard_map/dot_general | solution.py:19
  425.1 11.6 %collective-permute-done.101.refs_2_ = bf16[256,1024]{1,0:T(8,128)(2,1)S(1)} collective-permute-done((bf16[256,1024]{1,0:T(8,128)(2,1)}, bf16[256,1024]{1,0:T(8,128)(2,1)S(1)}, u32[]{:S(2)}, u32[]{:S(2)}) %collective-permute-start.101) | collective-permute-done | bytes 524320 | tf_op jit(solution)/shard_map/ppermute | solution.py:176
  441.8 10.4 %collective-permute-done.98.other_ref = bf16[512,2048]{1,0:T(8,128)(2,1)} collective-permute-done((bf16[512,2048]{1,0:T(8,128)(2,1)S(1)}, bf16[512,2048]{1,0:T(8,128)(2,1)}, u32[]{:S(2)}, u32[]{:S(2)}) %collective-permute-start.98) | collective-permute-done | bytes 2097184 | tf_op jit(solution)/shard_map/ppermute | solution.py:145
  452.2 8.7 norm_backward.2
  463.0 12.2 %collective-permute-done.103.refs_2_ = bf16[256,1024]{1,0:T(8,128)(2,1)S(1)} collective-permute-done((bf16[256,1024]{1,0:T(8,128)(2,1)S(1)}, bf16[256,1024]{1,0:T(8,128)(2,1)S(1)}, u32[]{:S(2)}, u32[]{:S(2)}) %collective-permute-start.103) | collective-permute-done | bytes 524320 | tf_op jit(solution)/shard_map/ppermute | solution.py:176
  489.6 12.2 %gate_backward.1 = (bf16[1024,1024]{1,0:T(8,128)(2,1)}, bf16[1024,1024]{1,0:T(8,128)(2,1)}, f32[1,1024]{1,0:T(1,128)}, f32[1,1024]{1,0:T(1,128)}) custom-call(bf16[1024,2048]{1,0:T(8,128)(2,1)} %both_halves.5.db_ref, bf16[2048,1024]{1,0:T(8,128)(2,1)} %assemble.9.mat_ref, f32[1024,1024]{1,0:T(8,128)} %get-tuple-element.743.gate_ref, ...), custom_call_target="tpu_custom_call" | custom-call | tf_op jit(solution)/shard_map/gate_backward/pallas_call | solution.py:326
  509.6 8.6 fusion.32.refs_0_
  545.6 12.0 %retain_backward.1 = (bf16[1024,512]{1,0:T(8,128)(2,1)}, f32[1024,512]{1,0:T(8,128)}, f32[1024,1024]{1,0:T(8,128)}) custom-call(f32[2]{0:T(128)} %copy-done.68, bf16[1024,512]{1,0:T(8,128)(2,1)} %get-tuple-element.590.q_ref, bf16[1024,512]{1,0:T(8,128)(2,1)} %get-tuple-element.591.k_ref, bf16[1024,1024]{1,0:T(8,128)(2,1)} %convolution_convert_fusion.1.v_ref, ...), custom_call_target="tpu_custom_call" | custom-call | tf_op jit(solution)/shard_map/retain_backward/pallas_call | solution.py:326
  571.3 14.5 %collective-permute-done.113.refs_3_ = bf16[256,1024]{1,0:T(8,128)(2,1)S(1)} collective-permute-done((bf16[256,1024]{1,0:T(8,128)(2,1)}, bf16[256,1024]{1,0:T(8,128)(2,1)S(1)}, u32[]{:S(2)}, u32[]{:S(2)}) %collective-permute-start.113) | collective-permute-done | bytes 524320 | tf_op jit(solution)/shard_map/ppermute | solution.py:176
  609.0 9.2 %fusion.34.refs_0_ = f32[2048,1024]{1,0:T(8,128)} fusion(bf16[1024,2048]{1,0:T(8,128)(2,1)} %first_norm.1.n1_ref, bf16[1024,1024]{1,0:T(8,128)(2,1)S(1)} %copy-done.3), kind=kOutput, calls=%fused_computation.113 | convolution fusion | flops 4294967296 | bytes 14680064 | tf_op jit(solution)/shard_map/dot_general | solution.py:19
  631.2 11.5 %partial_rows.10 = bf16[512,2048]{1,0:T(8,128)(2,1)} custom-call(s32[1]{0:T(128)} %bitcast.13.which_ref, bf16[1024,1024]{1,0:T(8,128)(2,1)} %get-tuple-element.878.refs_0_, bf16[1024,1024]{1,0:T(8,128)(2,1)} %get-tuple-element.879.refs_1_, bf16[1024,512]{1,0:T(8,128)(2,1)} %get-tuple-element.880.refs_2_, bf16[1024,512]{1,0:T(8,128)(2,1)} %get-tuple-element.881.refs_3_, ...), custom_call_target="tpu_custom_call" | custom-call | tf_op jit(solution)/shard_map/partial_rows/pallas_call | solution.py:326
  646.8 10.9 %collective-permute-done.122.refs_2_ = bf16[256,1024]{1,0:T(8,128)(2,1)S(1)} collective-permute-done((bf16[256,1024]{1,0:T(8,128)(2,1)}, bf16[256,1024]{1,0:T(8,128)(2,1)S(1)}, u32[]{:S(2)}, u32[]{:S(2)}) %collective-permute-start.122) | collective-permute-done | bytes 524320 | tf_op jit(solution)/shard_map/ppermute | solution.py:176
  674.2 12.0 %partial_rows.11.kept_ref = bf16[512,2048]{1,0:T(8,128)(2,1)} custom-call(s32[1]{0:T(128)} %bitcast.side_ref.which_ref, bf16[1024,1024]{1,0:T(8,128)(2,1)} %get-tuple-element.878.refs_0_, bf16[1024,1024]{1,0:T(8,128)(2,1)} %get-tuple-element.879.refs_1_, bf16[1024,512]{1,0:T(8,128)(2,1)} %get-tuple-element.880.refs_2_, ...), custom_call_target="tpu_custom_call" | custom-call | tf_op jit(solution)/shard_map/partial_rows/pallas_call | solution.py:326
  690.6 11.0 %collective-permute-done.126.refs_2_ = bf16[256,1024]{1,0:T(8,128)(2,1)S(1)} collective-permute-done((bf16[256,1024]{1,0:T(8,128)(2,1)}, bf16[256,1024]{1,0:T(8,128)(2,1)S(1)}, u32[]{:S(2)}, u32[]{:S(2)}) %collective-permute-start.126) | collective-permute-done | bytes 524320 | tf_op jit(solution)/shard_map/ppermute | solution.py:176
  750.0 8.7 norm_backward.3
  (706 shorter events, 605.5 us)
Async XLA Ops:
  172.3 36.8 %collective-permute-start.63 = (bf16[2,256,512]{2,1,0:T(8,128)(2,1)S(1)}, bf16[2,256,512]{2,1,0:T(8,128)(2,1)S(1)}, u32[]{:S(2)}, u32[]{:S(2)}) collective-permute-start(bf16[2,256,512]{2,1,0:T(8,128)(2,1)S(1)} %convert_element_type.131), channel_id=1, source_target_pairs={{0,4},{4,8},{8,12},{12,16},{16,20},{20,24},{24,28},{1,5},{5,9},{9,... | collective-permute-start | bytes 1572872 | tf_op jit(solution)/shard_map/ppermute | solution.py:28
  175.9 35.7 %collective-permute-start.64 = (bf16[2,256,512]{2,1,0:T(8,128)(2,1)S(1)}, bf16[2,256,512]{2,1,0:T(8,128)(2,1)S(1)}, u32[]{:S(2)}, u32[]{:S(2)}) collective-permute-start(bf16[2,256,512]{2,1,0:T(8,128)(2,1)S(1)} %convert_element_type.131), channel_id=1, source_target_pairs={{0,8},{4,12},{8,16},{12,20},{16,24},{20,28},{1,9},{5,13},{9,17},{1... | collective-permute-start | bytes 1572872 | tf_op jit(solution)/shard_map/ppermute | solution.py:28
  193.0 28.2 %collective-permute-start.65 = (bf16[128,1024]{1,0:T(8,128)(2,1)}, bf16[128,1024]{1,0:T(8,128)(2,1)S(1)}, u32[]{:S(2)}, u32[]{:S(2)}) collective-permute-start(bf16[128,1024]{1,0:T(8,128)(2,1)} %collective-permute-done.59.refs_6_), channel_id=1, source_target_pairs={{0,8},{8,16},{16,24},{24,28},{28,20},{20,12},{12,4},{4,0},{1,9},{9... | collective-permute-start | bytes 786440 | tf_op jit(solution)/shard_map/ppermute | solution.py:111
  194.8 26.4 %collective-permute-start.66 = (bf16[128,1024]{1,0:T(8,128)(2,1)}, bf16[128,1024]{1,0:T(8,128)(2,1)S(1)}, u32[]{:S(2)}, u32[]{:S(2)}) collective-permute-start(bf16[128,1024]{1,0:T(8,128)(2,1)} %collective-permute-done.60.refs_13_), channel_id=1, source_target_pairs={{8,0},{16,8},{24,16},{28,24},{20,28},{12,20},{4,12},{0,4},{9,1},{1... | collective-permute-start | bytes 786440 | tf_op jit(solution)/shard_map/ppermute | solution.py:111
  270.8 51.4 %collective-permute-start.92 = (bf16[512,2048]{1,0:T(8,128)(2,1)S(1)}, bf16[512,2048]{1,0:T(8,128)(2,1)S(1)}, u32[]{:S(2)}, u32[]{:S(2)}) collective-permute-start(bf16[512,2048]{1,0:T(8,128)(2,1)S(1)} %add_convert_fusion.kept_ref), channel_id=1, source_target_pairs={{0,2},{1,3},{2,0},{3,1},{4,6},{5,7},{6,4},{7,5},{8,10},{9,11},{10,... | collective-permute-start | bytes 6291464 | tf_op jit(solution)/shard_map/ppermute | solution.py:268
  404.0 48.1 %collective-permute-start.98 = (bf16[512,2048]{1,0:T(8,128)(2,1)S(1)}, bf16[512,2048]{1,0:T(8,128)(2,1)}, u32[]{:S(2)}, u32[]{:S(2)}) collective-permute-start(bf16[512,2048]{1,0:T(8,128)(2,1)S(1)} %copy-done.5), channel_id=1, source_target_pairs={{0,2},{1,3},{2,0},{3,1},{4,6},{5,7},{6,4},{7,5},{8,10},{9,11},{10,... | collective-permute-start | bytes 6291464 | tf_op jit(solution)/shard_map/ppermute | solution.py:145
  460.9 23.4 %collective-permute-start.105 = (bf16[512,2048]{1,0:T(8,128)(2,1)}, bf16[512,2048]{1,0:T(8,128)(2,1)}, u32[]{:S(2)}, u32[]{:S(2)}) collective-permute-start(bf16[512,2048]{1,0:T(8,128)(2,1)} %get-tuple-element.740.mine_ref), channel_id=1, source_target_pairs={{0,1},{1,0},{2,3},{3,2},{4,5},{5,4},{6,7},{7,6},{8,9},{9,8},{10,11... | collective-permute-start | bytes 6291464 | tf_op jit(solution)/shard_map/ppermute | solution.py:145
  540.3 25.1 %collective-permute-start.112 = (bf16[256,1024]{1,0:T(8,128)(2,1)}, bf16[256,1024]{1,0:T(8,128)(2,1)S(1)}, u32[]{:S(2)}, u32[]{:S(2)}) collective-permute-start(bf16[256,1024]{1,0:T(8,128)(2,1)} %get-tuple-element.787), channel_id=1, source_target_pairs={{0,8},{8,16},{16,24},{24,28},{28,20},{20,12},{12,4},{4,0},{1,9},{9... | collective-permute-start | bytes 1572872 | tf_op jit(solution)/shard_map/ppermute | solution.py:176
  543.0 46.6 %collective-permute-start.109 = (bf16[2,256,512]{2,1,0:T(8,128)(2,1)}, bf16[2,256,512]{2,1,0:T(8,128)(2,1)S(1)}, u32[]{:S(2)}, u32[]{:S(2)}) collective-permute-start(bf16[2,256,512]{2,1,0:T(8,128)(2,1)} %fusion.3), channel_id=1, source_target_pairs={{8,0},{12,4},{16,8},{20,12},{24,16},{28,20},{9,1},{13,5},{17,9},{2... | collective-permute-start | bytes 1572872 | tf_op jit(solution)/shard_map/ppermute | solution.py:145
  544.3 45.3 %collective-permute-start.108 = (bf16[2,256,512]{2,1,0:T(8,128)(2,1)}, bf16[2,256,512]{2,1,0:T(8,128)(2,1)}, u32[]{:S(2)}, u32[]{:S(2)}) collective-permute-start(bf16[2,256,512]{2,1,0:T(8,128)(2,1)} %fusion.3), channel_id=1, source_target_pairs={{4,0},{8,4},{12,8},{16,12},{20,16},{24,20},{28,24},{5,1},{9,5},{13... | collective-permute-start | bytes 1572872 | tf_op jit(solution)/shard_map/ppermute | solution.py:145
  557.6 28.2 %collective-permute-start.113 = (bf16[256,1024]{1,0:T(8,128)(2,1)}, bf16[256,1024]{1,0:T(8,128)(2,1)S(1)}, u32[]{:S(2)}, u32[]{:S(2)}) collective-permute-start(bf16[256,1024]{1,0:T(8,128)(2,1)} %get-tuple-element.788), channel_id=1, source_target_pairs={{8,0},{16,8},{24,16},{28,24},{20,28},{12,20},{4,12},{0,4},{9,1},{1... | collective-permute-start | bytes 1572872 | tf_op jit(solution)/shard_map/ppermute | solution.py:176
  564.0 40.2 %collective-permute-start.116 = (bf16[256,1024]{1,0:T(8,128)(2,1)}, bf16[256,1024]{1,0:T(8,128)(2,1)S(1)}, u32[]{:S(2)}, u32[]{:S(2)}) collective-permute-start(bf16[256,1024]{1,0:T(8,128)(2,1)} %get-tuple-element.818), channel_id=1, source_target_pairs={{0,8},{8,16},{16,24},{24,28},{28,20},{20,12},{12,4},{4,0},{1,9},{9... | collective-permute-start | bytes 1572872 | tf_op jit(solution)/shard_map/ppermute | solution.py:176
  565.4 38.8 %collective-permute-start.117 = (bf16[256,1024]{1,0:T(8,128)(2,1)}, bf16[256,1024]{1,0:T(8,128)(2,1)S(1)}, u32[]{:S(2)}, u32[]{:S(2)}) collective-permute-start(bf16[256,1024]{1,0:T(8,128)(2,1)} %get-tuple-element.819), channel_id=1, source_target_pairs={{8,0},{16,8},{24,16},{28,24},{20,28},{12,20},{4,12},{0,4},{9,1},{1... | collective-permute-start | bytes 1572872 | tf_op jit(solution)/shard_map/ppermute | solution.py:176
  599.2 25.8 %collective-permute-start.118 = (bf16[256,1024]{1,0:T(8,128)(2,1)}, bf16[256,1024]{1,0:T(8,128)(2,1)S(1)}, u32[]{:S(2)}, u32[]{:S(2)}) collective-permute-start(bf16[256,1024]{1,0:T(8,128)(2,1)} %get-tuple-element.842), channel_id=1, source_target_pairs={{0,8},{8,16},{16,24},{24,28},{28,20},{20,12},{12,4},{4,0},{1,9},{9... | collective-permute-start | bytes 1572872 | tf_op jit(solution)/shard_map/ppermute | solution.py:176
  600.2 24.8 %collective-permute-start.119 = (bf16[256,1024]{1,0:T(8,128)(2,1)}, bf16[256,1024]{1,0:T(8,128)(2,1)}, u32[]{:S(2)}, u32[]{:S(2)}) collective-permute-start(bf16[256,1024]{1,0:T(8,128)(2,1)} %get-tuple-element.843), channel_id=1, source_target_pairs={{8,0},{16,8},{24,16},{28,24},{20,28},{12,20},{4,12},{0,4},{9,1},{1... | collective-permute-start | bytes 1572872 | tf_op jit(solution)/shard_map/ppermute | solution.py:176
  642.6 30.3 %collective-permute-start.128 = (bf16[512,2048]{1,0:T(8,128)(2,1)}, bf16[512,2048]{1,0:T(8,128)(2,1)S(1)}, u32[]{:S(2)}, u32[]{:S(2)}) collective-permute-start(bf16[512,2048]{1,0:T(8,128)(2,1)} %partial_rows.10), channel_id=1, source_target_pairs={{0,1},{1,0},{2,3},{3,2},{4,5},{5,4},{6,7},{7,6},{8,9},{9,8},{10,11... | collective-permute-start | bytes 6291464 | tf_op jit(solution)/shard_map/ppermute | solution.py:145
  644.7 23.7 %collective-permute-start.120 = (bf16[256,1024]{1,0:T(8,128)(2,1)}, bf16[256,1024]{1,0:T(8,128)(2,1)S(1)}, u32[]{:S(2)}, u32[]{:S(2)}) collective-permute-start(bf16[256,1024]{1,0:T(8,128)(2,1)} %get-tuple-element.851), channel_id=1, source_target_pairs={{0,8},{8,16},{16,24},{24,28},{28,20},{20,12},{12,4},{4,0},{1,9},{9... | collective-permute-start | bytes 1572872 | tf_op jit(solution)/shard_map/ppermute | solution.py:176
  645.7 23.4 %collective-permute-start.121 = (bf16[256,1024]{1,0:T(8,128)(2,1)}, bf16[256,1024]{1,0:T(8,128)(2,1)S(1)}, u32[]{:S(2)}, u32[]{:S(2)}) collective-permute-start(bf16[256,1024]{1,0:T(8,128)(2,1)} %get-tuple-element.852), channel_id=1, source_target_pairs={{8,0},{16,8},{24,16},{28,24},{20,28},{12,20},{4,12},{0,4},{9,1},{1... | collective-permute-start | bytes 1572872 | tf_op jit(solution)/shard_map/ppermute | solution.py:176
  686.3 62.4 %collective-permute-start.135 = (bf16[512,2048]{1,0:T(8,128)(2,1)}, bf16[512,2048]{1,0:T(8,128)(2,1)S(1)}, u32[]{:S(2)}, u32[]{:S(2)}) collective-permute-start(bf16[512,2048]{1,0:T(8,128)(2,1)} %partial_rows.11.kept_ref), channel_id=1, source_target_pairs={{0,2},{1,3},{2,0},{3,1},{4,6},{5,7},{6,4},{7,5},{8,10},{9,11},{10,... | collective-permute-start | bytes 6291464 | tf_op jit(solution)/shard_map/ppermute | solution.py:145
  688.6 24.3 %collective-permute-start.124 = (bf16[256,1024]{1,0:T(8,128)(2,1)}, bf16[256,1024]{1,0:T(8,128)(2,1)S(1)}, u32[]{:S(2)}, u32[]{:S(2)}) collective-permute-start(bf16[256,1024]{1,0:T(8,128)(2,1)} %get-tuple-element.873), channel_id=1, source_target_pairs={{0,8},{8,16},{16,24},{24,28},{28,20},{20,12},{12,4},{4,0},{1,9},{9... | collective-permute-start | bytes 1572872 | tf_op jit(solution)/shard_map/ppermute | solution.py:176
  689.6 24.3 %collective-permute-start.125 = (bf16[256,1024]{1,0:T(8,128)(2,1)}, bf16[256,1024]{1,0:T(8,128)(2,1)S(1)}, u32[]{:S(2)}, u32[]{:S(2)}) collective-permute-start(bf16[256,1024]{1,0:T(8,128)(2,1)} %get-tuple-element.874), channel_id=1, source_target_pairs={{8,0},{16,8},{24,16},{28,24},{20,28},{12,20},{4,12},{0,4},{9,1},{1... | collective-permute-start | bytes 1572872 | tf_op jit(solution)/shard_map/ppermute | solution.py:176
  758.7 34.5 %collective-permute-start.142 = (f32[512,2048]{1,0:T(8,128)}, f32[512,2048]{1,0:T(8,128)}, u32[]{:S(2)}, u32[]{:S(2)}) collective-permute-start(f32[512,2048]{1,0:T(8,128)} %get-tuple-element.951.mine_ref), channel_id=1, source_target_pairs={{0,1},{1,0},{2,3},{3,2},{4,5},{5,4},{6,7},{7,6},{8,9},{9,8},{10,11... | collective-permute-start | bytes 12582920 | tf_op jit(solution)/shard_map/ppermute | solution.py:145
  760.9 23.7 %collective-permute-start.140 = (bf16[256,1024]{1,0:T(8,128)(2,1)}, bf16[256,1024]{1,0:T(8,128)(2,1)S(1)}, u32[]{:S(2)}, u32[]{:S(2)}) collective-permute-start(bf16[256,1024]{1,0:T(8,128)(2,1)} %get-tuple-element.941), channel_id=1, source_target_pairs={{0,8},{8,16},{16,24},{24,28},{28,20},{20,12},{12,4},{4,0},{1,9},{9... | collective-permute-start | bytes 1572872 | tf_op jit(solution)/shard_map/ppermute | solution.py:176
  791.4 46.7 %collective-permute-start.149 = (bf16[512,2048]{1,0:T(8,128)(2,1)S(1)}, bf16[512,2048]{1,0:T(8,128)(2,1)}, u32[]{:S(2)}, u32[]{:S(2)}) collective-permute-start(bf16[512,2048]{1,0:T(8,128)(2,1)S(1)} %copy-done.4), channel_id=1, source_target_pairs={{0,2},{1,3},{2,0},{3,1},{4,6},{5,7},{6,4},{7,5},{8,10},{9,11},{10,... | collective-permute-start | bytes 6291464 | tf_op jit(solution)/shard_map/ppermute | solution.py:145
  (263 other events, 3455.8 us)

commit v2 on v1

--- a/solution.py
+++ b/solution.py
@@ -19,14 +19,27 @@
     return lax.dot_general(a, b, (dims, ((), ())), preferred_element_type=F32)
 
 
-def from_others(block, direction, send=lax.ppermute):
-    size = lax.axis_size("seq")
-    parts = []
-    for turn in range(1, max(1, size // 4) + 1):
-        distance = direction * turn
-        route = [(i - distance, i) for i in range(size) if 0 <= i - distance < size]
-        parts.append(send(block, "seq", route))
-    return parts
+class Others:
+    def __init__(self, block, direction, send=lax.ppermute):
+        self.size = lax.axis_size("seq")
+        self.block, self.direction, self.send = block, direction, send
+        turns = max(1, self.size // 4)
+        self.paired = turns == 2
+        steps = [2] if self.paired else range(1, turns + 1)
+        self.parts = [self.shift(direction * step) for step in steps]
+
+    def shift(self, distance):
+        route = [(i, i + distance) for i in range(self.size) if 0 <= i + distance < self.size]
+        return self.send(self.block, "seq", route)
+
+    def second(self):
+        if self.paired:
+            (far,) = self.parts
+            first = lax.rem(lax.axis_index("seq"), 2) == (0 if self.direction > 0 else 1)
+            near = jnp.where(first, self.block, far)
+            near = self.send(near, "seq", [(i, i ^ 1) for i in range(self.size)])
+            self.parts = [near, far]
+        return self.parts
 
 
 def ring_owner(place, size):
@@ -44,47 +57,64 @@
     return ahead, [(b, a) for a, b in ahead]
 
 
-def assemble(own, ahead_parts, back_parts):
-    size = lax.axis_size("seq")
-    rows, cols = own.shape
-    half = rows // 2
-    count = 2 * (size - 1) + 1
-
+class Weight:
+    def __init__(self, own, ahead=(), back=()):
+        self.size = lax.axis_size("seq") if ahead else 1
+        self.rows, self.cols = own.shape
+        self.arrays = [own, *ahead, *back]
+        self.count = len(self.arrays)
+        self.shape = (self.size * self.rows, self.cols)
+        self.ins = [(array, None, None) for array in self.arrays]
+        self.outs = [(None, None)]
+        self.shapes = [(self.shape, own.dtype)]
+        self.scratch = [
+            pltpu.VMEM(self.shape, own.dtype),
+            pltpu.SemaphoreType.DMA((self.count,)),
+            pltpu.SemaphoreType.DMA,
+        ]
+
+    def copies(self, parts, whole, sems):
+        if self.size == 1:
+            return [pltpu.make_async_copy(parts[0], whole, sems.at[0])]
+        me = lax.axis_index("seq")
+        place = ring_place(me, self.size)
+        half = self.rows // 2
+        at = [(me * self.rows, self.rows)]
+        at += [(ring_owner(place - k, self.size) * self.rows, half) for k in range(1, self.size)]
+        at += [
+            (ring_owner(place + k, self.size) * self.rows + half, half)
+            for k in range(1, self.size)
+        ]
+        return [
+            pltpu.make_async_copy(part, whole.at[pl.ds(first, rows)], sems.at[i])
+            for i, (part, (first, rows)) in enumerate(zip(parts, at))
+        ]
+
+    def load(self, parts, out, whole, sems, out_sem):
+        @pl.when(pl.program_id(0) == 0)
+        def _():
+            copies = self.copies(parts, whole, sems)
+            for copy in copies:
+                copy.start()
+            for copy in copies:
+                copy.wait()
+            pltpu.make_async_copy(whole, out, out_sem).start()
+
+    def end(self, out, whole, out_sem):
+        @pl.when(pl.program_id(0) == pl.num_programs(0) - 1)
+        def _():
+            pltpu.make_async_copy(whole, out, out_sem).wait()
+
+
+def assemble(weight):
     def kernel(*refs):
-        parts, out, sems = refs[:count], refs[count], refs[count + 1]
-        me = lax.axis_index("seq")
-        place = ring_place(me, size)
-        copies = [pltpu.make_async_copy(parts[0], out.at[pl.ds(me * rows, rows)], sems.at[0])]
-        for k in range(1, size):
-            a = ring_owner(place - k, size)
-            b = ring_owner(place + k, size)
-            copies.append(
-                pltpu.make_async_copy(parts[k], out.at[pl.ds(a * rows, half)], sems.at[k])
-            )
-            copies.append(
-                pltpu.make_async_copy(
-                    parts[size - 1 + k],
-                    out.at[pl.ds(b * rows + half, half)],
-                    sems.at[size - 1 + k],
-                )
-            )
-        for copy in copies:
-            copy.start()
-        for copy in copies:
-            copy.wait()
-
-    return pl.pallas_call(
-        kernel,
-        out_shape=jax.ShapeDtypeStruct((size * rows, cols), own.dtype),
-        in_specs=[pl.BlockSpec(memory_space=pl.ANY)] * count,
-        out_specs=pl.BlockSpec(memory_space=pltpu.VMEM),
-        scratch_shapes=[pltpu.SemaphoreType.DMA((count,))],
-        compiler_params=pltpu.CompilerParams(vmem_limit_bytes=60 * 2**20),
-        cost_estimate=pl.CostEstimate(
-            flops=4 * 10**9, bytes_accessed=0, transcendentals=0
-        ),
-        name="assemble",
-    )(own, *ahead_parts, *back_parts)
+        parts, (out, whole, sems, out_sem) = refs[: weight.count], refs[weight.count :]
+        weight.load(parts, out, whole, sems, out_sem)
+        weight.end(out, whole, out_sem)
+
+    return kernel_call(
+        kernel, "assemble", (1,), weight.ins, weight.outs, weight.shapes, 4, scratch=weight.scratch
+    )[0]
 
 
 def barrier(*values):
@@ -92,50 +122,45 @@
 
 
 class Gather:
-    def __init__(self, own, extra=None):
+    def __init__(self, own):
         self.size = lax.axis_size("seq")
         self.own = own
         half = own.shape[0] // 2
-        self.now = [own[:half], own[half:]] + ([] if extra is None else [extra])
-        self.parts = [[own[:half]], [own[half:]], [extra]]
+        self.now = [own[:half], own[half:]]
+        self.parts = [[], []]
         self.left = self.size - 1
 
     def tick(self, *values):
-        count = len(self.now)
-        done = barrier(*self.now, *values)
-        self.now, values = list(done[:count]), done[count:]
+        *self.now, first = barrier(*self.now, values[0])
         if self.left > 0:
-            ahead, back = ring_routes(self.size)
-            routes = [ahead, back, ahead]
             self.now = [
-                lax.ppermute(block, "seq", route) for block, route in zip(self.now, routes)
+                lax.ppermute(block, "seq", route)
+                for block, route in zip(self.now, ring_routes(self.size))
             ]
             for part, block in zip(self.parts, self.now):
                 part.append(block)
         self.left -= 1
-        return values
+        return (first, *values[1:])
 
     @property
     def ended(self):
         return self.left < 0
 
     def result(self):
-        return assemble(self.own, self.parts[0][1:], self.parts[1][1:])
-
-    def table(self):
-        place = ring_place(lax.axis_index("seq"), self.size)
-        stack = jnp.concatenate(self.parts[2], axis=0)
-        index = jnp.arange(self.size)
-        return stack[lax.rem(place - ring_place(index, self.size) + self.size, self.size)]
+        return Weight(self.own, *self.parts)
 
 
 class Line:
+    cost = 0
+
     def __init__(self, token):
         self.token = token
 
-    def run(self, function, *values):
+    def run(self, function, *values, cost=0):
         *values, self.token = barrier(*values, self.token)
+        Line.cost = cost
         out = function(*values)
+        Line.cost = 0
         first, *rest = out if isinstance(out, (tuple, list)) else (out,)
         first, self.token = barrier(first, self.token)
         return (first, *rest) if len(rest) else first
@@ -144,10 +169,13 @@
         block, self.token = barrier(block, self.token)
         return lax.ppermute(block, axis, route)
 
-    def tick(self, *rings):
+    def tick(self, *rings, cost=0):
         for ring in rings:
             if not ring.ended:
-                (self.token,) = ring.tick(self.token)
+                self.token = ring.go(ring.add(self.token, cost))
+
+    def fill(self, small, cost):
+        return self.run(passed, small, cost=cost)
 
     def meet(self, *values):
         *values, self.token = barrier(*values, self.token)
@@ -155,35 +183,38 @@
 
 
 class Reduce:
-    def __init__(self, ahead, back=None):
+    def __init__(self, ahead, back, part=(0, 0, 1)):
         self.size = lax.axis_size("seq")
-        self.halves = back is None
-        self.grads = (ahead, ahead if back is None else back)
+        self.part = part
+        self.grads = (ahead, back)
         self.place = ring_place(lax.axis_index("seq"), self.size)
         self.arrived = ()
         self.step = 0
 
-    def tick(self, *values):
+    def add(self, token, cost=0):
         self.step += 1
         if self.arrived:
-            *self.arrived, first = barrier(*self.arrived, values[0])
-            values = (first, *values[1:])
-        self.now = ring_add(self.grads, self.arrived, self.place, self.step, self.halves)
-        *self.now, first = barrier(*self.now, values[0])
+            *self.arrived, token = barrier(*self.arrived, token)
+        Line.cost = cost
+        self.now = ring_add(self.grads, self.arrived, self.place, self.step, *self.part)
+        Line.cost = 0
+        *self.now, token = barrier(*self.now, token)
+        return token
+
+    def go(self, token):
         if self.step < self.size:
-            routes = ring_routes(self.size)
+            *self.now, token = barrier(*self.now, token)
             self.arrived = [
-                lax.ppermute(block, "seq", route) for block, route in zip(self.now, routes)
+                lax.ppermute(block, "seq", route)
+                for block, route in zip(self.now, ring_routes(self.size))
             ]
-        return (first, *values[1:])
+        return token
 
     @property
     def ended(self):
         return self.step >= self.size
 
     def result(self):
-        if self.halves:
-            return jnp.concatenate(self.now, axis=0)
         return self.now
 
 
@@ -234,34 +265,44 @@
         return values[0] if len(values) == 1 else tuple(values)
 
 
-def gather(own, extra=None):
+def gather(own):
     if lax.axis_size("seq") > RING_MOST:
-        return Builtin(lax.all_gather(own, "seq", axis=0, tiled=True))
-    return Gather(own, extra)
-
-
-def reduce(ahead, back=None):
+        return Builtin(Weight(lax.all_gather(own, "seq", axis=0, tiled=True)))
+    return Gather(own)
+
+
+def doubled(rows, distance):
+    route = [(i, i ^ distance) for i in range(lax.axis_size("seq"))]
+    return jnp.concatenate([rows, lax.ppermute(rows, "seq", route)], axis=0)
+
+
+def reduce(ahead, back):
     if lax.axis_size("seq") > RING_MOST:
         total = [
             lax.psum_scatter(grad.astype(F32), "seq", scatter_dimension=0, tiled=True)
             for grad in (ahead, back)
-            if grad is not None
         ]
-        return Builtin(total[0] if back is None else total)
+        return Builtin(total)
     return Reduce(ahead, back)
 
 
-def small_reduce(table):
-    me = lax.axis_index("seq")
+def reduce_one(grad):
+    if lax.axis_size("seq") > RING_MOST:
+        return reduce(grad, grad[:, :0])
+    return Reduce(grad, grad, (0, 1, 2))
+
+
+def reduced_one(ring):
+    return jnp.concatenate(ring.result(), axis=1)
+
+
+def halved(line, table):
     distance = table.shape[0] // 2
-    while distance >= 1:
-        route = [(i, i ^ distance) for i in range(lax.axis_size("seq"))]
-        high = (me // distance) % 2
-        kept = lax.dynamic_slice_in_dim(table, high * distance, distance)
-        sent = lax.dynamic_slice_in_dim(table, (1 - high) * distance, distance)
-        table = kept + lax.ppermute(sent, "seq", route)
-        distance //= 2
-    return table[0]
+    route = [(i, i ^ distance) for i in range(lax.axis_size("seq"))]
+    high = (lax.axis_index("seq") // distance) % 2
+    kept = lax.dynamic_slice_in_dim(table, high * distance, distance)
+    sent = lax.dynamic_slice_in_dim(table, (1 - high) * distance, distance)
+    return kept, line.send(sent, "seq", route)
 
 
 def swap(block, bit):
@@ -321,23 +362,39 @@
     return scale * (d_normed - first - normed * second)
 
 
-def kernel_call(body, name, grid, ins, outs, shapes, weight, prefetch=(), vmem=60):
+def kernel_call(body, name, grid, ins, outs, shapes, weight, prefetch=(), vmem=24, scratch=(), stay=False):
     arrays = [a for a, _, _ in ins]
+    arrays = [
+        pltpu.with_memory_space_constraint(a, pltpu.HBM) if stay or block is None else a
+        for a, block, _ in ins
+    ]
     return pl.pallas_call(
         body,
         out_shape=[jax.ShapeDtypeStruct(s, t) for s, t in shapes],
         grid_spec=pltpu.PrefetchScalarGridSpec(
             num_scalar_prefetch=len(prefetch),
             grid=grid,
-            in_specs=[pl.BlockSpec(block, index) for _, block, index in ins],
-            out_specs=[pl.BlockSpec(block, index) for block, index in outs],
+            in_specs=[spec(block, index) for _, block, index in ins],
+            out_specs=[
+                pl.BlockSpec(memory_space=pl.ANY) if block is None else pl.BlockSpec(block, index)
+                for block, index in outs
+            ],
+            scratch_shapes=list(scratch),
         ),
         compiler_params=pltpu.CompilerParams(vmem_limit_bytes=vmem * 2**20),
         cost_estimate=pl.CostEstimate(
-            flops=weight * 10**9, bytes_accessed=0, transcendentals=0
+            flops=weight * 10**9 // 2 + Line.cost * 10**9, bytes_accessed=0, transcendentals=0
         ),
         name=name,
     )(*prefetch, *arrays)
+
+
+def spec(block, index):
+    if block is None:
+        return pl.BlockSpec(memory_space=pl.ANY)
+    if index in (fixed, fixed3):
+        return pl.BlockSpec(block, index, pipeline_mode=pl.Buffered(1))
+    return pl.BlockSpec(block, index)
 
 
 def row_tile(i, *_):
@@ -379,16 +436,22 @@
     )[0]
 
 
-def project_turn(n1, qk_mat, cosine, sine, tile=256):
+def project_turn(n1, weight, cosine, sine, tile=256):
     rows, width = n1.shape
-    cols = qk_mat.shape[1] // 2
-
-    def kernel(n1_ref, mat_ref, cos_ref, sin_ref, q_ref, k_ref):
+    cols = weight.cols // 2
+
+    def kernel(n1_ref, cos_ref, sin_ref, *refs):
+        parts, (q_ref, k_ref, out, mat_ref, sems, out_sem) = (
+            refs[: weight.count],
+            refs[weight.count :],
+        )
+        weight.load(parts, out, mat_ref, sems, out_sem)
         raw = jnp.dot(n1_ref[...], mat_ref[...], preferred_element_type=F32)
         cos, sin = cos_ref[...], sin_ref[...]
         for at in range(0, cols, KD):
             q_ref[:, at : at + KD] = turn(raw[:, at : at + KD], cos, sin).astype(BF)
             k_ref[:, at : at + KD] = turn(raw[:, cols + at : cols + at + KD], cos, sin).astype(BF)
+        weight.end(out, mat_ref, out_sem)
 
     return kernel_call(
         kernel,
@@ -396,13 +459,35 @@
         (rows // tile,),
         [
             (n1, (tile, width), row_tile),
-            (qk_mat, (width, 2 * cols), fixed),
             (cosine, (tile, KD // 2), row_tile),
             (sine, (tile, KD // 2), row_tile),
+            *weight.ins,
         ],
-        [((tile, cols), row_tile)] * 2,
-        [((rows, cols), BF)] * 2,
+        [((tile, cols), row_tile)] * 2 + weight.outs,
+        [((rows, cols), BF)] * 2 + weight.shapes,
         9,
+        scratch=weight.scratch,
+    )
+
+
+def project(n1, weight, tile=256):
+    rows, width = n1.shape
+
+    def kernel(n1_ref, *refs):
+        parts, (v_ref, out, mat_ref, sems, out_sem) = refs[: weight.count], refs[weight.count :]
+        weight.load(parts, out, mat_ref, sems, out_sem)
+        v_ref[...] = jnp.dot(n1_ref[...], mat_ref[...], preferred_element_type=F32).astype(BF)
+        weight.end(out, mat_ref, out_sem)
+
+    return kernel_call(
+        kernel,
+        "value",
+        (rows // tile,),
+        [(n1, (tile, width), row_tile), *weight.ins],
+        [((tile, weight.cols), row_tile)] + weight.outs,
+        [((rows, weight.cols), BF)] + weight.shapes,
+        9,
+        scratch=weight.scratch,
     )
 
 
@@ -467,15 +552,19 @@
     )
 
 
-def gate_forward(n1, gate_mat, q, entry, state, local_out, scale, shift, tile=256):
+def gate_forward(n1, weight, q, entry, state, local_out, scale, shift, tile=256):
     rows, width = n1.shape
-    cols = gate_mat.shape[1]
+    cols = weight.cols
     heads = cols // VD
 
     def kernel(
-        n1_ref, mat_ref, q_ref, entry_ref, state_ref, local_ref, scale_ref, shift_ref,
-        y_ref, gate_ref, hat_ref, dev_ref,
+        n1_ref, q_ref, entry_ref, state_ref, local_ref, scale_ref, shift_ref, *refs
     ):
+        parts, (y_ref, gate_ref, hat_ref, dev_ref, out, mat_ref, sems, out_sem) = (
+            refs[: weight.count],
+            refs[weight.count :],
+        )
+        weight.load(parts, out, mat_ref, sems, out_sem)
         gate = jnp.dot(n1_ref[...], mat_ref[...], preferred_element_type=F32)
         gate_ref[...] = gate
         swish = gate * jax.nn.sigmoid(gate)
@@ -490,6 +579,7 @@
             affine = hat * scale_ref[:, at] + shift_ref[:, at]
             y_ref[:, at] = (affine * swish[:, at]).astype(BF)
         dev_ref[...] = jnp.concatenate(devs, axis=1)
+        weight.end(out, mat_ref, out_sem)
 
     return kernel_call(
         kernel,
@@ -497,33 +587,43 @@
         (rows // tile,),
         [
             (n1, (tile, width), row_tile),
-            (gate_mat, (width, cols), fixed),
             (q, (tile, heads * KD), row_tile),
             (entry, (tile, heads), row_tile),
             (state, state.shape, fixed3),
             (local_out, (tile, cols), row_tile),
             (scale[None, :], (1, cols), fixed),
             (shift[None, :], (1, cols), fixed),
+            *weight.ins,
         ],
-        [((tile, cols), row_tile)] * 3 + [((tile, heads), row_tile)],
-        [((rows, cols), BF), ((rows, cols), F32), ((rows, cols), F32), ((rows, heads), F32)],
+        [((tile, cols), row_tile)] * 3 + [((tile, heads), row_tile)] + weight.outs,
+        [((rows, cols), BF), ((rows, cols), F32), ((rows, cols), F32), ((rows, heads), F32)]
+        + weight.shapes,
         12,
-    )
-
-
-def gate_backward(d_branch, out_mat, gate, hat, dev, scale, shift, tile=256):
-    rows, width = d_branch.shape
+        scratch=weight.scratch,
+        vmem=32,
+    )
+
+
+def gate_backward(
+    db_mine, db_other, side, out_mat, gate, hat, dev, scale, shift, q, entry, tile=256
+):
+    half, width = db_mine.shape
+    rows = 2 * half
     cols = out_mat.shape[1]
     heads = cols // VD
+    mine_block, other_block, pick = half_tiles(side, half // tile, tile, width)
 
     def kernel(
-        db_ref, mat_ref, gate_ref, hat_ref, dev_ref, scale_ref, shift_ref,
-        dg_ref, dr_ref, gain_ref, bias_ref,
+        side_ref, mine_ref, other_ref, mat_ref, gate_ref, hat_ref, dev_ref, scale_ref, shift_ref,
+        q_ref, entry_ref, db_ref, dg_ref, dr_ref, gain_ref, bias_ref, state_ref, total_ref,
     ):
+        pick(side_ref, mine_ref, other_ref, db_ref)
+
         @pl.when(pl.program_id(0) == 0)
         def _():
             gain_ref[...] = jnp.zeros_like(gain_ref)
             bias_ref[...] = jnp.zeros_like(bias_ref)
+            total_ref[...] = jnp.zeros_like(total_ref)
 
         d_y = jnp.dot(db_ref[...], mat_ref[...], preferred_element_type=F32)
         for h in range(heads):
@@ -536,35 +636,92 @@
             gain_ref[:, at] += jnp.sum(d_affine * r_hat, axis=0, keepdims=True)
             bias_ref[:, at] += jnp.sum(d_affine, axis=0, keepdims=True)
             d_hat = d_affine * scale_ref[:, at]
-            dr_ref[:, at] = standardize_back(d_hat, r_hat, dev_ref[:, h : h + 1]).astype(BF)
+            d_r = standardize_back(d_hat, r_hat, dev_ref[:, h : h + 1]).astype(BF)
+            dr_ref[:, at] = d_r
+            qd = (q_ref[:, h * KD : (h + 1) * KD].astype(F32) * entry_ref[:, h : h + 1]).astype(BF)
+            total_ref[h] += lax.dot_general(
+                qd, d_r, (((0,), (0,)), ((), ())), preferred_element_type=F32
+            )
+
+        @pl.when(pl.program_id(0) == pl.num_programs(0) - 1)
+        def _():
+            state_ref[...] = total_ref[...].astype(BF)
 
     return kernel_call(
         kernel,
         "gate_backward",
         (rows // tile,),
         [
-            (d_branch, (tile, width), row_tile),
+            (db_mine, *mine_block),
+            (db_other, *other_block),
             (out_mat, (width, cols), fixed),
             (gate, (tile, cols), row_tile),
             (hat, (tile, cols), row_tile),
             (dev, (tile, heads), row_tile),
             (scale[None, :], (1, cols), fixed),
             (shift[None, :], (1, cols), fixed),
+            (q, (tile, heads * KD), row_tile),
+            (entry, (tile, heads), row_tile),
         ],
-        [((tile, cols), row_tile)] * 2 + [((1, cols), fixed)] * 2,
-        [((rows, cols), BF), ((rows, cols), BF), ((1, cols), F32), ((1, cols), F32)],
+        [((tile, width), row_tile)] + [((tile, cols), row_tile)] * 2 + [((1, cols), fixed)] * 2
+        + [((heads, KD, VD), fixed3)],
+        [
+            ((rows, width), BF),
+            ((rows, cols), BF),
+            ((rows, cols), BF),
+            ((1, cols), F32),
+            ((1, cols), F32),
+            ((heads, KD, VD), BF),
+        ],
         0,
-    )
-
-
-def feed_forward(n2, up_mat, up_shift, cotangent, down_mat, tile=256):
-    rows, width = n2.shape
-    cols = up_mat.shape[1]
-
-    def kernel(n2_ref, up_ref, shift_ref, cot_ref, down_ref, act_ref, dup_ref, sum_ref):
+        prefetch=(side[None],),
+        scratch=[pltpu.VMEM((heads, KD, VD), F32)],
+        stay=True,
+    )
+
+
+def half_tiles(side, steps, tile, width):
+    def within(which):
+        def index(i, side_ref):
+            return (jnp.clip(i - (side_ref[0] ^ which) * steps, 0, steps - 1), 0)
+
+        return index
+
+    def pick(side_ref, mine_ref, other_ref, out_ref):
+        own = pl.program_id(0) // steps == side_ref[0]
+
+        @pl.when(own)
+        def _():
+            out_ref[...] = mine_ref[...].astype(out_ref.dtype)
+
+        @pl.when(jnp.logical_not(own))
+        def _():
+            out_ref[...] = other_ref[...].astype(out_ref.dtype)
+
+    return ((tile, width), within(0)), ((tile, width), within(1)), pick
+
+
+def feed_forward(n2_mine, n2_other, side, up, up_shift, cotangent, down, tile=256):
+    half, width = n2_mine.shape
+    rows = 2 * half
+    cols = up.cols
+    mine_block, other_block, pick = half_tiles(side, half // tile, tile, width)
+
+    def kernel(
+        side_ref, mine_ref, other_ref, shift_ref, cot_ref, *refs
+    ):
+        up_parts, refs = refs[: up.count], refs[up.count :]
+        down_parts, refs = refs[: down.count], refs[down.count :]
+        n2_ref, act_ref, dup_ref, sum_ref, up_out, down_out, *refs = refs
+        up_ref, up_sems, up_sem, down_ref, down_sems, down_sem = refs
+        up.load(up_parts, up_out, up_ref, up_sems, up_sem)
+        down.load(down_parts, down_out, down_ref, down_sems, down_sem)
+
         @pl.when(pl.program_id(0) == 0)
         def _():
             sum_ref[...] = jnp.zeros_like(sum_ref)
+
+        pick(side_ref, mine_ref, other_ref, n2_ref)
 
         for at in range(0, cols, 256):
             part = slice(at, at + 256)
@@ -577,21 +734,33 @@
             d_up = (slope * d_act).astype(BF)
             dup_ref[:, part] = d_up
             sum_ref[:, part] += jnp.sum(d_up.astype(F32), axis=0, keepdims=True)
+        up.end(up_out, up_ref, up_sem)
+        down.end(down_out, down_ref, down_sem)
 
     return kernel_call(
         kernel,
         "feed_forward",
         (rows // tile,),
         [
-            (n2, (tile, width), row_tile),
-            (up_mat, (width, cols), fixed),
+            (n2_mine, *mine_block),
+            (n2_other, *other_block),
             (up_shift[None, :], (1, cols), fixed),
             (cotangent, (tile, width), row_tile),
-            (down_mat, (width, cols), fixed),
+            *up.ins,
+            *down.ins,
         ],
-        [((tile, cols), row_tile)] * 2 + [((1, cols), fixed)],
-        [((rows, cols), BF), ((rows, cols), BF), ((1, cols), F32)],
+        [((tile, width), row_tile)]
+        + [((tile, cols), row_tile)] * 2
+        + [((1, cols), fixed)]
+        + up.outs
+        + down.outs,
+        [((rows, width), BF), ((rows, cols), BF), ((rows, cols), BF), ((1, cols), F32)]
+        + up.shapes
+        + down.shapes,
         16,
+        scratch=up.scratch + down.scratch,
+        vmem=32,
+        prefetch=(side[None],),
     )
 
 
@@ -655,6 +824,7 @@
         [((rows, heads * KD), BF), ((rows, heads * KD), F32), ((rows, heads * VD), F32)],
         0,
         prefetch=(log_decay,),
+        stay=True,
     )
 
 
@@ -693,6 +863,7 @@
         [((tile, heads * KD), row_tile), ((tile, heads * VD), row_tile)],
         [((rows, heads * KD), BF), ((rows, heads * VD), BF)],
         0,
+        stay=True,
     )
 
 
@@ -763,11 +934,12 @@
         [((half, width), F32), ((half, width), BF), ((1, width), F32), ((1, width), F32)],
         0,
         prefetch=(side[None],),
+        stay=True,
     )
 
 
 def partial_rows(values, mats, which, added=(), pieces=1, tile=512):
-    rows, width = values[0].shape[0], mats[0].shape[0]
+    rows, width = values[0].shape[0], mats[0][0].shape[0]
     half, count = rows // 2, len(values)
 
     def kernel(which_ref, *refs):
@@ -786,7 +958,9 @@
         return (0, i)
 
     ins = [(v, (half, v.shape[1]), lambda i, which_ref: (which_ref[0], 0)) for v in values]
-    ins += [(m, (tile, m.shape[1]), row_tile) for m in mats]
+    ins += [
+        (m, (tile, v.shape[1]), lambda i, *_, at=at: (i, at)) for v, (m, at) in zip(values, mats)
+    ]
     ins += [(part, (part.shape[0], tile), column_tile) for part in added]
     return kernel_call(
         kernel,
@@ -797,6 +971,7 @@
         [((half // pieces, width), BF)] * pieces,
         0,
         prefetch=(which[None],),
+        stay=True,
     )
 
 
@@ -820,51 +995,67 @@
         [((tile, width), row_tile)],
         [((half, width), BF)],
         0,
+        stay=True,
     )[0]
 
 
-def both_halves(mine, others, side, tile=256):
+def passed(small):
+    def kernel(in_ref, out_ref):
+        out_ref[...] = in_ref[...]
+
+    return kernel_call(
+        kernel,
+        "passed",
+        (1,),
+        [(small, small.shape, fixed)],
+        [(small.shape, fixed)],
+        [(small.shape, small.dtype)],
+        0,
+    )[0]
+
+
+def both_halves(mine, other, side, kind, tile=256):
     half, width = mine.shape
-    tile = min(tile, half // len(others))
-    steps = half // tile
-    each = steps // len(others)
-
-    def kernel(side_ref, mine_ref, *refs):
-        out_ref = refs[-1]
-        at = pl.program_id(0)
-
-        @pl.when(at // steps == side_ref[0])
-        def _():
-            out_ref[...] = mine_ref[...]
-
-        for piece, ref in enumerate(refs[:-1]):
-
-            @pl.when((at // steps != side_ref[0]) & (at % steps // each == piece))
-            def _(ref=ref):
-                out_ref[...] = ref[...]
-
-    def within(which, first, count):
-        def index(i, side_ref):
-            return (jnp.clip(i - (side_ref[0] ^ which) * steps - first, 0, count - 1), 0)
-
-        return index
-
-    return kernel_call(
-        kernel,
+    mine_block, other_block, pick = half_tiles(side, half // tile, tile, width)
+    return kernel_call(
+        pick,
         "both_halves",
-        (2 * steps,),
-        [(mine, (tile, width), within(0, 0, steps))]
-        + [(ref, (tile, width), within(1, p * each, each)) for p, ref in enumerate(others)],
+        (2 * half // tile,),
+        [(mine, *mine_block), (other, *other_block)],
         [((tile, width), row_tile)],
-        [((2 * half, width), mine.dtype)],
+        [((2 * half, width), kind)],
         0,
         prefetch=(side[None],),
+        stay=True,
     )[0]
 
 
-def ring_add(grads, arrived, place, step, halves):
+def gradient(x, *dys, tile=256):
+    rows, width = x.shape
+    cols = [dy.shape[1] for dy in dys]
+
+    def kernel(x_ref, *refs):
+        at = 0
+        for dy_ref in refs[:-1]:
+            refs[-1][:, at : at + dy_ref.shape[1]] = lax.dot_general(
+                x_ref[...], dy_ref[...], (((0,), (0,)), ((), ())), preferred_element_type=F32
+            ).astype(BF)
+            at += dy_ref.shape[1]
+
+    return kernel_call(
+        kernel,
+        "gradient",
+        (width // tile,),
+        [(x, (rows, tile), lambda i, *_: (0, i))] + [(dy, dy.shape, fixed) for dy in dys],
+        [((tile, sum(cols)), row_tile)],
+        [((width, sum(cols)), BF)],
+        0,
+    )[0]
+
+
+def ring_add(grads, arrived, place, step, left, right, parts):
     size = lax.axis_size("seq")
-    rows = grads[0].shape[0] // size // (2 if halves else 1)
+    rows = grads[0].shape[0] // size
     kind = BF if step < size else F32
 
     def kernel(place_ref, *refs):
@@ -874,15 +1065,14 @@
                 total = total + refs[2 + i][...].astype(F32)
             refs[i - 2][...] = total.astype(kind)
 
-    def own(sign, low):
+    def own(sign, part):
         def index(i, place_ref):
-            owner = ring_owner(place_ref[0] + sign * step, size)
-            return (2 * owner + low if halves else owner, 0)
+            return (ring_owner(place_ref[0] + sign * step, size), part)
 
         return index
 
-    blocks = [(rows, grad.shape[1]) for grad in grads]
-    ins = [(grads[0], blocks[0], own(-1, 0)), (grads[1], blocks[1], own(1, 1))]
+    blocks = [(rows, grad.shape[1] // parts) for grad in grads]
+    ins = [(grads[0], blocks[0], own(-1, left)), (grads[1], blocks[1], own(1, right))]
     ins += [(block, block.shape, fixed) for block in arrived]
     return kernel_call(
         kernel,
@@ -942,7 +1132,7 @@
         ]
     ).astype(BF)[None, :]
     clock = Clock(2)
-    qk_ring = gather(qk_own, own_vector)
+    qk_ring = gather(qk_own)
     v_ring = gather(v_own)
     x = inputs
     (x,) = clock.add(0, qk_ring, x)
@@ -964,16 +1154,13 @@
         first_row, rows, lengths, offsets, log_decay
     )
     entry_cols, exit_cols = entry_weight.T, exit_weight.T
-    x = clock.tick(x, count=3)
-    x, cosine, sine, number, entry_cols, exit_cols = clock.tick(
-        x, cosine, sine, number, entry_cols, exit_cols
-    )
-    x = clock.until(v_ring, x)
-
-    if isinstance(qk_ring, Builtin):
-        table = lax.all_gather(own_vector, "seq", axis=0, tiled=True).astype(F32)
-    else:
-        table = qk_ring.table().astype(F32)
+    table = own_vector
+    distance = 1
+    while distance < size:
+        table = doubled(table, distance)
+        x, table = clock.tick(x, table, count=2)
+        distance *= 2
+    table = table[jnp.arange(size) ^ lax.axis_index("seq")].astype(F32)
 
     def wide(i):
         return table[:, i * shard : (i + 1) * shard].reshape(-1)
@@ -986,18 +1173,21 @@
     group_scale, group_shift, up_shift = [narrow(i) for i in range(3)]
 
     n1 = norm_rows(x, gain_one, bias_one)
+    grad_down_bias = jnp.sum(cotangent.astype(F32), axis=0)
+    n1, grad_down_bias = barrier(n1, grad_down_bias)
+    n1, cosine, sine, number, entry_cols, exit_cols = clock.tick(
+        n1, cosine, sine, number, entry_cols, exit_cols
+    )
+    n1 = clock.until(v_ring, n1)
+
     n1 = clock.tick(n1)
-    qk_mat = qk_ring.result()
-    n1, qk_mat = clock.tick(n1, qk_mat)
-    q, k = project_turn(n1, qk_mat, cosine, sine)
+    q, k, qk_mat = project_turn(n1, qk_ring.result(), cosine, sine)
     q, k, n1 = clock.tick(q, k, n1, count=2)
-    v_mat = v_ring.result()
-    n1, v_mat = clock.tick(n1, v_mat)
-    v = dot(n1, v_mat, ((1,), (0,))).astype(BF)
-    q, k, v = clock.tick(q, k, v)
+    v, v_mat = project(n1, v_ring.result())
+    v, q, k = clock.tick(v, q, k, count=2)
     local_out, local_state = retain(q, k, v, number, exit_cols, log_decay)
     local_out, local_state = clock.tick(local_out, local_state)
-    state_parts = from_others(local_state.astype(BF), 1)
+    state_parts = Others(local_state.astype(BF), 1).second()
     local_out = clock.until(o_ring, local_out)
 
     def gathered_state(first, rest, direction):
@@ -1011,13 +1201,12 @@
 
     state = gathered_state(state_parts[0], state_parts[1:], 1)
     state, local_out = barrier(state, local_out)
-    g_mat = g_ring.result()
-    g_mat, state = clock.tick(g_mat, state)
-    y, gate, r_hat, r_dev = gate_forward(
-        n1, g_mat, q, entry_cols, state, local_out, group_scale, group_shift
+    state = clock.tick(state)
+    y, gate, r_hat, r_dev, g_mat = gate_forward(
+        n1, g_ring.result(), q, entry_cols, state, local_out, group_scale, group_shift
     )
     y = clock.tick(y, count=2)
-    o_mat = o_ring.result()
+    o_mat = assemble(o_ring.result())
     y, o_mat = clock.tick(y, o_mat)
 
     def pick(values, which):
@@ -1035,12 +1224,12 @@
     kept = clock.tick(kept, count=7)
     kept, other = barrier(kept, other)
     mid, n2_mine = second_norm(inputs, side, kept, other, gain_two, bias_two)
-    n2_mine = clock.tick(n2_mine)
-    n2 = both_halves(n2_mine, [swap(n2_mine, 1)], side)
-    n2 = clock.until(w_ring, n2)
-    u_mat = u_ring.result()
-    w_mat = w_ring.result()
-    act, d_up, grad_up_bias = feed_forward(n2, u_mat, up_shift, cotangent, w_mat)
+    n2_other = swap(n2_mine, 1)
+    n2_mine, n2_other = barrier(n2_mine, n2_other)
+    n2_mine, n2_other = clock.until(w_ring, n2_mine, n2_other)
+    n2, act, d_up, grad_up_bias, u_mat, w_mat = feed_forward(
+        n2_mine, n2_other, side, u_ring.result(), up_shift, cotangent, w_ring.result()
+    )
 
     line = Line(grad_up_bias)
     pairs_two = [(i, i ^ 2) for i in range(lax.axis_size("tp"))]
@@ -1052,99 +1241,111 @@
             line.send(block[i * count : (i + 1) * count], "tp", pairs_one) for i in range(pieces)
         ]
 
-    def partial_sent(values, mats, pieces=2):
-        parts = line.run(lambda *v: partial_rows(v, mats, 1 - side, pieces=pieces), *values)
+    def partial_sent(values, mats, pieces=2, cost=0):
+        parts = line.run(
+            lambda *v: partial_rows(v, mats, 1 - side, pieces=pieces), *values, cost=cost
+        )
         parts = parts if isinstance(parts, tuple) else (parts,)
         return [line.send(part, "tp", pairs_one) for part in parts]
 
-    def partial_kept(values, mats, sent):
-        return line.run(lambda *v: partial_rows(v, mats, side, sent), *values)
-
-    def gradient(x, dy):
-        return dot(x, dy, ((0,), (0,)))
-
-    grad_w = line.run(gradient, cotangent, act)
-    sent_two = partial_sent((d_up,), (u_mat,), 1)
-    grad_u = line.run(gradient, n2, d_up)
-    kept_two = partial_kept((d_up,), (u_mat,), sent_two)
+    def partial_kept(values, mats, sent, cost=0):
+        return line.run(lambda *v: partial_rows(v, mats, side, sent), *values, cost=cost)
+
+    sent_two = partial_sent((d_up,), ((u_mat, 0),), 1)
+    grad_w = line.run(gradient, cotangent, act, cost=23)
+    kept_two = partial_kept((d_up,), ((u_mat, 0),), sent_two)
     other_two = line.send(kept_two, "tp", pairs_two)
+    grad_u = line.run(gradient, n2, d_up, cost=23)
     wu_back = reduce(grad_w, grad_u)
-    line.tick(wu_back)
-    sent_out = partial_sent((act,), (w_mat,), 1)
-    kept_out = partial_kept((act,), (w_mat,), sent_out)
-    line.tick(wu_back)
-    line.tick(wu_back)
+    line.tick(wu_back, wu_back, wu_back)
     d_mid, d_branch_mine, grad_second_gain, grad_second_bias = line.run(
         lambda kept, other: norm_backward(
             mid, False, kept, other, cotangent, True, gain_two, side
         ),
         kept_two,
         other_two,
-    )
-    d_branch_other = to_partner(d_branch_mine, 1)
-    line.tick(wu_back)
-    d_branch = line.run(lambda mine: both_halves(mine, d_branch_other, side), d_branch_mine)
-
-    d_gate, d_r, grad_group_gain, grad_group_bias = line.run(
-        lambda d: gate_backward(d, o_mat, gate, r_hat, r_dev, group_scale, group_shift), d_branch
-    )
-    line.tick(wu_back)
-
-    def state_part(d_r):
-        qd = (q.reshape(rows, heads, KD) * entry_cols[:, :, None]).astype(BF)
-        return jnp.einsum(
-            "scr,scq->crq", qd, d_r.reshape(rows, heads, VD), preferred_element_type=F32
-        ).astype(BF)
-
-    own_grad = line.run(state_part, d_r)
-    leaving_parts = from_others(own_grad, -1, line.send)
-    grad_o = line.run(gradient, d_branch, y)
-    grad_g = line.run(gradient, n1, d_gate)
-    line.tick(wu_back)
-    og_back = reduce(grad_o, grad_g)
-    line.tick(og_back)
+        cost=6,
+    )
+    d_branch_other = to_partner(d_branch_mine, 1)[0]
+    line.tick(wu_back, cost=23)
+
+    d_branch, d_gate, d_r, grad_group_gain, grad_group_bias, own_grad = line.run(
+        lambda mine, other: gate_backward(
+            mine,
+            other,
+            side,
+            o_mat,
+            gate,
+            r_hat,
+            r_dev,
+            group_scale,
+            group_shift,
+            q,
+            entry_cols,
+        ),
+        d_branch_mine,
+        d_branch_other,
+        cost=6,
+    )
+    others = Others(own_grad, -1, line.send)
     d_q, d_k, d_v = line.run(
         lambda d_r: retain_backward(
             q, k, v, d_r, state, number, entry_cols, log_decay, cosine, sine
         ),
         d_r,
-    )
-    line.tick(wu_back, og_back)
+        cost=6,
+    )
+    leaving_parts = others.second()
+    line.tick(wu_back)
+    grad_o = line.run(gradient, d_branch, y, cost=6)
+    grad_g = line.run(gradient, n1, d_gate)
+    line.tick(wu_back)
+    og_back = reduce(grad_o, grad_g)
+    line.tick(og_back)
     leaving = line.run(lambda first, *rest: gathered_state(first, rest, -1), *leaving_parts)
     d_k, d_v = line.run(
         lambda d_k, d_v: state_backward(k, v, exit_cols, leaving, d_k, d_v, cosine, sine),
         d_k,
         d_v,
-    )
+        cost=6,
+    )
+    grad_v = line.run(gradient, n1, d_v)
+    line.tick(wu_back, og_back)
+    grad_qk = line.run(gradient, n1, d_q, d_k, cost=6)
     line.tick(wu_back)
-    grad_v = line.run(gradient, n1, d_v)
-    grad_qk = line.run(gradient, n1, jnp.concatenate([d_q, d_k], axis=1))
-    line.tick(og_back)
     vqk_back = reduce(grad_v, grad_qk)
     line.tick(vqk_back)
     d_all = (d_gate, d_v, d_q, d_k)
-    mats_all = (g_mat, v_mat, qk_mat[:, : heads * KD], qk_mat[:, heads * KD :])
-    sent_one = partial_sent(d_all, mats_all, 1)
+    mats_all = ((g_mat, 0), (v_mat, 0), (qk_mat, 0), (qk_mat, 1))
+    sent_one = partial_sent(d_all, mats_all, 1, cost=6)
+    grad_second_gain = line.fill(grad_second_gain, 23)
     line.tick(og_back, vqk_back)
-    kept_one = partial_kept(d_all, mats_all, sent_one)
+    kept_one = partial_kept(d_all, mats_all, sent_one, cost=6)
     other_one = line.send(kept_one, "tp", pairs_two)
-    line.tick(og_back, vqk_back, og_back, vqk_back, og_back)
-    grad_mine, _, grad_first_gain, grad_first_bias = line.run(
+    grad_second_gain = line.fill(grad_second_gain, 23)
+    line.tick(og_back, vqk_back)
+    line.tick(og_back, vqk_back)
+    _, grad_mine, grad_first_gain, grad_first_bias = line.run(
         lambda kept, other: norm_backward(
             inputs, True, kept, other, d_mid, False, gain_one, side
         ),
         kept_one,
         other_one,
-    )
+        cost=6,
+    )
+    grad_other = to_partner(grad_mine, 1)[0]
+    sent_out = partial_sent((act,), ((w_mat, 0),), 1, cost=23)
+    line.tick(og_back, vqk_back, cost=12)
+    grad_inputs = line.run(
+        lambda mine, other: both_halves(mine, other, side, F32), grad_mine, grad_other
+    )
+    kept_out = partial_kept((act,), ((w_mat, 0),), sent_out)
     other_out = line.send(kept_out, "tp", pairs_two)
-    grad_other = to_partner(grad_mine, 1)
-    line.tick(vqk_back, og_back)
-    grad_inputs = line.run(lambda mine: both_halves(mine, grad_other, side), grad_mine)
-    line.tick(vqk_back, og_back)
+    grad_second_gain = line.fill(grad_second_gain, 23)
+    line.tick(og_back, vqk_back)
 
     grad_up_bias = line.token
-    grad_down_bias = jnp.sum(cotangent.astype(F32), axis=0)
-    vectors = jnp.concatenate(
+    table = jnp.concatenate(
         [
             vector.reshape(size, -1)
             for vector in (
@@ -1160,20 +1361,27 @@
         ],
         axis=1,
     )
-    small = small_reduce(vectors)
+    line.token = grad_inputs
+    table, sent = halved(line, table)
+    line.tick(vqk_back, og_back)
+    while table.shape[0] > 1:
+        table = line.run(lambda kept, sent: kept + sent, table, sent)
+        table, sent = halved(line, table)
+        line.tick(vqk_back, og_back)
+    small = line.run(lambda kept, sent: kept + sent, table, sent)[0]
     halves = small[: 4 * shard]
-    halves = halves + swap(halves, 1)
-    line.token = halves
-    line.tick(vqk_back, og_back)
+    sent = line.send(halves, "tp", pairs_one)
     output_mine = line.run(
-        lambda kept: finish_output(mid, kept, other_out, down_shift), kept_out
-    )
-    output_other = to_partner(output_mine, 1)
-    line.tick(vqk_back)
-    output = line.run(lambda mine: both_halves(mine, output_other, side), output_mine)
+        lambda kept, other: finish_output(mid, kept, other, down_shift), kept_out, other_out
+    )
+    output_other = to_partner(output_mine, 1)[0]
     while not (og_back.ended and vqk_back.ended):
-        line.tick(og_back, vqk_back)
-    halves = line.token
+        line.tick(vqk_back, og_back)
+    output = line.run(
+        lambda mine, other: both_halves(mine, other, side, BF), output_mine, output_other
+    )
+    halves = halves + sent
+    grad_inputs = line.token
     own = [halves[i * shard : (i + 1) * shard] for i in range(4)]
     own_down_bias = small[4 * shard : 5 * shard]
     own_units = [small[5 * shard + i * unit : 5 * shard + (i + 1) * unit] for i in range(3)]

time: 879 us -> 735 us (0.84)
  matrix products: 74.2 us -> 8.91 us
  Pallas kernels: 279 us -> 231 us
  waiting for transfers between devices: 250 us -> 210 us
  local copies, waits for them, and re-layouts: 48.2 us -> 85.5 us
  starting transfers between devices: 185 us -> 160 us
    ppermute x133 -> x84, waiting for transfers between devices: 215 us -> 101 us  [tick(): lax.ppermute(block, 'seq', route)]
    ppermute x133 -> x84, starting transfers between devices: 167 us -> 87.7 us  [tick(): lax.ppermute(block, 'seq', route)]
    ppermute x5 -> x47, waiting for transfers between devices: 12.4 us -> 76 us  [the longest x42 76 us: go(): lax.ppermute(block, 'seq', route)]
    dot_general x9 -> x2, matrix products: 71 us -> 8.91 us  [dot(): return lax.dot_general(a, b, (dims, ((), ())), preferred_element_type=F32)]
    ppermute x5 -> x47, starting transfers between devices: 10.5 us -> 60.8 us  [the longest x42 46.7 us: go(): lax.ppermute(block, 'seq', route)]
    unnamed x290 -> x316, local copies, waits for them, and re-layouts: 33.5 us -> 78.8 us
    pallas_call x6 -> x0, Pallas kernels: 25.9 us -> none  [assemble(): pl.pallas_call(kernel, out_shape=jax.ShapeDtypeStruct((size * rows, cols)...]
    pallas_call x46 -> x55, Pallas kernels: 253 us -> 231 us  [kernel_call(): pl.pallas_call(body, out_shape=[jax.ShapeDtypeStruct(s, t) for s, t in sh...]
  transfers between devices with their start and end apart: 153 -> 149, of which waited for: 70 -> 75; matrix products, arithmetic and copies ran while one was open for 11% -> 6% of each run, Pallas kernels for 20% -> 26%
where the time goes in v2:
time: 735 us; the launch traced here: 725 us
  Pallas kernels  231 us (31%)
  waiting for transfers between devices  210 us (29%)
  starting transfers between devices  160 us (22%)
  local copies, waits for them, and re-layouts  85.5 us (12%)
  other arithmetic  23.6 us (3%)
  matrix products  8.91 us (1%)
    pallas_call x55, Pallas kernels, kernel_call(): pl.pallas_call(body, out_shape=[jax.ShapeDtypeStruct(s, t) for s, t in sh...  231 us
    ppermute x84, waiting for transfers between devices, tick(): lax.ppermute(block, 'seq', route)  101 us
    ppermute x84, starting transfers between devices, tick(): lax.ppermute(block, 'seq', route)  87.7 us
    unnamed x316, local copies, waits for them, and re-layouts  78.8 us
    ppermute x42, waiting for transfers between devices, go(): lax.ppermute(block, 'seq', route)  76 us
    ppermute x42, starting transfers between devices, go(): lax.ppermute(block, 'seq', route)  46.7 us
    ppermute x15, waiting for transfers between devices, send(): return lax.ppermute(block, axis, route)  26.5 us
  transfers between devices with their start and end apart: 149, of which 75 were waited for; matrix products, arithmetic and copies ran while one was open for 6% of the time, Pallas kernels for 26%

profile of v2, /device:TPU:0, one launch (start us, length us, event | category | flops | bytes accessed | tf_op | source)
XLA Modules:
  0.0 725.2 jit_solution(7105773018071610086)
XLA Ops:
  111.1 7.7 %query_key.1 = (bf16[1024,512]{1,0:T(8,128)(2,1)S(1)}, bf16[1024,512]{1,0:T(8,128)(2,1)S(1)}, bf16[2048,1024]{1,0:T(8,128)(2,1)S(1)}) custom-call(bf16[1024,2048]{1,0:T(8,128)(2,1)S(1)} %copy-done.30, f32[1024,128]{1,0:T(8,128)S(1)} %get-tuple-element.1129.cos_ref, f32[1024,128]{1,0:T(8,128)S(1)} %get-tuple-element.1128.sin_ref, ...), custom_call_target="tpu_custom_call" | custom-call | flops 4499999744 | tf_op jit(solution)/shard_map/query_key/pallas_call | solution.py:371
  125.2 7.6 %value.1 = (bf16[1024,1024]{1,0:T(8,128)(2,1)S(1)}, bf16[2048,1024]{1,0:T(8,128)(2,1)S(1)}) custom-call(bf16[1024,2048]{1,0:T(8,128)(2,1)S(1)} %copy-done.30, bf16[256,1024]{1,0:T(8,128)(2,1)} %copy-done.88, bf16[128,1024]{1,0:T(8,128)(2,1)} %copy-done.108, bf16[128,1024]{1,0:T(8,128)(2,1)} %copy-done.113, ...), custom_call_target="tpu_custom_call" | custom-call | flops 4499999744 | tf_op jit(solution)/shard_map/value/pallas_call | solution.py:371
  161.4 8.5 %collective-permute-done.45.refs_5_ = bf16[128,1024]{1,0:T(8,128)(2,1)} collective-permute-done((bf16[128,1024]{1,0:T(8,128)(2,1)}, bf16[128,1024]{1,0:T(8,128)(2,1)}, u32[]{:S(2)}, u32[]{:S(2)}) %collective-permute-start.45) | collective-permute-done | bytes 262176 | tf_op jit(solution)/shard_map/ppermute | solution.py:137
  189.4 11.1 %collective-permute-done.53.refs_7_ = bf16[128,1024]{1,0:T(8,128)(2,1)S(1)} collective-permute-done((bf16[128,1024]{1,0:T(8,128)(2,1)S(1)}, bf16[128,1024]{1,0:T(8,128)(2,1)S(1)}, u32[]{:S(2)}, u32[]{:S(2)}) %collective-permute-start.53) | collective-permute-done | bytes 262176 | tf_op jit(solution)/shard_map/ppermute | solution.py:137
  209.2 10.8 %gate_forward.1 = (bf16[1024,1024]{1,0:T(8,128)(2,1)S(1)}, f32[1024,1024]{1,0:T(8,128)S(1)}, f32[1024,1024]{1,0:T(8,128)S(1)}, f32[1024,2]{1,0:T(8,128)S(1)}, bf16[2048,1024]{1,0:T(8,128)(2,1)S(1)}) custom-call(bf16[1024,2048]{1,0:T(8,128)(2,1)S(1)} %copy-done.31, bf16[1024,512]{1,0:T(8,128)(2,1)S(1)} %get-tuple-element.594.q_ref, ...), custom_call_target="tpu_custom_call" | custom-call | flops 6000000000 | tf_op jit(solution)/shard_map/gate_forward/pallas_call | solution.py:371
  314.1 18.5 %feed_forward.1 = (bf16[1024,2048]{1,0:T(8,128)(2,1)S(1)}, bf16[1024,1024]{1,0:T(8,128)(2,1)S(1)}, bf16[1024,1024]{1,0:T(8,128)(2,1)S(1)}, f32[1,1024]{1,0:T(1,1...) custom-call(s32[1]{0:T(128)} %bitcast.side_ref.which_ref, ...), custom_call_target="tpu_custom_call" | custom-call | flops 8000000000 | tf_op jit(solution)/shard_map/feed_forward/pallas_call | solution.py:371
  336.0 7.2 partial_rows.6
  351.3 7.0 partial_rows.7.kept_ref
  368.6 12.0 %collective-permute-done.94.refs_2_ = bf16[256,1024]{1,0:T(8,128)(2,1)S(1)} collective-permute-done((bf16[256,1024]{1,0:T(8,128)(2,1)S(1)}, bf16[256,1024]{1,0:T(8,128)(2,1)S(1)}, u32[]{:S(2)}, u32[]{:S(2)}) %collective-permute-start.94) | collective-permute-done | bytes 524320 | tf_op jit(solution)/shard_map/ppermute | solution.py:208
  385.2 10.1 %collective-permute-done.96.refs_2_ = bf16[256,1024]{1,0:T(8,128)(2,1)S(1)} collective-permute-done((bf16[256,1024]{1,0:T(8,128)(2,1)}, bf16[256,1024]{1,0:T(8,128)(2,1)S(1)}, u32[]{:S(2)}, u32[]{:S(2)}) %collective-permute-start.96) | collective-permute-done | bytes 524320 | tf_op jit(solution)/shard_map/ppermute | solution.py:208
  406.5 7.7 %norm_backward.2 = (f32[512,2048]{1,0:T(8,128)S(1)}, bf16[512,2048]{1,0:T(8,128)(2,1)S(1)}, f32[1,2048]{1,0:T(1,128)S(1)}, f32[1,2048]{1,0:T(1,128)S(1)}) custom-call(s32[1]{0:T(128)} %bitcast.side_ref.which_ref, f32[512,2048]{1,0:T(8,128)} %copy-done.44, bf16[512,2048]{1,0:T(8,128)(2,1)} %copy-done.50, bf16[512,2048]{1,0:T(8,128)(2,1)} %collective-permute-done.93.other_ref, ...), custom_call_target="tpu_custom_call" | custom-call | flops 6000000000 | tf_op jit(solution)/shard_map/norm_backward/pallas_call | solution.py:371
  421.8 13.2 %gate_backward.1 = (bf16[1024,2048]{1,0:T(8,128)(2,1)S(1)}, bf16[1024,1024]{1,0:T(8,128)(2,1)S(1)}, bf16[1024,1024]{1,0:T(8,128)(2,1)S(1)}, f32[1,1024]{1,0:T(1,...) custom-call(s32[1]{0:T(128)} %bitcast.side_ref.which_ref, bf16[512,2048]{1,0:T(8,128)(2,1)} %copy-done.69, ...), custom_call_target="tpu_custom_call" | custom-call | flops 6000000000 | tf_op jit(solution)/shard_map/gate_backward/pallas_call | solution.py:371
  437.6 10.6 %retain_backward.1 = (bf16[1024,512]{1,0:T(8,128)(2,1)S(1)}, f32[1024,512]{1,0:T(8,128)S(1)}, f32[1024,1024]{1,0:T(8,128)S(1)}) custom-call(f32[2]{0:T(128)S(1)} %subtract_log_fusion.decay_ref, bf16[1024,512]{1,0:T(8,128)(2,1)} %copy-done.73, bf16[1024,512]{1,0:T(8,128)(2,1)} %copy-done.82, bf16[1024,1024]{1,0:T(8,128)(2,1)} %copy-done.81, ...), custom_call_target="tpu_custom_call" | custom-call | flops 6000000000 | tf_op jit(solution)/shard_map/retain_backward/pallas_call | solution.py:371
  455.2 6.7 gradient.8.refs_0_
  461.9 6.7 gradient.9.refs_1_
  471.0 7.9 %collective-permute-done.102 = bf16[2,256,512]{2,1,0:T(8,128)(2,1)S(1)} collective-permute-done((bf16[2,256,512]{2,1,0:T(8,128)(2,1)S(1)}, bf16[2,256,512]{2,1,0:T(8,128)(2,1)S(1)}, u32[]{:S(2)}, u32[]{:S(2)}) %collective-permute-start.102) | collective-permute-done | bytes 524320 | tf_op jit(solution)/shard_map/ppermute | solution.py:170
  488.2 6.7 gradient.10.refs_0_
  519.5 10.6 %partial_rows.8 = bf16[512,2048]{1,0:T(8,128)(2,1)S(1)} custom-call(s32[1]{0:T(128)} %bitcast.13.which_ref, bf16[1024,1024]{1,0:T(8,128)(2,1)} %copy-done.27, bf16[1024,1024]{1,0:T(8,128)(2,1)} %copy-done.28, bf16[1024,512]{1,0:T(8,128)(2,1)} %copy-done.41, bf16[1024,512]{1,0:T(8,128)(2,1)} %copy-done.42, bf16[2048,1024]{1,0:T(8,128)(2,1)} %copy-done.36, ...), custom_call_target="tpu_custom_call" | custom-call | flops 6000000000 | tf_op jit(solution)/shard_map/partial_rows/pallas_call | solution.py:371
  541.8 11.0 %partial_rows.9.kept_ref = bf16[512,2048]{1,0:T(8,128)(2,1)S(1)} custom-call(s32[1]{0:T(128)} %bitcast.side_ref.which_ref, bf16[1024,1024]{1,0:T(8,128)(2,1)} %copy-done.27, bf16[1024,1024]{1,0:T(8,128)(2,1)} %copy-done.28, bf16[1024,512]{1,0:T(8,128)(2,1)} %copy-done.41, bf16[1024,512]{1,0:T(8,128)(2,1)} %copy-done.42, bf16[2048,1024]{1,0:T(8,128)(2,1)} %copy-done.36, ...), custom_call_target="tpu_custom_call" | custom-call | flops 6000000000 | tf_op jit(solution)/shard_map/partial_rows/pallas_call | solution.py:371
  588.2 8.8 %collective-permute-done.118.other_ref = bf16[512,2048]{1,0:T(8,128)(2,1)} collective-permute-done((bf16[512,2048]{1,0:T(8,128)(2,1)S(1)}, bf16[512,2048]{1,0:T(8,128)(2,1)}, u32[]{:S(2)}, u32[]{:S(2)}) %collective-permute-start.118) | collective-permute-done | bytes 2097184 | tf_op jit(solution)/shard_map/ppermute | solution.py:170
  597.0 8.1 %norm_backward.3 = (f32[512,2048]{1,0:T(8,128)}, bf16[512,2048]{1,0:T(8,128)(2,1)S(1)}, f32[1,2048]{1,0:T(1,128)S(1)}, f32[1,2048]{1,0:T(1,128)S(1)}) custom-call(s32[1]{0:T(128)} %bitcast.side_ref.which_ref, bf16[1024,2048]{1,0:T(8,128)(2,1)} %x_ref.5, bf16[512,2048]{1,0:T(8,128)(2,1)} %copy-done.47, bf16[512,2048]{1,0:T(8,128)(2,1)} %collective-permute-done.118.other_ref, ...), custom_call_target="tpu_custom_call" | custom-call | flops 6000000000 | tf_op jit(solution)/shard_map/norm_backward/pallas_call | solution.py:371
  605.2 7.8 %partial_rows.10 = bf16[512,2048]{1,0:T(8,128)(2,1)} custom-call(s32[1]{0:T(128)} %bitcast.13.which_ref, bf16[1024,1024]{1,0:T(8,128)(2,1)} %copy-done.49, bf16[2048,1024]{1,0:T(8,128)(2,1)} %copy-done.45), custom_call_target="tpu_custom_call" | custom-call | flops 23000000512 | tf_op jit(solution)/shard_map/partial_rows/pallas_call | solution.py:371
  641.0 7.2 collective-permute-done.136.refs_2_
  663.9 10.7 %collective-permute-done.141.refs_2_ = bf16[256,1024]{1,0:T(8,128)(2,1)S(1)} collective-permute-done((bf16[256,1024]{1,0:T(8,128)(2,1)S(1)}, bf16[256,1024]{1,0:T(8,128)(2,1)S(1)}, u32[]{:S(2)}, u32[]{:S(2)}) %collective-permute-start.141) | collective-permute-done | bytes 524320 | tf_op jit(solution)/shard_map/ppermute | solution.py:208
  (719 shorter events, 495.0 us)
Async XLA Ops:
  149.0 29.0 %collective-permute-start.59 = (bf16[2,256,512]{2,1,0:T(8,128)(2,1)}, bf16[2,256,512]{2,1,0:T(8,128)(2,1)}, u32[]{:S(2)}, u32[]{:S(2)}) collective-permute-start(bf16[2,256,512]{2,1,0:T(8,128)(2,1)} %convert_element_type.116), channel_id=1, source_target_pairs={{0,8},{4,12},{8,16},{12,20},{16,24},{20,28},{1,9},{5,13},{9,17},{1... | collective-permute-start | bytes 1572872 | tf_op jit(solution)/shard_map/ppermute | solution.py:33
  178.1 27.3 %collective-permute-start.60 = (bf16[2,256,512]{2,1,0:T(8,128)(2,1)S(1)}, bf16[2,256,512]{2,1,0:T(8,128)(2,1)S(1)}, u32[]{:S(2)}, u32[]{:S(2)}) collective-permute-start(bf16[2,256,512]{2,1,0:T(8,128)(2,1)S(1)} %broadcast_select_fusion.1), channel_id=1, source_target_pairs={{0,4},{4,0},{8,12},{12,8},{16,20},{20,16},{24,28},{28,24},{1,5},{5... | collective-permute-start | bytes 1572872 | tf_op jit(solution)/shard_map/ppermute | solution.py:40
  203.3 25.0 %collective-permute-start.65 = (bf16[128,1024]{1,0:T(8,128)(2,1)S(1)}, bf16[128,1024]{1,0:T(8,128)(2,1)}, u32[]{:S(2)}, u32[]{:S(2)}) collective-permute-start(bf16[128,1024]{1,0:T(8,128)(2,1)S(1)} %get-tuple-element.629), channel_id=1, source_target_pairs={{0,8},{8,16},{16,24},{24,28},{28,20},{20,12},{12,4},{4,0},{1,9},{9... | collective-permute-start | bytes 786440 | tf_op jit(solution)/shard_map/ppermute | solution.py:137
  203.4 24.9 %collective-permute-start.66 = (bf16[128,1024]{1,0:T(8,128)(2,1)S(1)}, bf16[128,1024]{1,0:T(8,128)(2,1)}, u32[]{:S(2)}, u32[]{:S(2)}) collective-permute-start(bf16[128,1024]{1,0:T(8,128)(2,1)S(1)} %get-tuple-element.630), channel_id=1, source_target_pairs={{8,0},{16,8},{24,16},{28,24},{20,28},{12,20},{4,12},{0,4},{9,1},{1... | collective-permute-start | bytes 786440 | tf_op jit(solution)/shard_map/ppermute | solution.py:137
  207.1 26.0 %collective-permute-start.63 = (bf16[128,1024]{1,0:T(8,128)(2,1)S(1)}, bf16[128,1024]{1,0:T(8,128)(2,1)}, u32[]{:S(2)}, u32[]{:S(2)}) collective-permute-start(bf16[128,1024]{1,0:T(8,128)(2,1)S(1)} %collective-permute-done.57.refs_1_), channel_id=1, source_target_pairs={{0,8},{8,16},{16,24},{24,28},{28,20},{20,12},{12,4},{4,0},{1,9},{9... | collective-permute-start | bytes 786440 | tf_op jit(solution)/shard_map/ppermute | solution.py:137
  208.0 25.0 %collective-permute-start.64 = (bf16[128,1024]{1,0:T(8,128)(2,1)}, bf16[128,1024]{1,0:T(8,128)(2,1)}, u32[]{:S(2)}, u32[]{:S(2)}) collective-permute-start(bf16[128,1024]{1,0:T(8,128)(2,1)} %collective-permute-done.58.refs_8_), channel_id=1, source_target_pairs={{8,0},{16,8},{24,16},{28,24},{20,28},{12,20},{4,12},{0,4},{9,1},{1... | collective-permute-start | bytes 786440 | tf_op jit(solution)/shard_map/ppermute | solution.py:137
  251.5 46.9 %collective-permute-start.88 = (bf16[512,2048]{1,0:T(8,128)(2,1)S(1)}, bf16[512,2048]{1,0:T(8,128)(2,1)S(1)}, u32[]{:S(2)}, u32[]{:S(2)}) collective-permute-start(bf16[512,2048]{1,0:T(8,128)(2,1)S(1)} %add_convert_fusion.kept_ref), channel_id=1, source_target_pairs={{0,2},{1,3},{2,0},{3,1},{4,6},{5,7},{6,4},{7,5},{8,10},{9,11},{10,... | collective-permute-start | bytes 6291464 | tf_op jit(solution)/shard_map/ppermute | solution.py:309
  358.3 48.2 %collective-permute-start.93 = (bf16[512,2048]{1,0:T(8,128)(2,1)S(1)}, bf16[512,2048]{1,0:T(8,128)(2,1)}, u32[]{:S(2)}, u32[]{:S(2)}) collective-permute-start(bf16[512,2048]{1,0:T(8,128)(2,1)S(1)} %partial_rows.7.kept_ref), channel_id=1, source_target_pairs={{0,2},{1,3},{2,0},{3,1},{4,6},{5,7},{6,4},{7,5},{8,10},{9,11},{10,... | collective-permute-start | bytes 6291464 | tf_op jit(solution)/shard_map/ppermute | solution.py:170
  417.6 35.0 %collective-permute-start.103 = (bf16[256,1024]{1,0:T(8,128)(2,1)S(1)}, bf16[256,1024]{1,0:T(8,128)(2,1)S(1)}, u32[]{:S(2)}, u32[]{:S(2)}) collective-permute-start(bf16[256,1024]{1,0:T(8,128)(2,1)S(1)} %get-tuple-element.753), channel_id=1, source_target_pairs={{0,8},{8,16},{16,24},{24,28},{28,20},{20,12},{12,4},{4,0},{1,9},{9... | collective-permute-start | bytes 1572872 | tf_op jit(solution)/shard_map/ppermute | solution.py:208
  418.0 34.6 %collective-permute-start.104 = (bf16[256,1024]{1,0:T(8,128)(2,1)S(1)}, bf16[256,1024]{1,0:T(8,128)(2,1)S(1)}, u32[]{:S(2)}, u32[]{:S(2)}) collective-permute-start(bf16[256,1024]{1,0:T(8,128)(2,1)S(1)} %get-tuple-element.754), channel_id=1, source_target_pairs={{8,0},{16,8},{24,16},{28,24},{20,28},{12,20},{4,12},{0,4},{9,1},{1... | collective-permute-start | bytes 1572872 | tf_op jit(solution)/shard_map/ppermute | solution.py:208
  454.9 24.0 %collective-permute-start.102 = (bf16[2,256,512]{2,1,0:T(8,128)(2,1)S(1)}, bf16[2,256,512]{2,1,0:T(8,128)(2,1)S(1)}, u32[]{:S(2)}, u32[]{:S(2)}) collective-permute-start(bf16[2,256,512]{2,1,0:T(8,128)(2,1)S(1)} %broadcast_select_fusion), channel_id=1, source_target_pairs={{0,4},{4,0},{8,12},{12,8},{16,20},{20,16},{24,28},{28,24},{1,5},{5... | collective-permute-start | bytes 1572872 | tf_op jit(solution)/shard_map/ppermute | solution.py:170
  469.0 25.9 %collective-permute-start.109 = (bf16[256,1024]{1,0:T(8,128)(2,1)S(1)}, bf16[256,1024]{1,0:T(8,128)(2,1)S(1)}, u32[]{:S(2)}, u32[]{:S(2)}) collective-permute-start(bf16[256,1024]{1,0:T(8,128)(2,1)S(1)} %get-tuple-element.804), channel_id=1, source_target_pairs={{0,8},{8,16},{16,24},{24,28},{28,20},{20,12},{12,4},{4,0},{1,9},{9... | collective-permute-start | bytes 1572872 | tf_op jit(solution)/shard_map/ppermute | solution.py:208
  470.4 24.5 %collective-permute-start.110 = (bf16[256,1024]{1,0:T(8,128)(2,1)S(1)}, bf16[256,1024]{1,0:T(8,128)(2,1)S(1)}, u32[]{:S(2)}, u32[]{:S(2)}) collective-permute-start(bf16[256,1024]{1,0:T(8,128)(2,1)S(1)} %get-tuple-element.805), channel_id=1, source_target_pairs={{8,0},{16,8},{24,16},{28,24},{20,28},{12,20},{4,12},{0,4},{9,1},{1... | collective-permute-start | bytes 1572872 | tf_op jit(solution)/shard_map/ppermute | solution.py:208
  530.5 24.0 %collective-permute-start.121 = (bf16[256,1024]{1,0:T(8,128)(2,1)S(1)}, bf16[256,1024]{1,0:T(8,128)(2,1)S(1)}, u32[]{:S(2)}, u32[]{:S(2)}) collective-permute-start(bf16[256,1024]{1,0:T(8,128)(2,1)S(1)} %get-tuple-element.875), channel_id=1, source_target_pairs={{0,8},{8,16},{16,24},{24,28},{28,20},{20,12},{12,4},{4,0},{1,9},{9... | collective-permute-start | bytes 1572872 | tf_op jit(solution)/shard_map/ppermute | solution.py:208
  552.9 44.1 %collective-permute-start.118 = (bf16[512,2048]{1,0:T(8,128)(2,1)S(1)}, bf16[512,2048]{1,0:T(8,128)(2,1)}, u32[]{:S(2)}, u32[]{:S(2)}) collective-permute-start(bf16[512,2048]{1,0:T(8,128)(2,1)S(1)} %partial_rows.9.kept_ref), channel_id=1, source_target_pairs={{0,2},{1,3},{2,0},{3,1},{4,6},{5,7},{6,4},{7,5},{8,10},{9,11},{10,... | collective-permute-start | bytes 6291464 | tf_op jit(solution)/shard_map/ppermute | solution.py:170
  584.0 32.1 %collective-permute-start.128 = (bf16[256,1024]{1,0:T(8,128)(2,1)}, bf16[256,1024]{1,0:T(8,128)(2,1)}, u32[]{:S(2)}, u32[]{:S(2)}) collective-permute-start(bf16[256,1024]{1,0:T(8,128)(2,1)} %get-tuple-element.916), channel_id=1, source_target_pairs={{0,8},{8,16},{16,24},{24,28},{28,20},{20,12},{12,4},{4,0},{1,9},{9... | collective-permute-start | bytes 1572872 | tf_op jit(solution)/shard_map/ppermute | solution.py:208
  586.2 29.9 %collective-permute-start.129 = (bf16[256,1024]{1,0:T(8,128)(2,1)}, bf16[256,1024]{1,0:T(8,128)(2,1)}, u32[]{:S(2)}, u32[]{:S(2)}) collective-permute-start(bf16[256,1024]{1,0:T(8,128)(2,1)} %get-tuple-element.917), channel_id=1, source_target_pairs={{8,0},{16,8},{24,16},{28,24},{20,28},{12,20},{4,12},{0,4},{9,1},{1... | collective-permute-start | bytes 1572872 | tf_op jit(solution)/shard_map/ppermute | solution.py:208
  586.2 26.8 %collective-permute-start.130 = (bf16[256,1024]{1,0:T(8,128)(2,1)S(1)}, bf16[256,1024]{1,0:T(8,128)(2,1)S(1)}, u32[]{:S(2)}, u32[]{:S(2)}) collective-permute-start(bf16[256,1024]{1,0:T(8,128)(2,1)S(1)} %get-tuple-element.918), channel_id=1, source_target_pairs={{0,8},{8,16},{16,24},{24,28},{28,20},{20,12},{12,4},{4,0},{1,9},{9... | collective-permute-start | bytes 1572872 | tf_op jit(solution)/shard_map/ppermute | solution.py:208
  588.2 24.7 %collective-permute-start.131 = (bf16[256,1024]{1,0:T(8,128)(2,1)S(1)}, bf16[256,1024]{1,0:T(8,128)(2,1)S(1)}, u32[]{:S(2)}, u32[]{:S(2)}) collective-permute-start(bf16[256,1024]{1,0:T(8,128)(2,1)S(1)} %get-tuple-element.919), channel_id=1, source_target_pairs={{8,0},{16,8},{24,16},{28,24},{20,28},{12,20},{4,12},{0,4},{9,1},{1... | collective-permute-start | bytes 1572872 | tf_op jit(solution)/shard_map/ppermute | solution.py:208
  622.7 33.6 %collective-permute-start.134 = (bf16[256,1024]{1,0:T(8,128)(2,1)}, bf16[256,1024]{1,0:T(8,128)(2,1)}, u32[]{:S(2)}, u32[]{:S(2)}) collective-permute-start(bf16[256,1024]{1,0:T(8,128)(2,1)} %get-tuple-element.957), channel_id=1, source_target_pairs={{0,8},{8,16},{16,24},{24,28},{28,20},{20,12},{12,4},{4,0},{1,9},{9... | collective-permute-start | bytes 1572872 | tf_op jit(solution)/shard_map/ppermute | solution.py:208
  624.5 31.8 %collective-permute-start.135 = (bf16[256,1024]{1,0:T(8,128)(2,1)}, bf16[256,1024]{1,0:T(8,128)(2,1)}, u32[]{:S(2)}, u32[]{:S(2)}) collective-permute-start(bf16[256,1024]{1,0:T(8,128)(2,1)} %get-tuple-element.958), channel_id=1, source_target_pairs={{8,0},{16,8},{24,16},{28,24},{20,28},{12,20},{4,12},{0,4},{9,1},{1... | collective-permute-start | bytes 1572872 | tf_op jit(solution)/shard_map/ppermute | solution.py:208
  638.8 69.7 %collective-permute-start.133 = (bf16[512,2048]{1,0:T(8,128)(2,1)S(1)}, bf16[512,2048]{1,0:T(8,128)(2,1)}, u32[]{:S(2)}, u32[]{:S(2)}) collective-permute-start(bf16[512,2048]{1,0:T(8,128)(2,1)S(1)} %partial_rows.11.kept_ref), channel_id=1, source_target_pairs={{0,2},{1,3},{2,0},{3,1},{4,6},{5,7},{6,4},{7,5},{8,10},{9,11},{10,... | collective-permute-start | bytes 6291464 | tf_op jit(solution)/shard_map/ppermute | solution.py:170
  661.8 24.1 %collective-permute-start.139 = (bf16[256,1024]{1,0:T(8,128)(2,1)S(1)}, bf16[256,1024]{1,0:T(8,128)(2,1)S(1)}, u32[]{:S(2)}, u32[]{:S(2)}) collective-permute-start(bf16[256,1024]{1,0:T(8,128)(2,1)S(1)} %get-tuple-element.976), channel_id=1, source_target_pairs={{0,8},{8,16},{16,24},{24,28},{28,20},{20,12},{12,4},{4,0},{1,9},{9... | collective-permute-start | bytes 1572872 | tf_op jit(solution)/shard_map/ppermute | solution.py:208
  663.3 25.2 %collective-permute-start.140 = (bf16[256,1024]{1,0:T(8,128)(2,1)}, bf16[256,1024]{1,0:T(8,128)(2,1)}, u32[]{:S(2)}, u32[]{:S(2)}) collective-permute-start(bf16[256,1024]{1,0:T(8,128)(2,1)} %get-tuple-element.977), channel_id=1, source_target_pairs={{8,0},{16,8},{24,16},{28,24},{20,28},{12,20},{4,12},{0,4},{9,1},{1... | collective-permute-start | bytes 1572872 | tf_op jit(solution)/shard_map/ppermute | solution.py:208
  (272 other events, 3950.0 us)

commit v3 on v2

--- a/solution.py
+++ b/solution.py
@@ -58,11 +58,11 @@
 
 
 class Weight:
-    def __init__(self, own, ahead=(), back=()):
-        self.size = lax.axis_size("seq") if ahead else 1
+    def __init__(self, own, parts=(), sign=0):
+        self.size = len(parts) + 1
         self.rows, self.cols = own.shape
-        self.arrays = [own, *ahead, *back]
-        self.count = len(self.arrays)
+        self.arrays = [own, *parts]
+        self.count, self.sign = self.size, sign
         self.shape = (self.size * self.rows, self.cols)
         self.ins = [(array, None, None) for array in self.arrays]
         self.outs = [(None, None)]
@@ -76,18 +76,11 @@
     def copies(self, parts, whole, sems):
         if self.size == 1:
             return [pltpu.make_async_copy(parts[0], whole, sems.at[0])]
-        me = lax.axis_index("seq")
-        place = ring_place(me, self.size)
-        half = self.rows // 2
-        at = [(me * self.rows, self.rows)]
-        at += [(ring_owner(place - k, self.size) * self.rows, half) for k in range(1, self.size)]
-        at += [
-            (ring_owner(place + k, self.size) * self.rows + half, half)
-            for k in range(1, self.size)
-        ]
+        place = ring_place(lax.axis_index("seq"), self.size)
+        owners = [ring_owner(place + self.sign * k, self.size) for k in range(self.size)]
         return [
-            pltpu.make_async_copy(part, whole.at[pl.ds(first, rows)], sems.at[i])
-            for i, (part, (first, rows)) in enumerate(zip(parts, at))
+            pltpu.make_async_copy(part, whole.at[pl.ds(owner * self.rows, self.rows)], sems.at[i])
+            for i, (part, owner) in enumerate(zip(parts, owners))
         ]
 
     def load(self, parts, out, whole, sems, out_sem):
@@ -122,11 +115,9 @@
 
 
 class Gather:
-    def __init__(self, own):
+    def __init__(self, ahead, back):
         self.size = lax.axis_size("seq")
-        self.own = own
-        half = own.shape[0] // 2
-        self.now = [own[:half], own[half:]]
+        self.own = self.now = [ahead, back]
         self.parts = [[], []]
         self.left = self.size - 1
 
@@ -147,7 +138,9 @@
         return self.left < 0
 
     def result(self):
-        return Weight(self.own, *self.parts)
+        return [
+            Weight(own, parts, sign) for own, parts, sign in zip(self.own, self.parts, (-1, 1))
+        ]
 
 
 class Line:
@@ -183,10 +176,10 @@
 
 
 class Reduce:
-    def __init__(self, ahead, back, part=(0, 0, 1)):
+    def __init__(self, ahead, back, turned, cut):
         self.size = lax.axis_size("seq")
-        self.part = part
         self.grads = (ahead, back)
+        self.form = (turned, cut)
         self.place = ring_place(lax.axis_index("seq"), self.size)
         self.arrived = ()
         self.step = 0
@@ -196,7 +189,7 @@
         if self.arrived:
             *self.arrived, token = barrier(*self.arrived, token)
         Line.cost = cost
-        self.now = ring_add(self.grads, self.arrived, self.place, self.step, *self.part)
+        self.now = ring_add(self.grads, self.arrived, self.place, self.step, *self.form)
         Line.cost = 0
         *self.now, token = barrier(*self.now, token)
         return token
@@ -228,47 +221,37 @@
 
 
 class Clock:
-    def __init__(self, lanes):
-        self.lanes = [[] for _ in range(lanes)]
+    def __init__(self, *rings):
+        self.queue = [(ring, left) for ring, left in rings if not ring.ended]
+        self.active = []
         self.turn = 0
 
-    def add(self, lane, chain, *values):
-        self.lanes[lane].append(chain)
-        if len(self.lanes[lane]) == 1:
-            values = self.settle(lane, values)
-        return values
-
-    def settle(self, lane, values):
-        queue = self.lanes[lane]
-        while queue:
-            if not queue[0].ended:
-                values = queue[0].tick(*values)
-            if not queue[0].ended:
-                break
-            queue.pop(0)
-        return values
+    def tick(self, *values, count=1):
+        for _ in range(count):
+            if self.queue and (not self.active or self.active[-1].left <= self.queue[0][1]):
+                self.active.append(self.queue.pop(0)[0])
+                values = self.active[-1].tick(*values)
+            elif self.active:
+                self.turn = (self.turn + 1) % len(self.active)
+                ring = self.active[self.turn]
+                values = ring.tick(*values)
+                if ring.ended:
+                    self.active.remove(ring)
+        return values[0] if len(values) == 1 else tuple(values)
 
     def until(self, ring, *values):
-        while any(ring in lane for lane in self.lanes):
+        while not ring.ended:
             values = self.tick(*values)
             values = values if isinstance(values, tuple) else (values,)
         return values[0] if len(values) == 1 else values
 
-    def tick(self, *values, count=1):
-        for _ in range(count):
-            for _ in self.lanes:
-                lane = self.turn
-                self.turn = (self.turn + 1) % len(self.lanes)
-                if self.lanes[lane]:
-                    values = self.settle(lane, values)
-                    break
-        return values[0] if len(values) == 1 else tuple(values)
-
-
-def gather(own):
+
+def gather(ahead, back):
     if lax.axis_size("seq") > RING_MOST:
-        return Builtin(Weight(lax.all_gather(own, "seq", axis=0, tiled=True)))
-    return Gather(own)
+        return Builtin(
+            [Weight(lax.all_gather(own, "seq", axis=0, tiled=True)) for own in (ahead, back)]
+        )
+    return Gather(ahead, back)
 
 
 def doubled(rows, distance):
@@ -276,24 +259,15 @@
     return jnp.concatenate([rows, lax.ppermute(rows, "seq", route)], axis=0)
 
 
-def reduce(ahead, back):
+def reduce(ahead, back, turned=False, cut=False):
     if lax.axis_size("seq") > RING_MOST:
-        total = [
+        first, second = [
             lax.psum_scatter(grad.astype(F32), "seq", scatter_dimension=0, tiled=True)
             for grad in (ahead, back)
         ]
-        return Builtin(total)
-    return Reduce(ahead, back)
-
-
-def reduce_one(grad):
-    if lax.axis_size("seq") > RING_MOST:
-        return reduce(grad, grad[:, :0])
-    return Reduce(grad, grad, (0, 1, 2))
-
-
-def reduced_one(ring):
-    return jnp.concatenate(ring.result(), axis=1)
+        first = first.T if turned else first
+        return Builtin([first, *jnp.split(second, 2, axis=1)] if cut else [first, second])
+    return Reduce(ahead, back, turned, cut)
 
 
 def halved(line, table):
@@ -712,7 +686,7 @@
     ):
         up_parts, refs = refs[: up.count], refs[up.count :]
         down_parts, refs = refs[: down.count], refs[down.count :]
-        n2_ref, act_ref, dup_ref, sum_ref, up_out, down_out, *refs = refs
+        n2_ref, act_ref, dup_ref, sum_ref, sent_ref, kept_ref, up_out, down_out, *refs = refs
         up_ref, up_sems, up_sem, down_ref, down_sems, down_sem = refs
         up.load(up_parts, up_out, up_ref, up_sems, up_sem)
         down.load(down_parts, down_out, down_ref, down_sems, down_sem)
@@ -728,12 +702,27 @@
             z = jnp.dot(n2_ref[...], up_ref[:, part], preferred_element_type=F32)
             z = z + shift_ref[:, part]
             d_act = jnp.dot(cot_ref[...], down_ref[:, part], preferred_element_type=F32)
-            half = 0.5 * (1.0 + lax.erf(z * (0.5**0.5)))
-            act_ref[:, part] = (z * half).astype(BF)
-            slope = half + z * (jnp.exp(-0.5 * z * z) * (1.0 / math.sqrt(2.0 * math.pi)))
+            below = 0.5 * (1.0 + lax.erf(z * (0.5**0.5)))
+            act_ref[:, part] = (z * below).astype(BF)
+            slope = below + z * (jnp.exp(-0.5 * z * z) * (1.0 / math.sqrt(2.0 * math.pi)))
             d_up = (slope * d_act).astype(BF)
             dup_ref[:, part] = d_up
             sum_ref[:, part] += jnp.sum(d_up.astype(F32), axis=0, keepdims=True)
+        own = pl.program_id(0) // (half // tile) == side_ref[0]
+        for at in range(0, width, 512):
+            part = slice(at, at + 512)
+            d_n2 = lax.dot_general(
+                dup_ref[...], up_ref[part], (((1,), (1,)), ((), ())), preferred_element_type=F32
+            )
+
+            @pl.when(own)
+            def _(part=part, d_n2=d_n2):
+                kept_ref[:, part] = d_n2
+
+            @pl.when(jnp.logical_not(own))
+            def _(part=part, d_n2=d_n2):
+                sent_ref[:, part] = d_n2.astype(BF)
+
         up.end(up_out, up_ref, up_sem)
         down.end(down_out, down_ref, down_sem)
 
@@ -751,15 +740,16 @@
         ],
         [((tile, width), row_tile)]
         + [((tile, cols), row_tile)] * 2
-        + [((1, cols), fixed)]
+        + [((1, cols), fixed), other_block, mine_block]
         + up.outs
         + down.outs,
         [((rows, width), BF), ((rows, cols), BF), ((rows, cols), BF), ((1, cols), F32)]
+        + [((half, width), BF), ((half, width), F32)]
         + up.shapes
         + down.shapes,
         16,
         scratch=up.scratch + down.scratch,
-        vmem=32,
+        vmem=44,
         prefetch=(side[None],),
     )
 
@@ -975,6 +965,24 @@
     )
 
 
+def add_sent(kept, sent, tile=256):
+    half, width = kept.shape
+
+    def kernel(kept_ref, sent_ref, out_ref):
+        out_ref[...] = (kept_ref[...] + sent_ref[...].astype(F32)).astype(BF)
+
+    return kernel_call(
+        kernel,
+        "add_sent",
+        (half // tile,),
+        [(kept, (tile, width), row_tile), (sent, (tile, width), row_tile)],
+        [((tile, width), row_tile)],
+        [((half, width), BF)],
+        0,
+        stay=True,
+    )[0]
+
+
 def finish_output(mid, kept, other, shift, tile=256):
     half, width = mid.shape
 
@@ -999,6 +1007,29 @@
     )[0]
 
 
+def owners_table(size, vectors):
+    if size > RING_MOST:
+        return jnp.concatenate([vector.reshape(size, -1) for vector in vectors], axis=1)
+    wide = [vector.shape[1] // size for vector in vectors]
+
+    def kernel(*refs):
+        at = 0
+        for ref, width in zip(refs, wide):
+            for i in range(size):
+                refs[-1][i : i + 1, at : at + width] = ref[:, i * width : (i + 1) * width]
+            at += width
+
+    return kernel_call(
+        kernel,
+        "owners_table",
+        (1,),
+        [(vector, vector.shape, fixed) for vector in vectors],
+        [((size, sum(wide)), fixed)],
+        [((size, sum(wide)), F32)],
+        0,
+    )[0]
+
+
 def passed(small):
     def kernel(in_ref, out_ref):
         out_ref[...] = in_ref[...]
@@ -1053,34 +1084,49 @@
     )[0]
 
 
-def ring_add(grads, arrived, place, step, left, right, parts):
+def ring_add(grads, arrived, place, step, turned, cut):
     size = lax.axis_size("seq")
     rows = grads[0].shape[0] // size
-    kind = BF if step < size else F32
+    last = step == size
+    kind = F32 if last else BF
 
     def kernel(place_ref, *refs):
+        outs = refs[2 + len(arrived) :]
         for i in range(2):
             total = refs[i][...].astype(F32)
             if arrived:
                 total = total + refs[2 + i][...].astype(F32)
-            refs[i - 2][...] = total.astype(kind)
-
-    def own(sign, part):
+            if last and turned and i == 0:
+                total = total.T
+            if last and cut and i == 1:
+                width = total.shape[1] // 2
+                outs[1][...] = total[:, :width]
+                outs[2][...] = total[:, width:]
+            else:
+                outs[i][...] = total.astype(kind)
+
+    def own(sign):
         def index(i, place_ref):
-            return (ring_owner(place_ref[0] + sign * step, size), part)
+            return (ring_owner(place_ref[0] + sign * step, size), 0)
 
         return index
 
-    blocks = [(rows, grad.shape[1] // parts) for grad in grads]
-    ins = [(grads[0], blocks[0], own(-1, left)), (grads[1], blocks[1], own(1, right))]
+    blocks = [(rows, grad.shape[1]) for grad in grads]
+    outs = list(blocks)
+    if last and turned:
+        outs[0] = blocks[0][::-1]
+    if last and cut:
+        outs[1:] = [(rows, blocks[1][1] // 2)] * 2
+    grads = [pltpu.with_memory_space_constraint(grad, pltpu.HBM) for grad in grads]
+    ins = [(grads[0], blocks[0], own(-1)), (grads[1], blocks[1], own(1))]
     ins += [(block, block.shape, fixed) for block in arrived]
     return kernel_call(
         kernel,
         "ring_add",
         (1,),
         ins,
-        [(block, fixed) for block in blocks],
-        [(block, kind) for block in blocks],
+        [(block, fixed) for block in outs],
+        [(block, kind) for block in outs],
         0,
         prefetch=(place[None],),
     )
@@ -1131,19 +1177,11 @@
             up_bias,
         ]
     ).astype(BF)[None, :]
-    clock = Clock(2)
-    qk_ring = gather(qk_own)
-    v_ring = gather(v_own)
-    x = inputs
-    (x,) = clock.add(0, qk_ring, x)
-    (x,) = clock.add(1, v_ring, x)
-    g_own = gate_weight.astype(BF)
-    o_own = out_weight.astype(BF).T
-    u_own = up_weight.astype(BF)
-    w_own = down_weight.astype(BF).T
-    g_ring, o_ring, u_ring, w_ring = [gather(own) for own in (g_own, o_own, u_own, w_own)]
-    for lane, ring in enumerate((g_ring, o_ring, u_ring, w_ring)):
-        clock.add(lane % 2, ring)
+    qkv_ring = gather(qk_own, v_own)
+    go_ring = gather(gate_weight.astype(BF), out_weight.astype(BF).T)
+    uw_ring = gather(up_weight.astype(BF), down_weight.astype(BF).T)
+    clock = Clock((qkv_ring, 0), (go_ring, 1), (uw_ring, 0))
+    x = clock.tick(inputs)
 
     first_row = lax.axis_index("seq") * rows
     log_decay = jnp.log(
@@ -1158,7 +1196,7 @@
     distance = 1
     while distance < size:
         table = doubled(table, distance)
-        x, table = clock.tick(x, table, count=2)
+        table = clock.tick(table)
         distance *= 2
     table = table[jnp.arange(size) ^ lax.axis_index("seq")].astype(F32)
 
@@ -1178,17 +1216,18 @@
     n1, cosine, sine, number, entry_cols, exit_cols = clock.tick(
         n1, cosine, sine, number, entry_cols, exit_cols
     )
-    n1 = clock.until(v_ring, n1)
-
+    n1 = clock.until(qkv_ring, n1)
+
+    qk_weight, v_weight = qkv_ring.result()
+    q, k, qk_mat = project_turn(n1, qk_weight, cosine, sine)
+    n1, q, k = barrier(n1, q, k)
     n1 = clock.tick(n1)
-    q, k, qk_mat = project_turn(n1, qk_ring.result(), cosine, sine)
-    q, k, n1 = clock.tick(q, k, n1, count=2)
-    v, v_mat = project(n1, v_ring.result())
-    v, q, k = clock.tick(v, q, k, count=2)
+    v, v_mat = project(n1, v_weight)
+    v, q, k = clock.tick(v, q, k)
     local_out, local_state = retain(q, k, v, number, exit_cols, log_decay)
     local_out, local_state = clock.tick(local_out, local_state)
     state_parts = Others(local_state.astype(BF), 1).second()
-    local_out = clock.until(o_ring, local_out)
+    local_out = clock.until(go_ring, local_out)
 
     def gathered_state(first, rest, direction):
         total, weight = first.astype(F32), 1.0
@@ -1201,13 +1240,13 @@
 
     state = gathered_state(state_parts[0], state_parts[1:], 1)
     state, local_out = barrier(state, local_out)
-    state = clock.tick(state)
+    g_weight, o_weight = go_ring.result()
     y, gate, r_hat, r_dev, g_mat = gate_forward(
-        n1, g_ring.result(), q, entry_cols, state, local_out, group_scale, group_shift
-    )
-    y = clock.tick(y, count=2)
-    o_mat = assemble(o_ring.result())
-    y, o_mat = clock.tick(y, o_mat)
+        n1, g_weight, q, entry_cols, state, local_out, group_scale, group_shift
+    )
+    y = clock.tick(y)
+    o_mat = assemble(o_weight)
+    y, o_mat = barrier(y, o_mat)
 
     def pick(values, which):
         return lax.dynamic_slice_in_dim(values, which * half, half)
@@ -1219,16 +1258,16 @@
         return (make(pick(value, side)) + sent.astype(F32)).astype(BF)
 
     kept = tp_first(lambda part: dot(part, o_mat, ((1,), (1,))), y)
-    kept = clock.tick(kept)
     other = swap(kept, 2)
-    kept = clock.tick(kept, count=7)
+    kept = clock.tick(kept, count=4)
     kept, other = barrier(kept, other)
     mid, n2_mine = second_norm(inputs, side, kept, other, gain_two, bias_two)
     n2_other = swap(n2_mine, 1)
     n2_mine, n2_other = barrier(n2_mine, n2_other)
-    n2_mine, n2_other = clock.until(w_ring, n2_mine, n2_other)
-    n2, act, d_up, grad_up_bias, u_mat, w_mat = feed_forward(
-        n2_mine, n2_other, side, u_ring.result(), up_shift, cotangent, w_ring.result()
+    n2_mine, n2_other = clock.until(uw_ring, n2_mine, n2_other)
+    u_weight, w_weight = uw_ring.result()
+    n2, act, d_up, grad_up_bias, sent_two, kept_two, u_mat, w_mat = feed_forward(
+        n2_mine, n2_other, side, u_weight, up_shift, cotangent, w_weight
     )
 
     line = Line(grad_up_bias)
@@ -1251,12 +1290,12 @@
     def partial_kept(values, mats, sent, cost=0):
         return line.run(lambda *v: partial_rows(v, mats, side, sent), *values, cost=cost)
 
-    sent_two = partial_sent((d_up,), ((u_mat, 0),), 1)
+    sent_two = line.send(sent_two, "tp", pairs_one)
     grad_w = line.run(gradient, cotangent, act, cost=23)
-    kept_two = partial_kept((d_up,), ((u_mat, 0),), sent_two)
+    kept_two = line.run(add_sent, kept_two, sent_two)
     other_two = line.send(kept_two, "tp", pairs_two)
     grad_u = line.run(gradient, n2, d_up, cost=23)
-    wu_back = reduce(grad_w, grad_u)
+    wu_back = reduce(grad_w, grad_u, turned=True)
     line.tick(wu_back, wu_back, wu_back)
     d_mid, d_branch_mine, grad_second_gain, grad_second_bias = line.run(
         lambda kept, other: norm_backward(
@@ -1288,6 +1327,7 @@
         cost=6,
     )
     others = Others(own_grad, -1, line.send)
+    line.tick(wu_back)
     d_q, d_k, d_v = line.run(
         lambda d_r: retain_backward(
             q, k, v, d_r, state, number, entry_cols, log_decay, cosine, sine
@@ -1298,9 +1338,9 @@
     leaving_parts = others.second()
     line.tick(wu_back)
     grad_o = line.run(gradient, d_branch, y, cost=6)
-    grad_g = line.run(gradient, n1, d_gate)
     line.tick(wu_back)
-    og_back = reduce(grad_o, grad_g)
+    grad_g = line.run(gradient, n1, d_gate, cost=6)
+    og_back = reduce(grad_o, grad_g, turned=True)
     line.tick(og_back)
     leaving = line.run(lambda first, *rest: gathered_state(first, rest, -1), *leaving_parts)
     d_k, d_v = line.run(
@@ -1309,12 +1349,11 @@
         d_v,
         cost=6,
     )
+    line.tick(wu_back)
     grad_v = line.run(gradient, n1, d_v)
-    line.tick(wu_back, og_back)
     grad_qk = line.run(gradient, n1, d_q, d_k, cost=6)
-    line.tick(wu_back)
-    vqk_back = reduce(grad_v, grad_qk)
-    line.tick(vqk_back)
+    vqk_back = reduce(grad_v, grad_qk, cut=True)
+    line.tick(vqk_back, og_back)
     d_all = (d_gate, d_v, d_q, d_k)
     mats_all = ((g_mat, 0), (v_mat, 0), (qk_mat, 0), (qk_mat, 1))
     sent_one = partial_sent(d_all, mats_all, 1, cost=6)
@@ -1324,6 +1363,7 @@
     other_one = line.send(kept_one, "tp", pairs_two)
     grad_second_gain = line.fill(grad_second_gain, 23)
     line.tick(og_back, vqk_back)
+    part_out = line.run(lambda act: partial_rows((act,), ((w_mat, 0),), 1 - side), act)
     line.tick(og_back, vqk_back)
     _, grad_mine, grad_first_gain, grad_first_bias = line.run(
         lambda kept, other: norm_backward(
@@ -1334,47 +1374,45 @@
         cost=6,
     )
     grad_other = to_partner(grad_mine, 1)[0]
-    sent_out = partial_sent((act,), ((w_mat, 0),), 1, cost=23)
+    sent_out = line.send(part_out, "tp", pairs_one)
     line.tick(og_back, vqk_back, cost=12)
     grad_inputs = line.run(
         lambda mine, other: both_halves(mine, other, side, F32), grad_mine, grad_other
     )
-    kept_out = partial_kept((act,), ((w_mat, 0),), sent_out)
+    kept_out = partial_kept((act,), ((w_mat, 0),), (sent_out,))
     other_out = line.send(kept_out, "tp", pairs_two)
     grad_second_gain = line.fill(grad_second_gain, 23)
     line.tick(og_back, vqk_back)
 
     grad_up_bias = line.token
-    table = jnp.concatenate(
-        [
-            vector.reshape(size, -1)
-            for vector in (
-                grad_first_gain,
-                grad_first_bias,
-                grad_second_gain,
-                grad_second_bias,
-                grad_down_bias,
-                grad_group_gain,
-                grad_group_bias,
-                grad_up_bias,
-            )
-        ],
-        axis=1,
+    table = line.run(
+        lambda *vectors: owners_table(size, vectors),
+        grad_first_gain,
+        grad_first_bias,
+        grad_second_gain,
+        grad_second_bias,
+        grad_down_bias[None, :],
+        grad_group_gain,
+        grad_group_bias,
+        grad_up_bias,
     )
     line.token = grad_inputs
     table, sent = halved(line, table)
     line.tick(vqk_back, og_back)
+    output_mine = line.run(
+        lambda kept, other: finish_output(mid, kept, other, down_shift),
+        kept_out,
+        other_out,
+        cost=6,
+    )
     while table.shape[0] > 1:
         table = line.run(lambda kept, sent: kept + sent, table, sent)
         table, sent = halved(line, table)
         line.tick(vqk_back, og_back)
+    output_other = to_partner(output_mine, 1)[0]
     small = line.run(lambda kept, sent: kept + sent, table, sent)[0]
     halves = small[: 4 * shard]
     sent = line.send(halves, "tp", pairs_one)
-    output_mine = line.run(
-        lambda kept, other: finish_output(mid, kept, other, down_shift), kept_out, other_out
-    )
-    output_other = to_partner(output_mine, 1)[0]
     while not (og_back.ended and vqk_back.ended):
         line.tick(vqk_back, og_back)
     output = line.run(
@@ -1387,8 +1425,7 @@
     own_units = [small[5 * shard + i * unit : 5 * shard + (i + 1) * unit] for i in range(3)]
     own_w, own_u = wu_back.result()
     own_o, own_g = og_back.result()
-    own_v, own_qk = vqk_back.result()
-    own_q, own_k = own_qk[:, : heads * KD], own_qk[:, heads * KD :]
+    own_v, own_q, own_k = vqk_back.result()
     return (
         output,
         grad_inputs,
@@ -1400,12 +1437,12 @@
         own_g,
         own_units[0],
         own_units[1],
-        own_o.T,
+        own_o,
         own[2],
         own[3],
         own_u,
         own_units[2],
-        own_w.T,
+        own_w,
         own_down_bias,
     )
 

time: 735 us -> 703 us (0.956)
  waiting for transfers between devices: 210 us -> 258 us
  starting transfers between devices: 160 us -> 114 us
  local copies, waits for them, and re-layouts: 85.5 us -> 48.1 us
  Pallas kernels: 231 us -> 246 us
  other arithmetic: 23.6 us -> 13.8 us
    ppermute x84 -> x42, starting transfers between devices: 87.7 us -> 45.5 us  [tick(): lax.ppermute(block, 'seq', route)]
    unnamed x316 -> x223, local copies, waits for them, and re-layouts: 78.8 us -> 45 us
    ppermute x3, waiting for transfers between devices: 0.01 us -> 27.2 us  [doubled(): return jnp.concatenate([rows, lax.ppermute(rows, 'seq', route)], axis=0)]
    pallas_call x55, Pallas kernels: 231 us -> 246 us  [kernel_call(): pl.pallas_call(body, out_shape=[jax.ShapeDtypeStruct(s, t) for s, t in sh...]
    ppermute x84 -> x42, waiting for transfers between devices: 101 us -> 111 us  [tick(): lax.ppermute(block, 'seq', route)]
    ppermute x15, waiting for transfers between devices: 26.5 us -> 17.2 us  [send(): return lax.ppermute(block, axis, route)]
    ppermute x42, waiting for transfers between devices: 76 us -> 85 us  [go(): lax.ppermute(block, 'seq', route)]
  transfers between devices with their start and end apart: 149 -> 107, of which waited for: 75 -> 65; matrix products, arithmetic and copies ran while one was open for 6% -> 3% of each run, Pallas kernels for 26% -> 30%
where the time goes in v3:
time: 703 us; the launch traced here: 695 us
  waiting for transfers between devices  258 us (37%)
  Pallas kernels  246 us (35%)
  starting transfers between devices  114 us (16%)
  local copies, waits for them, and re-layouts  48.1 us (7%)
  other arithmetic  13.8 us (2%)
  matrix products  8.94 us (1%)
    pallas_call x55, Pallas kernels, kernel_call(): pl.pallas_call(body, out_shape=[jax.ShapeDtypeStruct(s, t) for s, t in sh...  246 us
    ppermute x42, waiting for transfers between devices, tick(): lax.ppermute(block, 'seq', route)  111 us
    ppermute x42, waiting for transfers between devices, go(): lax.ppermute(block, 'seq', route)  85 us
    ppermute x42, starting transfers between devices, tick(): lax.ppermute(block, 'seq', route)  45.5 us
    unnamed x223, local copies, waits for them, and re-layouts  45 us
    ppermute x42, starting transfers between devices, go(): lax.ppermute(block, 'seq', route)  44.1 us
    ppermute x3, waiting for transfers between devices, doubled(): return jnp.concatenate([rows, lax.ppermute(rows, 'seq', route)], axis=0)  27.2 us
    ppermute x15, waiting for transfers between devices, send(): return lax.ppermute(block, axis, route)  17.2 us
  transfers between devices with their start and end apart: 107, of which 65 were waited for; matrix products, arithmetic and copies ran while one was open for 3% of the time, Pallas kernels for 30%

profile of v3, /device:TPU:0, one launch (start us, length us, event | category | flops | bytes accessed | tf_op | source)
XLA Modules:
  0.0 694.8 jit_solution(7458146873798150354)
XLA Ops:
  9.6 9.8 %collective-permute-done.2 = bf16[1,1664]{1,0:T(2,128)(2,1)S(1)} collective-permute-done((bf16[1,1664]{1,0:T(2,128)(2,1)S(1)}, bf16[1,1664]{1,0:T(2,128)(2,1)S(1)}, u32[]{:S(2)}, u32[]{:S(2)}) %collective-permute-start.2) | collective-permute-done | bytes 3360 | tf_op jit(solution)/shard_map/ppermute | solution.py:259
  24.4 10.3 %collective-permute-done.5 = bf16[2,1664]{1,0:T(2,128)(2,1)S(1)} collective-permute-done((bf16[2,1664]{1,0:T(2,128)(2,1)S(1)}, bf16[2,1664]{1,0:T(2,128)(2,1)S(1)}, u32[]{:S(2)}, u32[]{:S(2)}) %collective-permute-start.5) | collective-permute-done | bytes 6688 | tf_op jit(solution)/shard_map/ppermute | solution.py:259
  42.5 7.1 %collective-permute-done.8 = bf16[4,1664]{1,0:T(4,128)(2,1)S(1)} collective-permute-done((bf16[4,1664]{1,0:T(4,128)(2,1)S(1)}, bf16[4,1664]{1,0:T(4,128)(2,1)S(1)}, u32[]{:S(2)}, u32[]{:S(2)}) %collective-permute-start.8) | collective-permute-done | bytes 13344 | tf_op jit(solution)/shard_map/ppermute | solution.py:259
  64.1 8.4 %collective-permute-done.11.refs_5_ = bf16[256,1024]{1,0:T(8,128)(2,1)} collective-permute-done((bf16[256,1024]{1,0:T(8,128)(2,1)}, bf16[256,1024]{1,0:T(8,128)(2,1)}, u32[]{:S(2)}, u32[]{:S(2)}) %collective-permute-start.11) | collective-permute-done | bytes 524320 | tf_op jit(solution)/shard_map/ppermute | solution.py:128
  79.4 9.4 %collective-permute-done.13.refs_1_ = bf16[256,1024]{1,0:T(8,128)(2,1)S(1)} collective-permute-done((bf16[256,1024]{1,0:T(8,128)(2,1)S(1)}, bf16[256,1024]{1,0:T(8,128)(2,1)S(1)}, u32[]{:S(2)}, u32[]{:S(2)}) %collective-permute-start.13) | collective-permute-done | bytes 524320 | tf_op jit(solution)/shard_map/ppermute | solution.py:128
  92.7 7.4 %collective-permute-done.17.refs_6_ = bf16[256,1024]{1,0:T(8,128)(2,1)} collective-permute-done((bf16[256,1024]{1,0:T(8,128)(2,1)}, bf16[256,1024]{1,0:T(8,128)(2,1)}, u32[]{:S(2)}, u32[]{:S(2)}) %collective-permute-start.17) | collective-permute-done | bytes 524320 | tf_op jit(solution)/shard_map/ppermute | solution.py:128
  124.4 7.7 %query_key.1 = (bf16[1024,512]{1,0:T(8,128)(2,1)S(1)}, bf16[1024,512]{1,0:T(8,128)(2,1)S(1)}, bf16[2048,1024]{1,0:T(8,128)(2,1)S(1)}) custom-call(bf16[1024,2048]{1,0:T(8,128)(2,1)S(1)} %copy-done.16, f32[1024,128]{1,0:T(8,128)S(1)} %get-tuple-element.968.cos_ref, f32[1024,128]{1,0:T(8,128)S(1)} %get-tuple-element.967.sin_ref, bf16[256,1024]{1,0:T(8,128)(2,1)} %copy-done.75, ...), custom_call_target="tpu_custom_call" | custom-call | flops 4499999744 | tf_op jit(solution)/shard_map/query_key/pallas_call | solution.py:345
  140.4 7.9 %value.1 = (bf16[1024,1024]{1,0:T(8,128)(2,1)S(1)}, bf16[2048,1024]{1,0:T(8,128)(2,1)S(1)}) custom-call(bf16[1024,2048]{1,0:T(8,128)(2,1)S(1)} %copy-done.17, bf16[256,1024]{1,0:T(8,128)(2,1)} %copy-done.68, bf16[256,1024]{1,0:T(8,128)(2,1)} %copy-done.81, bf16[256,1024]{1,0:T(8,128)(2,1)} %copy-done.84, bf16[256,1024]{1,0:T(8,128)(2,1)} %collective-permute-done.7.refs_3_, ...), custom_call_target="tpu_custom_call" | custom-call | flops 4499999744 | tf_op jit(solution)/shard_map/value/pallas_call | solution.py:345
  190.9 11.0 %collective-permute-done.29.refs_1_ = bf16[256,1024]{1,0:T(8,128)(2,1)} collective-permute-done((bf16[256,1024]{1,0:T(8,128)(2,1)S(1)}, bf16[256,1024]{1,0:T(8,128)(2,1)}, u32[]{:S(2)}, u32[]{:S(2)}) %collective-permute-start.29) | collective-permute-done | bytes 524320 | tf_op jit(solution)/shard_map/ppermute | solution.py:128
  213.4 11.7 %gate_forward.1 = (bf16[1024,1024]{1,0:T(8,128)(2,1)S(1)}, f32[1024,1024]{1,0:T(8,128)S(1)}, f32[1024,1024]{1,0:T(8,128)S(1)}, f32[1024,2]{1,0:T(8,128)S(1)}, bf16[2048,1024]{1,0:T(8,128)(2,1)S(1)}) custom-call(bf16[1024,2048]{1,0:T(8,128)(2,1)S(1)} %copy-done.18, bf16[1024,512]{1,0:T(8,128)(2,1)S(1)} %copy-done.46, ...), custom_call_target="tpu_custom_call" | custom-call | flops 6000000000 | tf_op jit(solution)/shard_map/gate_forward/pallas_call | solution.py:345
  252.3 11.5 %collective-permute-done.42.refs_5_ = bf16[256,1024]{1,0:T(8,128)(2,1)S(1)} collective-permute-done((bf16[256,1024]{1,0:T(8,128)(2,1)S(1)}, bf16[256,1024]{1,0:T(8,128)(2,1)S(1)}, u32[]{:S(2)}, u32[]{:S(2)}) %collective-permute-start.42) | collective-permute-done | bytes 524320 | tf_op jit(solution)/shard_map/ppermute | solution.py:128
  267.0 10.0 %collective-permute-done.44.refs_6_ = bf16[256,1024]{1,0:T(8,128)(2,1)S(1)} collective-permute-done((bf16[256,1024]{1,0:T(8,128)(2,1)S(1)}, bf16[256,1024]{1,0:T(8,128)(2,1)S(1)}, u32[]{:S(2)}, u32[]{:S(2)}) %collective-permute-start.44) | collective-permute-done | bytes 524320 | tf_op jit(solution)/shard_map/ppermute | solution.py:128
  279.8 8.9 %collective-permute-done.46.refs_7_ = bf16[256,1024]{1,0:T(8,128)(2,1)S(1)} collective-permute-done((bf16[256,1024]{1,0:T(8,128)(2,1)S(1)}, bf16[256,1024]{1,0:T(8,128)(2,1)S(1)}, u32[]{:S(2)}, u32[]{:S(2)}) %collective-permute-start.46) | collective-permute-done | bytes 524320 | tf_op jit(solution)/shard_map/ppermute | solution.py:128
  302.0 28.5 %feed_forward.1 = (bf16[1024,2048]{1,0:T(8,128)(2,1)}, bf16[1024,1024]{1,0:T(8,128)(2,1)S(1)}, bf16[1024,1024]{1,0:T(8,128)(2,1)S(1)}, f32[1,1024]{1,0:T(1,128)S...) custom-call(s32[1]{0:T(128)} %bitcast.side_ref.which_ref, ...), custom_call_target="tpu_custom_call" | custom-call | flops 8000000000 | tf_op jit(solution)/shard_map/feed_forward/pallas_call | solution.py:345
  356.0 12.0 %collective-permute-done.52.refs_2_ = bf16[256,1024]{1,0:T(8,128)(2,1)S(1)} collective-permute-done((bf16[256,1024]{1,0:T(8,128)(2,1)S(1)}, bf16[256,1024]{1,0:T(8,128)(2,1)S(1)}, u32[]{:S(2)}, u32[]{:S(2)}) %collective-permute-start.52) | collective-permute-done | bytes 524320 | tf_op jit(solution)/shard_map/ppermute | solution.py:201
  375.0 9.9 %collective-permute-done.54.refs_2_ = bf16[256,1024]{1,0:T(8,128)(2,1)S(1)} collective-permute-done((bf16[256,1024]{1,0:T(8,128)(2,1)}, bf16[256,1024]{1,0:T(8,128)(2,1)S(1)}, u32[]{:S(2)}, u32[]{:S(2)}) %collective-permute-start.54) | collective-permute-done | bytes 524320 | tf_op jit(solution)/shard_map/ppermute | solution.py:201
  404.8 13.2 %gate_backward.1 = (bf16[1024,2048]{1,0:T(8,128)(2,1)S(1)}, bf16[1024,1024]{1,0:T(8,128)(2,1)S(1)}, bf16[1024,1024]{1,0:T(8,128)(2,1)S(1)}, f32[1,1024]{1,0:T(1,...) custom-call(s32[1]{0:T(128)} %bitcast.side_ref.which_ref, bf16[512,2048]{1,0:T(8,128)(2,1)} %copy-done.39, ...), custom_call_target="tpu_custom_call" | custom-call | flops 6000000000 | tf_op jit(solution)/shard_map/gate_backward/pallas_call | solution.py:345
  424.9 10.6 %retain_backward.1 = (bf16[1024,512]{1,0:T(8,128)(2,1)S(1)}, f32[1024,512]{1,0:T(8,128)S(1)}, f32[1024,1024]{1,0:T(8,128)S(1)}) custom-call(f32[2]{0:T(128)S(1)} %subtract_log_fusion.decay_ref, bf16[1024,512]{1,0:T(8,128)(2,1)} %copy-done.44, bf16[1024,512]{1,0:T(8,128)(2,1)} %copy-done.55, bf16[1024,1024]{1,0:T(8,128)(2,1)} %copy-done.53, ...), custom_call_target="tpu_custom_call" | custom-call | flops 6000000000 | tf_op jit(solution)/shard_map/retain_backward/pallas_call | solution.py:345
  439.5 6.8 collective-permute-done.64.refs_3_
  518.3 10.6 %partial_rows.4 = bf16[512,2048]{1,0:T(8,128)(2,1)S(1)} custom-call(s32[1]{0:T(128)} %bitcast.14.which_ref, bf16[1024,1024]{1,0:T(8,128)(2,1)} %copy-done.11, bf16[1024,1024]{1,0:T(8,128)(2,1)} %copy-done.7, bf16[1024,512]{1,0:T(8,128)(2,1)} %copy-done.12, bf16[1024,512]{1,0:T(8,128)(2,1)} %copy-done.13, bf16[2048,1024]{1,0:T(8,128)(2,1)} %copy-done.9, ...), custom_call_target="tpu_custom_call" | custom-call | flops 6000000000 | tf_op jit(solution)/shard_map/partial_rows/pallas_call | solution.py:345
  542.6 11.0 %partial_rows.5.kept_ref = bf16[512,2048]{1,0:T(8,128)(2,1)S(1)} custom-call(s32[1]{0:T(128)} %bitcast.side_ref.which_ref, bf16[1024,1024]{1,0:T(8,128)(2,1)} %copy-done.11, bf16[1024,1024]{1,0:T(8,128)(2,1)} %copy-done.7, bf16[1024,512]{1,0:T(8,128)(2,1)} %copy-done.12, bf16[1024,512]{1,0:T(8,128)(2,1)} %copy-done.13, bf16[2048,1024]{1,0:T(8,128)(2,1)} %copy-done.9, ...), custom_call_target="tpu_custom_call" | custom-call | flops 6000000000 | tf_op jit(solution)/shard_map/partial_rows/pallas_call | solution.py:345
  588.9 6.9 collective-permute-done.76.other_ref
  597.2 8.1 %norm_backward.3 = (f32[512,2048]{1,0:T(8,128)}, bf16[512,2048]{1,0:T(8,128)(2,1)S(1)}, f32[1,2048]{1,0:T(1,128)S(1)}, f32[1,2048]{1,0:T(1,128)S(1)}) custom-call(s32[1]{0:T(128)} %bitcast.side_ref.which_ref, bf16[1024,2048]{1,0:T(8,128)(2,1)} %x_ref.5, bf16[512,2048]{1,0:T(8,128)(2,1)} %copy-done.21, bf16[512,2048]{1,0:T(8,128)(2,1)} %copy-done.79, ...), custom_call_target="tpu_custom_call" | custom-call | flops 6000000000 | tf_op jit(solution)/shard_map/norm_backward/pallas_call | solution.py:345
  642.2 10.5 %collective-permute-done.98.refs_2_ = bf16[256,1024]{1,0:T(8,128)(2,1)} collective-permute-done((bf16[256,1024]{1,0:T(8,128)(2,1)}, bf16[256,1024]{1,0:T(8,128)(2,1)}, u32[]{:S(2)}, u32[]{:S(2)}) %collective-permute-start.98) | collective-permute-done | bytes 524320 | tf_op jit(solution)/shard_map/ppermute | solution.py:201
  (524 shorter events, 440.2 us)
Async XLA Ops:
  76.0 24.1 %collective-permute-start.17 = (bf16[256,1024]{1,0:T(8,128)(2,1)}, bf16[256,1024]{1,0:T(8,128)(2,1)}, u32[]{:S(2)}, u32[]{:S(2)}) collective-permute-start(bf16[256,1024]{1,0:T(8,128)(2,1)} %collective-permute-done.11.refs_5_), channel_id=1, source_target_pairs={{0,8},{8,16},{16,24},{24,28},{28,20},{20,12},{12,4},{4,0},{1,9},{9... | collective-permute-start | bytes 1572872 | tf_op jit(solution)/shard_map/ppermute | solution.py:128
  77.3 24.0 %collective-permute-start.18 = (bf16[256,1024]{1,0:T(8,128)(2,1)}, bf16[256,1024]{1,0:T(8,128)(2,1)}, u32[]{:S(2)}, u32[]{:S(2)}) collective-permute-start(bf16[256,1024]{1,0:T(8,128)(2,1)} %collective-permute-done.12.refs_5_), channel_id=1, source_target_pairs={{8,0},{16,8},{24,16},{28,24},{20,28},{12,20},{4,12},{0,4},{9,1},{1... | collective-permute-start | bytes 1572872 | tf_op jit(solution)/shard_map/ppermute | solution.py:128
  90.4 22.1 %collective-permute-start.16 = (bf16[256,1024]{1,0:T(8,128)(2,1)S(1)}, bf16[256,1024]{1,0:T(8,128)(2,1)S(1)}, u32[]{:S(2)}, u32[]{:S(2)}) collective-permute-start(bf16[256,1024]{1,0:T(8,128)(2,1)S(1)} %collective-permute-done.14.refs_1_), channel_id=1, source_target_pairs={{8,0},{16,8},{24,16},{28,24},{20,28},{12,20},{4,12},{0,4},{9,1},{1... | collective-permute-start | bytes 1572872 | tf_op jit(solution)/shard_map/ppermute | solution.py:128
  112.5 22.6 %collective-permute-start.19 = (bf16[256,1024]{1,0:T(8,128)(2,1)}, bf16[256,1024]{1,0:T(8,128)(2,1)}, u32[]{:S(2)}, u32[]{:S(2)}) collective-permute-start(bf16[256,1024]{1,0:T(8,128)(2,1)} %collective-permute-done.15.refs_2_), channel_id=1, source_target_pairs={{0,8},{8,16},{16,24},{24,28},{28,20},{20,12},{12,4},{4,0},{1,9},{9... | collective-permute-start | bytes 1572872 | tf_op jit(solution)/shard_map/ppermute | solution.py:128
  112.8 22.2 %collective-permute-start.20 = (bf16[256,1024]{1,0:T(8,128)(2,1)S(1)}, bf16[256,1024]{1,0:T(8,128)(2,1)S(1)}, u32[]{:S(2)}, u32[]{:S(2)}) collective-permute-start(bf16[256,1024]{1,0:T(8,128)(2,1)S(1)} %collective-permute-done.16.refs_2_), channel_id=1, source_target_pairs={{8,0},{16,8},{24,16},{28,24},{20,28},{12,20},{4,12},{0,4},{9,1},{1... | collective-permute-start | bytes 1572872 | tf_op jit(solution)/shard_map/ppermute | solution.py:128
  187.1 23.0 %collective-permute-start.35 = (bf16[256,1024]{1,0:T(8,128)(2,1)}, bf16[256,1024]{1,0:T(8,128)(2,1)}, u32[]{:S(2)}, u32[]{:S(2)}) collective-permute-start(bf16[256,1024]{1,0:T(8,128)(2,1)} %collective-permute-done.27.refs_6_), channel_id=1, source_target_pairs={{0,8},{8,16},{16,24},{24,28},{28,20},{20,12},{12,4},{4,0},{1,9},{9... | collective-permute-start | bytes 1572872 | tf_op jit(solution)/shard_map/ppermute | solution.py:128
  201.9 23.2 %collective-permute-start.31 = (bf16[256,1024]{1,0:T(8,128)(2,1)}, bf16[256,1024]{1,0:T(8,128)(2,1)S(1)}, u32[]{:S(2)}, u32[]{:S(2)}) collective-permute-start(bf16[256,1024]{1,0:T(8,128)(2,1)} %collective-permute-done.29.refs_1_), channel_id=1, source_target_pairs={{0,8},{8,16},{16,24},{24,28},{28,20},{20,12},{12,4},{4,0},{1,9},{9... | collective-permute-start | bytes 1572872 | tf_op jit(solution)/shard_map/ppermute | solution.py:128
  202.0 23.1 %collective-permute-start.32 = (bf16[256,1024]{1,0:T(8,128)(2,1)}, bf16[256,1024]{1,0:T(8,128)(2,1)S(1)}, u32[]{:S(2)}, u32[]{:S(2)}) collective-permute-start(bf16[256,1024]{1,0:T(8,128)(2,1)} %collective-permute-done.30.refs_9_), channel_id=1, source_target_pairs={{8,0},{16,8},{24,16},{28,24},{20,28},{12,20},{4,12},{0,4},{9,1},{1... | collective-permute-start | bytes 1572872 | tf_op jit(solution)/shard_map/ppermute | solution.py:128
  245.6 47.7 %collective-permute-start.48 = (bf16[512,2048]{1,0:T(8,128)(2,1)S(1)}, bf16[512,2048]{1,0:T(8,128)(2,1)S(1)}, u32[]{:S(2)}, u32[]{:S(2)}) collective-permute-start(bf16[512,2048]{1,0:T(8,128)(2,1)S(1)} %add_convert_fusion.kept_ref), channel_id=1, source_target_pairs={{0,2},{1,3},{2,0},{3,1},{4,6},{5,7},{6,4},{7,5},{8,10},{9,11},{10,... | collective-permute-start | bytes 6291464 | tf_op jit(solution)/shard_map/ppermute | solution.py:283
  342.5 48.0 %collective-permute-start.51 = (bf16[512,2048]{1,0:T(8,128)(2,1)S(1)}, bf16[512,2048]{1,0:T(8,128)(2,1)}, u32[]{:S(2)}, u32[]{:S(2)}) collective-permute-start(bf16[512,2048]{1,0:T(8,128)(2,1)S(1)} %add_sent.1.kept_ref), channel_id=1, source_target_pairs={{0,2},{1,3},{2,0},{3,1},{4,6},{5,7},{6,4},{7,5},{8,10},{9,11},{10,... | collective-permute-start | bytes 6291464 | tf_op jit(solution)/shard_map/ppermute | solution.py:163
  437.7 36.5 %collective-permute-start.62 = (bf16[2,256,512]{2,1,0:T(8,128)(2,1)S(1)}, bf16[2,256,512]{2,1,0:T(8,128)(2,1)S(1)}, u32[]{:S(2)}, u32[]{:S(2)}) collective-permute-start(bf16[2,256,512]{2,1,0:T(8,128)(2,1)S(1)} %broadcast_select_fusion), channel_id=1, source_target_pairs={{0,4},{4,0},{8,12},{12,8},{16,20},{20,16},{24,28},{28,24},{1,5},{5... | collective-permute-start | bytes 1572872 | tf_op jit(solution)/shard_map/ppermute | solution.py:163
  483.3 31.5 %collective-permute-start.71 = (bf16[256,1024]{1,0:T(8,128)(2,1)S(1)}, bf16[256,1024]{1,0:T(8,128)(2,1)S(1)}, u32[]{:S(2)}, u32[]{:S(2)}) collective-permute-start(bf16[256,1024]{1,0:T(8,128)(2,1)S(1)} %get-tuple-element.720), channel_id=1, source_target_pairs={{0,8},{8,16},{16,24},{24,28},{28,20},{20,12},{12,4},{4,0},{1,9},{9... | collective-permute-start | bytes 1572872 | tf_op jit(solution)/shard_map/ppermute | solution.py:201
  484.8 30.0 %collective-permute-start.72 = (bf16[256,1024]{1,0:T(8,128)(2,1)S(1)}, bf16[256,1024]{1,0:T(8,128)(2,1)S(1)}, u32[]{:S(2)}, u32[]{:S(2)}) collective-permute-start(bf16[256,1024]{1,0:T(8,128)(2,1)S(1)} %get-tuple-element.721), channel_id=1, source_target_pairs={{8,0},{16,8},{24,16},{28,24},{20,28},{12,20},{4,12},{0,4},{9,1},{1... | collective-permute-start | bytes 1572872 | tf_op jit(solution)/shard_map/ppermute | solution.py:201
  512.7 22.7 %collective-permute-start.69 = (bf16[256,1024]{1,0:T(8,128)(2,1)S(1)}, bf16[256,1024]{1,0:T(8,128)(2,1)S(1)}, u32[]{:S(2)}, u32[]{:S(2)}) collective-permute-start(bf16[256,1024]{1,0:T(8,128)(2,1)S(1)} %get-tuple-element.718), channel_id=1, source_target_pairs={{0,8},{8,16},{16,24},{24,28},{28,20},{20,12},{12,4},{4,0},{1,9},{9... | collective-permute-start | bytes 1572872 | tf_op jit(solution)/shard_map/ppermute | solution.py:201
  536.9 25.6 %collective-permute-start.77 = (bf16[256,1024]{1,0:T(8,128)(2,1)S(1)}, bf16[256,1024]{1,0:T(8,128)(2,1)S(1)}, u32[]{:S(2)}, u32[]{:S(2)}) collective-permute-start(bf16[256,1024]{1,0:T(8,128)(2,1)S(1)} %get-tuple-element.764), channel_id=1, source_target_pairs={{0,8},{8,16},{16,24},{24,28},{28,20},{20,12},{12,4},{4,0},{1,9},{9... | collective-permute-start | bytes 1572872 | tf_op jit(solution)/shard_map/ppermute | solution.py:201
  538.4 24.1 %collective-permute-start.78 = (bf16[256,1024]{1,0:T(8,128)(2,1)S(1)}, bf16[256,1024]{1,0:T(8,128)(2,1)S(1)}, u32[]{:S(2)}, u32[]{:S(2)}) collective-permute-start(bf16[256,1024]{1,0:T(8,128)(2,1)S(1)} %get-tuple-element.765), channel_id=1, source_target_pairs={{8,0},{16,8},{24,16},{28,24},{20,28},{12,20},{4,12},{0,4},{9,1},{1... | collective-permute-start | bytes 1572872 | tf_op jit(solution)/shard_map/ppermute | solution.py:201
  553.7 42.1 %collective-permute-start.76 = (bf16[512,2048]{1,0:T(8,128)(2,1)S(1)}, bf16[512,2048]{1,0:T(8,128)(2,1)S(1)}, u32[]{:S(2)}, u32[]{:S(2)}) collective-permute-start(bf16[512,2048]{1,0:T(8,128)(2,1)S(1)} %partial_rows.5.kept_ref), channel_id=1, source_target_pairs={{0,2},{1,3},{2,0},{3,1},{4,6},{5,7},{6,4},{7,5},{8,10},{9,11},{10,... | collective-permute-start | bytes 6291464 | tf_op jit(solution)/shard_map/ppermute | solution.py:163
  584.8 22.7 %collective-permute-start.86 = (bf16[256,1024]{1,0:T(8,128)(2,1)S(1)}, bf16[256,1024]{1,0:T(8,128)(2,1)S(1)}, u32[]{:S(2)}, u32[]{:S(2)}) collective-permute-start(bf16[256,1024]{1,0:T(8,128)(2,1)S(1)} %get-tuple-element.811), channel_id=1, source_target_pairs={{0,8},{8,16},{16,24},{24,28},{28,20},{20,12},{12,4},{4,0},{1,9},{9... | collective-permute-start | bytes 1572872 | tf_op jit(solution)/shard_map/ppermute | solution.py:201
  611.0 22.9 %collective-permute-start.96 = (bf16[256,1024]{1,0:T(8,128)(2,1)S(1)}, bf16[256,1024]{1,0:T(8,128)(2,1)S(1)}, u32[]{:S(2)}, u32[]{:S(2)}) collective-permute-start(bf16[256,1024]{1,0:T(8,128)(2,1)S(1)} %get-tuple-element.853), channel_id=1, source_target_pairs={{0,8},{8,16},{16,24},{24,28},{28,20},{20,12},{12,4},{4,0},{1,9},{9... | collective-permute-start | bytes 1572872 | tf_op jit(solution)/shard_map/ppermute | solution.py:201
  612.5 22.6 %collective-permute-start.97 = (bf16[256,1024]{1,0:T(8,128)(2,1)S(1)}, bf16[256,1024]{1,0:T(8,128)(2,1)S(1)}, u32[]{:S(2)}, u32[]{:S(2)}) collective-permute-start(bf16[256,1024]{1,0:T(8,128)(2,1)S(1)} %get-tuple-element.854), channel_id=1, source_target_pairs={{8,0},{16,8},{24,16},{28,24},{20,28},{12,20},{4,12},{0,4},{9,1},{1... | collective-permute-start | bytes 1572872 | tf_op jit(solution)/shard_map/ppermute | solution.py:201
  627.2 46.7 %collective-permute-start.91 = (bf16[512,2048]{1,0:T(8,128)(2,1)S(1)}, bf16[512,2048]{1,0:T(8,128)(2,1)}, u32[]{:S(2)}, u32[]{:S(2)}) collective-permute-start(bf16[512,2048]{1,0:T(8,128)(2,1)S(1)} %partial_rows.7.kept_ref), channel_id=1, source_target_pairs={{0,2},{1,3},{2,0},{3,1},{4,6},{5,7},{6,4},{7,5},{8,10},{9,11},{10,... | collective-permute-start | bytes 6291464 | tf_op jit(solution)/shard_map/ppermute | solution.py:163
  639.5 22.0 %collective-permute-start.94 = (bf16[256,1024]{1,0:T(8,128)(2,1)}, bf16[256,1024]{1,0:T(8,128)(2,1)S(1)}, u32[]{:S(2)}, u32[]{:S(2)}) collective-permute-start(bf16[256,1024]{1,0:T(8,128)(2,1)} %get-tuple-element.851), channel_id=1, source_target_pairs={{0,8},{8,16},{16,24},{24,28},{28,20},{20,12},{12,4},{4,0},{1,9},{9... | collective-permute-start | bytes 1572872 | tf_op jit(solution)/shard_map/ppermute | solution.py:201
  641.2 22.1 %collective-permute-start.95 = (bf16[256,1024]{1,0:T(8,128)(2,1)}, bf16[256,1024]{1,0:T(8,128)(2,1)S(1)}, u32[]{:S(2)}, u32[]{:S(2)}) collective-permute-start(bf16[256,1024]{1,0:T(8,128)(2,1)} %get-tuple-element.852), channel_id=1, source_target_pairs={{8,0},{16,8},{24,16},{28,24},{20,28},{12,20},{4,12},{0,4},{9,1},{1... | collective-permute-start | bytes 1572872 | tf_op jit(solution)/shard_map/ppermute | solution.py:201
  652.6 25.1 %collective-permute-start.100 = (f32[4,1664]{1,0:T(4,128)S(1)}, f32[4,1664]{1,0:T(4,128)S(1)}, u32[]{:S(2)}, u32[]{:S(2)}) collective-permute-start(f32[4,1664]{1,0:T(4,128)S(1)} %get-tuple-element.897), channel_id=1, source_target_pairs={{0,16},{4,20},{8,24},{12,28},{16,0},{20,4},{24,8},{28,12},{1,17},{... | collective-permute-start | bytes 79880 | tf_op jit(solution)/shard_map/ppermute | solution.py:163
  (188 other events, 2767.8 us)

commit v4 on v3

--- a/solution.py
+++ b/solution.py
@@ -441,6 +441,7 @@
         [((rows, cols), BF)] * 2 + weight.shapes,
         9,
         scratch=weight.scratch,
+        stay=True,
     )
 
 
@@ -462,6 +463,7 @@
         [((rows, weight.cols), BF)] + weight.shapes,
         9,
         scratch=weight.scratch,
+        stay=True,
     )
 
 
@@ -575,6 +577,7 @@
         12,
         scratch=weight.scratch,
         vmem=32,
+        stay=True,
     )
 
 
@@ -697,8 +700,8 @@
 
         pick(side_ref, mine_ref, other_ref, n2_ref)
 
-        for at in range(0, cols, 256):
-            part = slice(at, at + 256)
+        for at in range(0, cols, 1024):
+            part = slice(at, at + 1024)
             z = jnp.dot(n2_ref[...], up_ref[:, part], preferred_element_type=F32)
             z = z + shift_ref[:, part]
             d_act = jnp.dot(cot_ref[...], down_ref[:, part], preferred_element_type=F32)
@@ -751,6 +754,7 @@
         scratch=up.scratch + down.scratch,
         vmem=44,
         prefetch=(side[None],),
+        stay=True,
     )
 
 
@@ -1218,6 +1222,7 @@
     )
     n1 = clock.until(qkv_ring, n1)
 
+    n1 = clock.tick(n1)
     qk_weight, v_weight = qkv_ring.result()
     q, k, qk_mat = project_turn(n1, qk_weight, cosine, sine)
     n1, q, k = barrier(n1, q, k)
@@ -1336,24 +1341,24 @@
         cost=6,
     )
     leaving_parts = others.second()
-    line.tick(wu_back)
     grad_o = line.run(gradient, d_branch, y, cost=6)
     line.tick(wu_back)
     grad_g = line.run(gradient, n1, d_gate, cost=6)
     og_back = reduce(grad_o, grad_g, turned=True)
+    leaving = line.run(lambda first, *rest: gathered_state(first, rest, -1), *leaving_parts)
     line.tick(og_back)
-    leaving = line.run(lambda first, *rest: gathered_state(first, rest, -1), *leaving_parts)
     d_k, d_v = line.run(
         lambda d_k, d_v: state_backward(k, v, exit_cols, leaving, d_k, d_v, cosine, sine),
         d_k,
         d_v,
-        cost=6,
     )
     line.tick(wu_back)
-    grad_v = line.run(gradient, n1, d_v)
-    grad_qk = line.run(gradient, n1, d_q, d_k, cost=6)
+    grad_v = line.run(gradient, n1, d_v, cost=6)
+    grad_qk = line.run(gradient, n1, d_q, d_k)
     vqk_back = reduce(grad_v, grad_qk, cut=True)
-    line.tick(vqk_back, og_back)
+    line.tick(wu_back)
+    line.tick(vqk_back)
+    line.tick(og_back)
     d_all = (d_gate, d_v, d_q, d_k)
     mats_all = ((g_mat, 0), (v_mat, 0), (qk_mat, 0), (qk_mat, 1))
     sent_one = partial_sent(d_all, mats_all, 1, cost=6)
@@ -1376,12 +1381,11 @@
     grad_other = to_partner(grad_mine, 1)[0]
     sent_out = line.send(part_out, "tp", pairs_one)
     line.tick(og_back, vqk_back, cost=12)
-    grad_inputs = line.run(
-        lambda mine, other: both_halves(mine, other, side, F32), grad_mine, grad_other
-    )
     kept_out = partial_kept((act,), ((w_mat, 0),), (sent_out,))
     other_out = line.send(kept_out, "tp", pairs_two)
-    grad_second_gain = line.fill(grad_second_gain, 23)
+    grad_inputs = line.run(
+        lambda mine, other: both_halves(mine, other, side, F32), grad_mine, grad_other, cost=23
+    )
     line.tick(og_back, vqk_back)
 
     grad_up_bias = line.token

time: 703 us -> 694 us (0.987)
  waiting for transfers between devices: 258 us -> 245 us
    unnamed x223 -> x207, local copies, waits for them, and re-layouts: 45 us -> 38.2 us
    pallas_call x55 -> x54, Pallas kernels: 246 us -> 250 us  [kernel_call(): pl.pallas_call(body, out_shape=[jax.ShapeDtypeStruct(s, t) for s, t in sh...]
  transfers between devices with their start and end apart: 107 -> 107, of which waited for: 65 -> 62; matrix products, arithmetic and copies ran while one was open for 3% -> 4% of each run, Pallas kernels for 30% -> 31%
where the time goes in v4:
time: 694 us; the launch traced here: 684 us
  Pallas kernels  250 us (36%)
  waiting for transfers between devices  245 us (35%)
  starting transfers between devices  115 us (17%)
  local copies, waits for them, and re-layouts  41.9 us (6%)
  other arithmetic  18 us (3%)
  matrix products  8.94 us (1%)
    pallas_call x54, Pallas kernels, kernel_call(): pl.pallas_call(body, out_shape=[jax.ShapeDtypeStruct(s, t) for s, t in sh...  250 us
    ppermute x42, waiting for transfers between devices, tick(): lax.ppermute(block, 'seq', route)  110 us
    ppermute x42, waiting for transfers between devices, go(): lax.ppermute(block, 'seq', route)  79.2 us
    ppermute x42, starting transfers between devices, tick(): lax.ppermute(block, 'seq', route)  45.9 us
    ppermute x42, starting transfers between devices, go(): lax.ppermute(block, 'seq', route)  44.1 us
    unnamed x207, local copies, waits for them, and re-layouts  38.2 us
    ppermute x3, waiting for transfers between devices, doubled(): return jnp.concatenate([rows, lax.ppermute(rows, 'seq', route)], axis=0)  26.7 us
  transfers between devices with their start and end apart: 107, of which 62 were waited for; matrix products, arithmetic and copies ran while one was open for 4% of the time, Pallas kernels for 31%

profile of v4, /device:TPU:0, one launch (start us, length us, event | category | flops | bytes accessed | tf_op | source)
XLA Modules:
  0.0 684.0 jit_solution(9670431396678758767)
XLA Ops:
  9.8 9.6 %collective-permute-done.2 = bf16[1,1664]{1,0:T(2,128)(2,1)S(1)} collective-permute-done((bf16[1,1664]{1,0:T(2,128)(2,1)S(1)}, bf16[1,1664]{1,0:T(2,128)(2,1)S(1)}, u32[]{:S(2)}, u32[]{:S(2)}) %collective-permute-start.2) | collective-permute-done | bytes 3360 | tf_op jit(solution)/shard_map/ppermute | solution.py:259
  24.4 10.3 %collective-permute-done.5 = bf16[2,1664]{1,0:T(2,128)(2,1)S(1)} collective-permute-done((bf16[2,1664]{1,0:T(2,128)(2,1)S(1)}, bf16[2,1664]{1,0:T(2,128)(2,1)S(1)}, u32[]{:S(2)}, u32[]{:S(2)}) %collective-permute-start.5) | collective-permute-done | bytes 6688 | tf_op jit(solution)/shard_map/ppermute | solution.py:259
  63.3 9.0 %collective-permute-done.11.refs_5_ = bf16[256,1024]{1,0:T(8,128)(2,1)} collective-permute-done((bf16[256,1024]{1,0:T(8,128)(2,1)}, bf16[256,1024]{1,0:T(8,128)(2,1)}, u32[]{:S(2)}, u32[]{:S(2)}) %collective-permute-start.11) | collective-permute-done | bytes 524320 | tf_op jit(solution)/shard_map/ppermute | solution.py:128
  79.9 9.3 %collective-permute-done.13.refs_1_ = bf16[256,1024]{1,0:T(8,128)(2,1)S(1)} collective-permute-done((bf16[256,1024]{1,0:T(8,128)(2,1)S(1)}, bf16[256,1024]{1,0:T(8,128)(2,1)S(1)}, u32[]{:S(2)}, u32[]{:S(2)}) %collective-permute-start.13) | collective-permute-done | bytes 524320 | tf_op jit(solution)/shard_map/ppermute | solution.py:128
  93.0 7.6 %collective-permute-done.17.refs_6_ = bf16[256,1024]{1,0:T(8,128)(2,1)} collective-permute-done((bf16[256,1024]{1,0:T(8,128)(2,1)}, bf16[256,1024]{1,0:T(8,128)(2,1)}, u32[]{:S(2)}, u32[]{:S(2)}) %collective-permute-start.17) | collective-permute-done | bytes 524320 | tf_op jit(solution)/shard_map/ppermute | solution.py:128
  103.1 8.7 %collective-permute-done.15.refs_2_ = bf16[256,1024]{1,0:T(8,128)(2,1)} collective-permute-done((bf16[256,1024]{1,0:T(8,128)(2,1)S(1)}, bf16[256,1024]{1,0:T(8,128)(2,1)}, u32[]{:S(2)}, u32[]{:S(2)}) %collective-permute-start.15) | collective-permute-done | bytes 524320 | tf_op jit(solution)/shard_map/ppermute | solution.py:128
  133.3 9.2 %query_key.1 = (bf16[1024,512]{1,0:T(8,128)(2,1)S(1)}, bf16[1024,512]{1,0:T(8,128)(2,1)S(1)}, bf16[2048,1024]{1,0:T(8,128)(2,1)S(1)}) custom-call(bf16[1024,2048]{1,0:T(8,128)(2,1)} %copy-done.15, f32[1024,128]{1,0:T(8,128)} %get-tuple-element.960.cos_ref, f32[1024,128]{1,0:T(8,128)} %get-tuple-element.959.sin_ref, bf16[256,1024]{1,0:T(8,128)(2,1)} %copy-done.63, ...), custom_call_target="tpu_custom_call" | custom-call | flops 4499999744 | tf_op jit(solution)/shard_map/query_key/pallas_call | solution.py:345
  149.4 9.1 %value.1 = (bf16[1024,1024]{1,0:T(8,128)(2,1)S(1)}, bf16[2048,1024]{1,0:T(8,128)(2,1)S(1)}) custom-call(bf16[1024,2048]{1,0:T(8,128)(2,1)} %copy-done.15, bf16[256,1024]{1,0:T(8,128)(2,1)} %copy-done.56, bf16[256,1024]{1,0:T(8,128)(2,1)} %copy-done.71, bf16[256,1024]{1,0:T(8,128)(2,1)} %copy-done.73, bf16[256,1024]{1,0:T(8,128)(2,1)} %copy-done.75, ...), custom_call_target="tpu_custom_call" | custom-call | flops 4499999744 | tf_op jit(solution)/shard_map/value/pallas_call | solution.py:345
  188.7 8.1 %collective-permute-done.29.refs_1_ = bf16[256,1024]{1,0:T(8,128)(2,1)} collective-permute-done((bf16[256,1024]{1,0:T(8,128)(2,1)S(1)}, bf16[256,1024]{1,0:T(8,128)(2,1)}, u32[]{:S(2)}, u32[]{:S(2)}) %collective-permute-start.29) | collective-permute-done | bytes 524320 | tf_op jit(solution)/shard_map/ppermute | solution.py:128
  199.4 7.5 %collective-permute-done.35.refs_7_ = bf16[256,1024]{1,0:T(8,128)(2,1)} collective-permute-done((bf16[256,1024]{1,0:T(8,128)(2,1)}, bf16[256,1024]{1,0:T(8,128)(2,1)}, u32[]{:S(2)}, u32[]{:S(2)}) %collective-permute-start.35) | collective-permute-done | bytes 524320 | tf_op jit(solution)/shard_map/ppermute | solution.py:128
  212.9 13.0 %gate_forward.1 = (bf16[1024,1024]{1,0:T(8,128)(2,1)S(1)}, f32[1024,1024]{1,0:T(8,128)S(1)}, f32[1024,1024]{1,0:T(8,128)S(1)}, f32[1024,2]{1,0:T(8,128)S(1)}, bf16[2048,1024]{1,0:T(8,128)(2,1)S(1)}) custom-call(bf16[1024,2048]{1,0:T(8,128)(2,1)} %copy-done.15, bf16[1024,512]{1,0:T(8,128)(2,1)} %copy-done.40, f32[1024,2]{1,0:T(8,128)} %get-tuple-element.967.entry_ref, ...), custom_call_target="tpu_custom_call" | custom-call | flops 6000000000 | tf_op jit(solution)/shard_map/gate_forward/pallas_call | solution.py:345
  252.2 11.7 %collective-permute-done.42.refs_5_ = bf16[256,1024]{1,0:T(8,128)(2,1)S(1)} collective-permute-done((bf16[256,1024]{1,0:T(8,128)(2,1)S(1)}, bf16[256,1024]{1,0:T(8,128)(2,1)S(1)}, u32[]{:S(2)}, u32[]{:S(2)}) %collective-permute-start.42) | collective-permute-done | bytes 524320 | tf_op jit(solution)/shard_map/ppermute | solution.py:128
  266.6 10.1 %collective-permute-done.44.refs_6_ = bf16[256,1024]{1,0:T(8,128)(2,1)S(1)} collective-permute-done((bf16[256,1024]{1,0:T(8,128)(2,1)S(1)}, bf16[256,1024]{1,0:T(8,128)(2,1)S(1)}, u32[]{:S(2)}, u32[]{:S(2)}) %collective-permute-start.44) | collective-permute-done | bytes 524320 | tf_op jit(solution)/shard_map/ppermute | solution.py:128
  280.0 9.4 %collective-permute-done.46.refs_7_ = bf16[256,1024]{1,0:T(8,128)(2,1)S(1)} collective-permute-done((bf16[256,1024]{1,0:T(8,128)(2,1)S(1)}, bf16[256,1024]{1,0:T(8,128)(2,1)S(1)}, u32[]{:S(2)}, u32[]{:S(2)}) %collective-permute-start.46) | collective-permute-done | bytes 524320 | tf_op jit(solution)/shard_map/ppermute | solution.py:128
  302.9 26.8 %feed_forward.1 = (bf16[1024,2048]{1,0:T(8,128)(2,1)}, bf16[1024,1024]{1,0:T(8,128)(2,1)S(1)}, bf16[1024,1024]{1,0:T(8,128)(2,1)S(1)}, f32[1,1024]{1,0:T(1,128)S...) custom-call(s32[1]{0:T(128)} %bitcast.side_ref.which_ref, ...), custom_call_target="tpu_custom_call" | custom-call | flops 8000000000 | tf_op jit(solution)/shard_map/feed_forward/pallas_call | solution.py:345
  355.4 12.0 %collective-permute-done.52.refs_2_ = bf16[256,1024]{1,0:T(8,128)(2,1)S(1)} collective-permute-done((bf16[256,1024]{1,0:T(8,128)(2,1)S(1)}, bf16[256,1024]{1,0:T(8,128)(2,1)S(1)}, u32[]{:S(2)}, u32[]{:S(2)}) %collective-permute-start.52) | collective-permute-done | bytes 524320 | tf_op jit(solution)/shard_map/ppermute | solution.py:201
  373.2 10.2 %collective-permute-done.54.refs_2_ = bf16[256,1024]{1,0:T(8,128)(2,1)S(1)} collective-permute-done((bf16[256,1024]{1,0:T(8,128)(2,1)}, bf16[256,1024]{1,0:T(8,128)(2,1)S(1)}, u32[]{:S(2)}, u32[]{:S(2)}) %collective-permute-start.54) | collective-permute-done | bytes 524320 | tf_op jit(solution)/shard_map/ppermute | solution.py:201
  403.9 13.2 %gate_backward.1 = (bf16[1024,2048]{1,0:T(8,128)(2,1)S(1)}, bf16[1024,1024]{1,0:T(8,128)(2,1)S(1)}, bf16[1024,1024]{1,0:T(8,128)(2,1)S(1)}, f32[1,1024]{1,0:T(1,...) custom-call(s32[1]{0:T(128)} %bitcast.side_ref.which_ref, bf16[512,2048]{1,0:T(8,128)(2,1)} %copy-done.35, ...), custom_call_target="tpu_custom_call" | custom-call | flops 6000000000 | tf_op jit(solution)/shard_map/gate_backward/pallas_call | solution.py:345
  420.1 10.7 %retain_backward.1 = (bf16[1024,512]{1,0:T(8,128)(2,1)S(1)}, f32[1024,512]{1,0:T(8,128)S(1)}, f32[1024,1024]{1,0:T(8,128)S(1)}) custom-call(f32[2]{0:T(128)S(1)} %subtract_log_fusion.decay_ref, bf16[1024,512]{1,0:T(8,128)(2,1)} %copy-done.40, bf16[1024,512]{1,0:T(8,128)(2,1)} %copy-done.26, bf16[1024,1024]{1,0:T(8,128)(2,1)} %copy-done.21, ...), custom_call_target="tpu_custom_call" | custom-call | flops 6000000000 | tf_op jit(solution)/shard_map/retain_backward/pallas_call | solution.py:345
  504.1 10.6 %partial_rows.4 = bf16[512,2048]{1,0:T(8,128)(2,1)S(1)} custom-call(s32[1]{0:T(128)} %bitcast.14.which_ref, bf16[1024,1024]{1,0:T(8,128)(2,1)} %copy-done.12, bf16[1024,1024]{1,0:T(8,128)(2,1)} %copy-done.13, bf16[1024,512]{1,0:T(8,128)(2,1)} %copy-done.9, bf16[1024,512]{1,0:T(8,128)(2,1)} %copy-done.10, bf16[2048,1024]{1,0:T(8,128)(2,1)} %copy-done.8, ...), custom_call_target="tpu_custom_call" | custom-call | flops 6000000000 | tf_op jit(solution)/shard_map/partial_rows/pallas_call | solution.py:345
  531.6 11.0 %partial_rows.5.kept_ref = bf16[512,2048]{1,0:T(8,128)(2,1)S(1)} custom-call(s32[1]{0:T(128)} %bitcast.side_ref.which_ref, bf16[1024,1024]{1,0:T(8,128)(2,1)} %copy-done.12, bf16[1024,1024]{1,0:T(8,128)(2,1)} %copy-done.13, bf16[1024,512]{1,0:T(8,128)(2,1)} %copy-done.9, bf16[1024,512]{1,0:T(8,128)(2,1)} %copy-done.10, bf16[2048,1024]{1,0:T(8,128)(2,1)} %copy-done.8, ...), custom_call_target="tpu_custom_call" | custom-call | flops 6000000000 | tf_op jit(solution)/shard_map/partial_rows/pallas_call | solution.py:345
  579.2 7.3 %collective-permute-done.88.other_ref = bf16[512,2048]{1,0:T(8,128)(2,1)S(1)} collective-permute-done((bf16[512,2048]{1,0:T(8,128)(2,1)S(1)}, bf16[512,2048]{1,0:T(8,128)(2,1)S(1)}, u32[]{:S(2)}, u32[]{:S(2)}) %collective-permute-start.88) | collective-permute-done | bytes 2097184 | tf_op jit(solution)/shard_map/ppermute | solution.py:163
  587.8 8.1 %norm_backward.3 = (f32[512,2048]{1,0:T(8,128)}, bf16[512,2048]{1,0:T(8,128)(2,1)S(1)}, f32[1,2048]{1,0:T(1,128)S(1)}, f32[1,2048]{1,0:T(1,128)S(1)}) custom-call(s32[1]{0:T(128)} %bitcast.side_ref.which_ref, bf16[1024,2048]{1,0:T(8,128)(2,1)} %x_ref.5, bf16[512,2048]{1,0:T(8,128)(2,1)} %copy-done.19, bf16[512,2048]{1,0:T(8,128)(2,1)} %copy-done.67, ...), custom_call_target="tpu_custom_call" | custom-call | flops 6000000000 | tf_op jit(solution)/shard_map/norm_backward/pallas_call | solution.py:345
  633.1 10.5 %collective-permute-done.98.refs_2_ = bf16[256,1024]{1,0:T(8,128)(2,1)} collective-permute-done((bf16[256,1024]{1,0:T(8,128)(2,1)}, bf16[256,1024]{1,0:T(8,128)(2,1)}, u32[]{:S(2)}, u32[]{:S(2)}) %collective-permute-start.98) | collective-permute-done | bytes 524320 | tf_op jit(solution)/shard_map/ppermute | solution.py:201
  (507 shorter events, 425.7 us)
Async XLA Ops:
  77.9 22.7 %collective-permute-start.17 = (bf16[256,1024]{1,0:T(8,128)(2,1)}, bf16[256,1024]{1,0:T(8,128)(2,1)}, u32[]{:S(2)}, u32[]{:S(2)}) collective-permute-start(bf16[256,1024]{1,0:T(8,128)(2,1)} %collective-permute-done.11.refs_5_), channel_id=1, source_target_pairs={{0,8},{8,16},{16,24},{24,28},{28,20},{20,12},{12,4},{4,0},{1,9},{9... | collective-permute-start | bytes 1572872 | tf_op jit(solution)/shard_map/ppermute | solution.py:128
  78.4 22.7 %collective-permute-start.18 = (bf16[256,1024]{1,0:T(8,128)(2,1)}, bf16[256,1024]{1,0:T(8,128)(2,1)}, u32[]{:S(2)}, u32[]{:S(2)}) collective-permute-start(bf16[256,1024]{1,0:T(8,128)(2,1)} %collective-permute-done.12.refs_5_), channel_id=1, source_target_pairs={{8,0},{16,8},{24,16},{28,24},{20,28},{12,20},{4,12},{0,4},{9,1},{1... | collective-permute-start | bytes 1572872 | tf_op jit(solution)/shard_map/ppermute | solution.py:128
  178.1 28.8 %collective-permute-start.35 = (bf16[256,1024]{1,0:T(8,128)(2,1)}, bf16[256,1024]{1,0:T(8,128)(2,1)}, u32[]{:S(2)}, u32[]{:S(2)}) collective-permute-start(bf16[256,1024]{1,0:T(8,128)(2,1)} %collective-permute-done.27.refs_6_), channel_id=1, source_target_pairs={{0,8},{8,16},{16,24},{24,28},{28,20},{20,12},{12,4},{4,0},{1,9},{9... | collective-permute-start | bytes 1572872 | tf_op jit(solution)/shard_map/ppermute | solution.py:128
  178.5 28.4 %collective-permute-start.36 = (bf16[256,1024]{1,0:T(8,128)(2,1)}, bf16[256,1024]{1,0:T(8,128)(2,1)S(1)}, u32[]{:S(2)}, u32[]{:S(2)}) collective-permute-start(bf16[256,1024]{1,0:T(8,128)(2,1)} %collective-permute-done.28.refs_6_), channel_id=1, source_target_pairs={{8,0},{16,8},{24,16},{28,24},{20,28},{12,20},{4,12},{0,4},{9,1},{1... | collective-permute-start | bytes 1572872 | tf_op jit(solution)/shard_map/ppermute | solution.py:128
  186.6 22.7 %collective-permute-start.34 = (bf16[2,256,512]{2,1,0:T(8,128)(2,1)}, bf16[2,256,512]{2,1,0:T(8,128)(2,1)S(1)}, u32[]{:S(2)}, u32[]{:S(2)}) collective-permute-start(bf16[2,256,512]{2,1,0:T(8,128)(2,1)} %broadcast_select_fusion.1), channel_id=1, source_target_pairs={{0,4},{4,0},{8,12},{12,8},{16,20},{20,16},{24,28},{28,24},{1,5},{5... | collective-permute-start | bytes 1572872 | tf_op jit(solution)/shard_map/ppermute | solution.py:40
  196.8 29.2 %collective-permute-start.31 = (bf16[256,1024]{1,0:T(8,128)(2,1)}, bf16[256,1024]{1,0:T(8,128)(2,1)S(1)}, u32[]{:S(2)}, u32[]{:S(2)}) collective-permute-start(bf16[256,1024]{1,0:T(8,128)(2,1)} %collective-permute-done.29.refs_1_), channel_id=1, source_target_pairs={{0,8},{8,16},{16,24},{24,28},{28,20},{20,12},{12,4},{4,0},{1,9},{9... | collective-permute-start | bytes 1572872 | tf_op jit(solution)/shard_map/ppermute | solution.py:128
  199.4 26.6 %collective-permute-start.32 = (bf16[256,1024]{1,0:T(8,128)(2,1)}, bf16[256,1024]{1,0:T(8,128)(2,1)S(1)}, u32[]{:S(2)}, u32[]{:S(2)}) collective-permute-start(bf16[256,1024]{1,0:T(8,128)(2,1)} %collective-permute-done.30.refs_9_), channel_id=1, source_target_pairs={{8,0},{16,8},{24,16},{28,24},{20,28},{12,20},{4,12},{0,4},{9,1},{1... | collective-permute-start | bytes 1572872 | tf_op jit(solution)/shard_map/ppermute | solution.py:128
  246.4 47.7 %collective-permute-start.48 = (bf16[512,2048]{1,0:T(8,128)(2,1)S(1)}, bf16[512,2048]{1,0:T(8,128)(2,1)S(1)}, u32[]{:S(2)}, u32[]{:S(2)}) collective-permute-start(bf16[512,2048]{1,0:T(8,128)(2,1)S(1)} %add_convert_fusion.kept_ref), channel_id=1, source_target_pairs={{0,2},{1,3},{2,0},{3,1},{4,6},{5,7},{6,4},{7,5},{8,10},{9,11},{10,... | collective-permute-start | bytes 6291464 | tf_op jit(solution)/shard_map/ppermute | solution.py:283
  341.8 48.0 %collective-permute-start.51 = (bf16[512,2048]{1,0:T(8,128)(2,1)S(1)}, bf16[512,2048]{1,0:T(8,128)(2,1)}, u32[]{:S(2)}, u32[]{:S(2)}) collective-permute-start(bf16[512,2048]{1,0:T(8,128)(2,1)S(1)} %add_sent.1.kept_ref), channel_id=1, source_target_pairs={{0,2},{1,3},{2,0},{3,1},{4,6},{5,7},{6,4},{7,5},{8,10},{9,11},{10,... | collective-permute-start | bytes 6291464 | tf_op jit(solution)/shard_map/ppermute | solution.py:163
  436.8 26.7 %collective-permute-start.62 = (bf16[2,256,512]{2,1,0:T(8,128)(2,1)S(1)}, bf16[2,256,512]{2,1,0:T(8,128)(2,1)S(1)}, u32[]{:S(2)}, u32[]{:S(2)}) collective-permute-start(bf16[2,256,512]{2,1,0:T(8,128)(2,1)S(1)} %broadcast_select_fusion), channel_id=1, source_target_pairs={{0,4},{4,0},{8,12},{12,8},{16,20},{20,16},{24,28},{28,24},{1,5},{5... | collective-permute-start | bytes 1572872 | tf_op jit(solution)/shard_map/ppermute | solution.py:163
  473.1 22.5 %collective-permute-start.67 = (bf16[256,1024]{1,0:T(8,128)(2,1)S(1)}, bf16[256,1024]{1,0:T(8,128)(2,1)S(1)}, u32[]{:S(2)}, u32[]{:S(2)}) collective-permute-start(bf16[256,1024]{1,0:T(8,128)(2,1)S(1)} %get-tuple-element.705), channel_id=1, source_target_pairs={{0,8},{8,16},{16,24},{24,28},{28,20},{20,12},{12,4},{4,0},{1,9},{9... | collective-permute-start | bytes 1572872 | tf_op jit(solution)/shard_map/ppermute | solution.py:201
  475.2 25.3 %collective-permute-start.71 = (bf16[256,1024]{1,0:T(8,128)(2,1)S(1)}, bf16[256,1024]{1,0:T(8,128)(2,1)S(1)}, u32[]{:S(2)}, u32[]{:S(2)}) collective-permute-start(bf16[256,1024]{1,0:T(8,128)(2,1)S(1)} %get-tuple-element.716), channel_id=1, source_target_pairs={{0,8},{8,16},{16,24},{24,28},{28,20},{20,12},{12,4},{4,0},{1,9},{9... | collective-permute-start | bytes 1572872 | tf_op jit(solution)/shard_map/ppermute | solution.py:201
  476.2 24.3 %collective-permute-start.72 = (bf16[256,1024]{1,0:T(8,128)(2,1)S(1)}, bf16[256,1024]{1,0:T(8,128)(2,1)S(1)}, u32[]{:S(2)}, u32[]{:S(2)}) collective-permute-start(bf16[256,1024]{1,0:T(8,128)(2,1)S(1)} %get-tuple-element.717), channel_id=1, source_target_pairs={{8,0},{16,8},{24,16},{28,24},{20,28},{12,20},{4,12},{0,4},{9,1},{1... | collective-permute-start | bytes 1572872 | tf_op jit(solution)/shard_map/ppermute | solution.py:201
  498.5 25.9 %collective-permute-start.69 = (bf16[256,1024]{1,0:T(8,128)(2,1)S(1)}, bf16[256,1024]{1,0:T(8,128)(2,1)S(1)}, u32[]{:S(2)}, u32[]{:S(2)}) collective-permute-start(bf16[256,1024]{1,0:T(8,128)(2,1)S(1)} %get-tuple-element.714), channel_id=1, source_target_pairs={{0,8},{8,16},{16,24},{24,28},{28,20},{20,12},{12,4},{4,0},{1,9},{9... | collective-permute-start | bytes 1572872 | tf_op jit(solution)/shard_map/ppermute | solution.py:201
  499.7 24.8 %collective-permute-start.70 = (bf16[256,1024]{1,0:T(8,128)(2,1)S(1)}, bf16[256,1024]{1,0:T(8,128)(2,1)S(1)}, u32[]{:S(2)}, u32[]{:S(2)}) collective-permute-start(bf16[256,1024]{1,0:T(8,128)(2,1)S(1)} %get-tuple-element.715), channel_id=1, source_target_pairs={{8,0},{16,8},{24,16},{28,24},{20,28},{12,20},{4,12},{0,4},{9,1},{1... | collective-permute-start | bytes 1572872 | tf_op jit(solution)/shard_map/ppermute | solution.py:201
  525.9 27.1 %collective-permute-start.75 = (bf16[256,1024]{1,0:T(8,128)(2,1)S(1)}, bf16[256,1024]{1,0:T(8,128)(2,1)S(1)}, u32[]{:S(2)}, u32[]{:S(2)}) collective-permute-start(bf16[256,1024]{1,0:T(8,128)(2,1)S(1)} %get-tuple-element.751), channel_id=1, source_target_pairs={{0,8},{8,16},{16,24},{24,28},{28,20},{20,12},{12,4},{4,0},{1,9},{9... | collective-permute-start | bytes 1572872 | tf_op jit(solution)/shard_map/ppermute | solution.py:201
  527.7 25.3 %collective-permute-start.76 = (bf16[256,1024]{1,0:T(8,128)(2,1)S(1)}, bf16[256,1024]{1,0:T(8,128)(2,1)S(1)}, u32[]{:S(2)}, u32[]{:S(2)}) collective-permute-start(bf16[256,1024]{1,0:T(8,128)(2,1)S(1)} %get-tuple-element.752), channel_id=1, source_target_pairs={{8,0},{16,8},{24,16},{28,24},{20,28},{12,20},{4,12},{0,4},{9,1},{1... | collective-permute-start | bytes 1572872 | tf_op jit(solution)/shard_map/ppermute | solution.py:201
  542.7 43.8 %collective-permute-start.88 = (bf16[512,2048]{1,0:T(8,128)(2,1)S(1)}, bf16[512,2048]{1,0:T(8,128)(2,1)S(1)}, u32[]{:S(2)}, u32[]{:S(2)}) collective-permute-start(bf16[512,2048]{1,0:T(8,128)(2,1)S(1)} %partial_rows.5.kept_ref), channel_id=1, source_target_pairs={{0,2},{1,3},{2,0},{3,1},{4,6},{5,7},{6,4},{7,5},{8,10},{9,11},{10,... | collective-permute-start | bytes 6291464 | tf_op jit(solution)/shard_map/ppermute | solution.py:163
  575.1 23.1 %collective-permute-start.84 = (bf16[256,1024]{1,0:T(8,128)(2,1)S(1)}, bf16[256,1024]{1,0:T(8,128)(2,1)S(1)}, u32[]{:S(2)}, u32[]{:S(2)}) collective-permute-start(bf16[256,1024]{1,0:T(8,128)(2,1)S(1)} %get-tuple-element.798), channel_id=1, source_target_pairs={{0,8},{8,16},{16,24},{24,28},{28,20},{20,12},{12,4},{4,0},{1,9},{9... | collective-permute-start | bytes 1572872 | tf_op jit(solution)/shard_map/ppermute | solution.py:201
  575.8 22.4 %collective-permute-start.85 = (bf16[256,1024]{1,0:T(8,128)(2,1)S(1)}, bf16[256,1024]{1,0:T(8,128)(2,1)S(1)}, u32[]{:S(2)}, u32[]{:S(2)}) collective-permute-start(bf16[256,1024]{1,0:T(8,128)(2,1)S(1)} %get-tuple-element.799), channel_id=1, source_target_pairs={{8,0},{16,8},{24,16},{28,24},{20,28},{12,20},{4,12},{0,4},{9,1},{1... | collective-permute-start | bytes 1572872 | tf_op jit(solution)/shard_map/ppermute | solution.py:201
  601.8 23.0 %collective-permute-start.96 = (bf16[256,1024]{1,0:T(8,128)(2,1)S(1)}, bf16[256,1024]{1,0:T(8,128)(2,1)S(1)}, u32[]{:S(2)}, u32[]{:S(2)}) collective-permute-start(bf16[256,1024]{1,0:T(8,128)(2,1)S(1)} %get-tuple-element.845), channel_id=1, source_target_pairs={{0,8},{8,16},{16,24},{24,28},{28,20},{20,12},{12,4},{4,0},{1,9},{9... | collective-permute-start | bytes 1572872 | tf_op jit(solution)/shard_map/ppermute | solution.py:201
  603.3 22.7 %collective-permute-start.97 = (bf16[256,1024]{1,0:T(8,128)(2,1)S(1)}, bf16[256,1024]{1,0:T(8,128)(2,1)S(1)}, u32[]{:S(2)}, u32[]{:S(2)}) collective-permute-start(bf16[256,1024]{1,0:T(8,128)(2,1)S(1)} %get-tuple-element.846), channel_id=1, source_target_pairs={{8,0},{16,8},{24,16},{28,24},{20,28},{12,20},{4,12},{0,4},{9,1},{1... | collective-permute-start | bytes 1572872 | tf_op jit(solution)/shard_map/ppermute | solution.py:201
  610.2 48.6 %collective-permute-start.90 = (bf16[512,2048]{1,0:T(8,128)(2,1)S(1)}, bf16[512,2048]{1,0:T(8,128)(2,1)}, u32[]{:S(2)}, u32[]{:S(2)}) collective-permute-start(bf16[512,2048]{1,0:T(8,128)(2,1)S(1)} %partial_rows.7.kept_ref), channel_id=1, source_target_pairs={{0,2},{1,3},{2,0},{3,1},{4,6},{5,7},{6,4},{7,5},{8,10},{9,11},{10,... | collective-permute-start | bytes 6291464 | tf_op jit(solution)/shard_map/ppermute | solution.py:163
  631.8 22.1 %collective-permute-start.95 = (bf16[256,1024]{1,0:T(8,128)(2,1)}, bf16[256,1024]{1,0:T(8,128)(2,1)S(1)}, u32[]{:S(2)}, u32[]{:S(2)}) collective-permute-start(bf16[256,1024]{1,0:T(8,128)(2,1)} %get-tuple-element.844), channel_id=1, source_target_pairs={{8,0},{16,8},{24,16},{28,24},{20,28},{12,20},{4,12},{0,4},{9,1},{1... | collective-permute-start | bytes 1572872 | tf_op jit(solution)/shard_map/ppermute | solution.py:201
  (180 other events, 2521.7 us)
